TPU v7x, 256 devices: a whole 4x4x8 slice. The times are simulated.
256 devices in a mesh: rep: 32 (over y, x, z_hi), shard: 8 (over z_lo, core).
Axes of the slice: x: 4, y: 4, z: 8 (z_hi: 2, z_lo: 4; z = z_hi * 4 + z_lo), core: 2. Of those that a mesh axis runs over, the one named last changes fastest.
Arguments:
- x_in: bfloat16 [49152, 6144], P(('rep', 'shard')), may hold values from -6 to 6
- attn_out: bfloat16 [49152, 6144], P(('rep', 'shard')), may hold values from -6 to 6
- grads_out: bfloat16 [49152, 512], P(('rep', 'shard')), may hold values from -0.18042196 to 0.18042196
- master: float32 [128, 24576], P('shard'), may hold values from -0.51031036 to 0.51031036
- moment: float32 [128, 24576], P('shard'), may hold values from -3 to 3
- second: float32 [128, 24576], P('shard'), may hold values from 0.05 to 2
Outputs:
- new_master: float32 [128, 24576], P('shard')
- new_moment: float32 [128, 24576], P('shard')
- new_second: float32 [128, 24576], P('shard')
- gathered: bfloat16 [128, 24576], replicated
All inputs are finite; a program needn't handle non-finite values.
Results may differ from a plain program's by a relative error of at most 0.0004.
Values may be sent and summed in bfloat16 or wider, within the bound.
No kernel may reach another device: no remote copies, remote signals or barrier semaphores. Data moves between devices by JAX's collectives and lax.ppermute only.
A program may use at most 128 MiB of HBM per device.

v0:
```python
import jax
import jax.numpy as jnp
from jax import lax
from jax.sharding import PartitionSpec as P

beta_one = 0.9
beta_two = 0.95
learn_rate = 0.002
bias_one = 1.0 - 0.9**10
bias_two = 1.0 - 0.95**10


def adam_update(gradient, master, moment, second):
    new_moment = beta_one * moment + (1.0 - beta_one) * gradient
    new_second = beta_two * second + (1.0 - beta_two) * gradient * gradient
    stepped = master - learn_rate * (new_moment / bias_one) / (
        jnp.sqrt(new_second / bias_two) + 1e-08
    )
    return (stepped, new_moment, new_second)


def shards(x_in, attn_out, grads_out, master, moment, second):
    local_rows = master.shape[0]
    feature_width = x_in.shape[1]
    token_count = x_in.shape[0]
    shaped = grads_out.reshape(token_count, lax.axis_size("shard") * local_rows, 4)
    triple = jnp.einsum("trk,td->rkd", shaped[:, :, :3], x_in, preferred_element_type=jnp.float32)
    output_part = jnp.einsum(
        "tr,td->rd", shaped[:, :, 3], attn_out, preferred_element_type=jnp.float32
    )
    partial_grad = lax.psum_scatter(
        jnp.concatenate(
            [triple.reshape(lax.axis_size("shard") * local_rows, 3 * feature_width), output_part],
            axis=1,
        ),
        "shard",
        scatter_dimension=0,
        tiled=True,
    )
    gradient = lax.psum(partial_grad, "rep")
    stepped, new_moment, new_second = adam_update(gradient, master, moment, second)
    shaped = stepped.reshape(local_rows, 4, feature_width)
    scale_rows = jnp.sqrt(jnp.sum(shaped * shaped, axis=2, keepdims=True) + 1e-06)
    new_master = (shaped / scale_rows).reshape(local_rows, 4 * feature_width)
    gathered = lax.all_gather(new_master.astype(jnp.bfloat16), "shard", axis=0, tiled=True)
    return (new_master, new_moment, new_second, gathered)


def solution(mesh):
    in_specs = (
        P(("rep", "shard"), None),
        P(("rep", "shard"), None),
        P(("rep", "shard"), None),
        P("shard", None),
        P("shard", None),
        P("shard", None),
    )
    out_specs = (P("shard", None), P("shard", None), P("shard", None), P())
    return jax.shard_map(shards, mesh=mesh, in_specs=in_specs, out_specs=out_specs, check_vma=False)
```

profile of v0, /device:TPU:1, one launch (start us, length us, event | category | flops | bytes accessed | tf_op | source)
XLA Modules:
  0.0 707.6 jit_solution(7145786194673466493)
XLA Ops:
  7.2 0.0 copy-start
  7.2 0.0 reduce-scatter.4.cloned.1.call-start
  7.2 1.2 copy.51
  8.4 0.1 reshape.24
  8.5 0.1 slice.9
  8.7 0.1 copy.54
  8.8 3.0 fusion.4
  11.8 0.0 copy-done
  11.8 1.9 fusion
  13.7 8.5 %pad_maximum_fusion = f32[128,24576]{0,1:T(8,128)} fusion(f32[128,6144]{0,1:T(8,128)S(1)} %fusion.4, f32[128,18432]{0,1:T(8,128)S(1)} %bitcast.14), kind=kLoop, calls=%fused_computation | loop fusion | flops 3145728 | bytes 25165824 | tf_op jit(solution)/shard_map/concatenate | solution.py:32
  22.3 12.6 %copy.59 = f32[128,24576]{1,0:T(8,128)} copy(f32[128,24576]{0,1:T(8,128)} %pad_maximum_fusion) | data formatting | bytes 25165824
  34.9 0.0 reduce-scatter.4.cloned.1.call-update
  34.9 0.0 copy-start.2
  34.9 0.0 all-reduce.2.cloned.1.call-start
  34.9 136.0 %reduce-scatter.4.cloned.1.call-done = f32[16,24576]{1,0:T(8,128)} async-done(((f32[128,24576]{1,0:T(8,128)}), f32[16,24576]{1,0:T(8,128)}) %reduce-scatter.4.cloned.1.call-update) | async-done | bytes 1572880 | tf_op jit(solution)/shard_map/reduce_scatter | solution.py:31
  170.9 0.0 all-reduce.2.cloned.1.call-update
  170.9 0.0 all-gather.2.cloned.1.call-start
  171.0 417.2 %all-reduce.2.cloned.1.call-done = f32[16,24576]{1,0:T(8,128)} async-done(((f32[16,24576]{1,0:T(8,128)}), f32[16,24576]{1,0:T(8,128)}) %all-reduce.2.cloned.1.call-update) | async-done | bytes 1572880 | tf_op jit(solution)/shard_map/psum | solution.py:40
  588.2 5.2 fusion.7
  593.3 2.5 mul.51
  595.8 0.3 reduce_sum.9
  596.1 0.3 div.25
  596.4 0.0 copy-start.3
  596.4 0.0 copy-start.4
  596.4 0.9 copy.62
  597.3 0.2 copy-done.5
  597.5 0.5 copy-done.3
  598.1 0.5 copy-done.4
  598.5 2.2 fusion.8
  600.7 0.0 all-gather.2.cloned.1.call-update
  600.8 94.1 %all-gather.2.cloned.1.call-done = bf16[128,24576]{1,0:T(8,128)(2,1)} async-done(((bf16[16,24576]{1,0:T(8,128)(2,1)}), bf16[128,24576]{1,0:T(8,128)(2,1)}) %all-gather.2.cloned.1.call-update) | async-done | bytes 6291472 | tf_op jit(solution)/shard_map/all_gather | solution.py:45
  694.9 6.2 copy.67
  (5 shorter events, 0.0 us)
Async XLA Ops:
  7.2 4.7 copy-start
  7.2 163.7 %reduce-scatter.4.cloned.1.call-start = ((), (), s32[]{:S(2)}) async-start(), calls=%async_computation.3 | async-start | bytes 14155776 | tf_op jit(solution)/shard_map/reduce_scatter | solution.py:31
  34.9 553.3 %copy-start.2 = (f32[16,24576]{1,0:T(8,128)S(1)}, f32[16,24576]{1,0:T(8,128)}, u32[]{:S(2)}) copy-start(f32[16,24576]{1,0:T(8,128)} %param.9) | copy-start | bytes 4718596
  34.9 553.3 %all-reduce.2.cloned.1.call-start = ((), (), s32[]{:S(2)}) async-start(), calls=%async_computation.1 | async-start | bytes 3145728 | tf_op jit(solution)/shard_map/psum | solution.py:40
  170.9 523.9 %all-gather.2.cloned.1.call-start = ((), (), s32[]{:S(2)}) async-start(), calls=%async_computation.2 | async-start | bytes 7077888 | tf_op jit(solution)/shard_map/all_gather | solution.py:45
  596.1 1.4 copy-start.5
  596.4 1.7 copy-start.3
  596.4 2.1 copy-start.4
  694.9 6.2 copy-start.1
Sparse Core Ops, SparseCore 0:
  35.0 135.8 reduce-scatter.3
  173.5 414.5 all-reduce.1
  600.9 93.9 all-gather.1
where the time goes:
time: 709 us; the launch traced here: 708 us
  waiting for transfers between devices  647 us (91%)
  local copies, waits for them, and re-layouts  25.3 us (4%)
  other arithmetic  16.2 us (2%)
  between operations  13.8 us (2%)
    psum x1, waiting for transfers between devices, shards(): gradient = lax.psum(partial_grad, 'rep')  417 us
    reduce_scatter x1, waiting for transfers between devices, shards(): lax.psum_scatter(jnp.concatenate([triple.reshape(lax.axis_size('shard') *...  136 us
    all_gather x1, waiting for transfers between devices, shards(): lax.all_gather(new_master.astype(jnp.bfloat16), 'shard', axis=0, tiled=True)  94.1 us
    unnamed x16, local copies, waits for them, and re-layouts  22.2 us
  transfers between devices with their start and end apart: 3, of which 3 were waited for; matrix products, arithmetic and copies ran while one was open for 0% of the time, Pallas kernels for 0%

commit v1 on v0

v1 whole, which is shorter than its diff:
```python
import functools

import jax
import jax.numpy as jnp
from jax import lax
from jax.experimental import pallas as pl
from jax.experimental.pallas import tpu as pltpu
from jax.sharding import Mesh
from jax.sharding import PartitionSpec as P

beta_one = 0.9
beta_two = 0.95
learn_rate = 0.002
bias_one = 1.0 - 0.9**10
bias_two = 1.0 - 0.95**10

REP = ("y", "x", "zh")
SHARD = ("zl", "c")
NY, NX, NZH, NZL, NC = 4, 4, 2, 4, 2
PLANE = NY * NX
PROJ = 4
SEND_SCALE = 128.0
UNIT_SCALE = 32768.0


def adam_update(gradient, master, moment, second):
    new_moment = beta_one * moment + (1.0 - beta_one) * gradient
    new_second = beta_two * second + (1.0 - beta_two) * gradient * gradient
    stepped = master - learn_rate * (new_moment / bias_one) / (
        jnp.sqrt(new_second / bias_two) + 1e-08
    )
    return (stepped, new_moment, new_second)


def terms_kernel(core_ref, g0_ref, g1_ref, x0_ref, x1_ref, a0_ref, a1_ref, out_ref, left_ref):
    rows = out_ref.shape[0]
    tokens, columns = g0_ref.shape

    @pl.when(pl.program_id(0) == 0)
    def _():
        m = lax.broadcasted_iota(jnp.int32, (rows, columns), 0)
        j = lax.broadcasted_iota(jnp.int32, (rows, columns), 1)
        k = m & 3
        want = 128 * ((m >> 2) & 3) + 64 * core_ref[0] + 4 * (m >> 4) + k
        pick = jnp.where(j == want, 1.0, 0.0)
        for which in range(2):
            keep = (k == 3) if which else (k < 3)
            chosen = jnp.where(keep, pick, 0.0).astype(jnp.bfloat16)
            for at, g_ref in enumerate((g0_ref, g1_ref)):
                left_ref[2 * which + at] = lax.dot_general(
                    chosen, g_ref[...], (((1,), (1,)), ((), ())), preferred_element_type=jnp.float32
                ).astype(jnp.bfloat16)

    total = jnp.dot(left_ref[0], x0_ref[...], preferred_element_type=jnp.float32)
    total += jnp.dot(left_ref[1], x1_ref[...], preferred_element_type=jnp.float32)
    total += jnp.dot(left_ref[2], a0_ref[...], preferred_element_type=jnp.float32)
    total += jnp.dot(left_ref[3], a1_ref[...], preferred_element_type=jnp.float32)
    out_ref[...] = total * SEND_SCALE


def terms(core, g0, g1, x0, x1, a0, a1, tile=1024):
    tokens, width = x0.shape
    rows = g0.shape[1] // NC
    whole = pl.BlockSpec(g0.shape, lambda j: (0, 0))
    block = pl.BlockSpec((tokens, tile), lambda j: (0, j))
    return pl.pallas_call(
        terms_kernel,
        grid=(width // tile,),
        in_specs=[pl.BlockSpec(memory_space=pltpu.SMEM), whole, whole, block, block, block, block],
        out_specs=pl.BlockSpec((rows, tile), lambda j: (0, j)),
        out_shape=jax.ShapeDtypeStruct((rows, width), jnp.float32),
        scratch_shapes=[pltpu.VMEM((4, rows, tokens), jnp.bfloat16)],
        compiler_params=pltpu.CompilerParams(vmem_limit_bytes=32 * 2**20),
        cost_estimate=pl.CostEstimate(
            flops=8 * rows * tokens * width, bytes_accessed=10 * tokens * width, transcendentals=0
        ),
        name="terms",
    )(core, g0, g1, x0, x1, a0, a1)


def step_kernel(u_ref, master_ref, moment_ref, second_ref, nm_ref, mo_ref, se_ref, grad_ref):
    k = pl.program_id(0)
    rows, width = master_ref.shape

    @pl.when(k == 0)
    def _():
        parts = u_ref.shape[0]
        m = lax.broadcasted_iota(jnp.int32, (PROJ * rows, parts), 0)
        j = lax.broadcasted_iota(jnp.int32, (PROJ * rows, parts), 1)
        first = (m & 15) * 24 + 16 + (m >> 4)
        pick = jnp.where((j == first) | (j == first + PROJ), 1.0, 0.0).astype(jnp.bfloat16)
        grad_ref[...] = jnp.dot(
            pick, u_ref[...], preferred_element_type=jnp.float32
        )

    gradient = grad_ref[pl.ds(pl.multiple_of(k * rows, rows), rows), :]
    stepped, new_moment, new_second = adam_update(
        gradient, master_ref[...], moment_ref[...], second_ref[...]
    )
    mo_ref[...] = new_moment
    se_ref[...] = new_second
    scale = jnp.sqrt(jnp.sum(stepped * stepped, axis=1, keepdims=True) + 1e-06)
    nm_ref[...] = stepped / scale


def step(u, master, moment, second):
    rows, width = master.shape
    width //= PROJ
    block = pl.BlockSpec((rows, width), lambda k: (0, k))
    return pl.pallas_call(
        step_kernel,
        grid=(PROJ,),
        in_specs=[pl.BlockSpec(u.shape, lambda k: (0, 0)), block, block, block],
        out_specs=[block, block, block],
        out_shape=[jax.ShapeDtypeStruct(master.shape, jnp.float32)] * 3,
        scratch_shapes=[pltpu.VMEM((PROJ * rows, width), jnp.float32)],
        compiler_params=pltpu.CompilerParams(vmem_limit_bytes=40 * 2**20),
        cost_estimate=pl.CostEstimate(
            flops=2 * 64 * 384 * width, bytes_accessed=24 * rows * width * PROJ, transcendentals=0
        ),
        name="step",
    )(u, master, moment, second)


def lay_kernel(core_ref, own_ref, other_ref, out_ref):
    j = pl.program_id(0)
    parts, tile = own_ref.shape
    width = tile * pl.num_programs(0)
    m = lax.broadcasted_iota(jnp.int32, (256, parts), 0)
    n = lax.broadcasted_iota(jnp.int32, (256, parts), 1)
    pick = jnp.where(n == (m & 15) * 24 + ((m >> 4) & 3) * 4 + (m >> 6), 1.0, 0.0)
    pick = pick.astype(jnp.bfloat16)

    def rows_of(ref):
        picked = jnp.dot(pick, ref[...], preferred_element_type=jnp.float32)
        return (picked * (1.0 / UNIT_SCALE)).astype(out_ref.dtype)

    own, other = rows_of(own_ref), rows_of(other_ref)
    mine = core_ref[0] == 0
    low, high = jnp.where(mine, own, other), jnp.where(mine, other, own)
    for k in range(PROJ):
        at = pl.ds(pl.multiple_of(k * width + j * tile, 128), tile)
        for zl in range(NZL):
            part = slice(64 * k + 16 * zl, 64 * k + 16 * zl + 16)
            out_ref[32 * zl : 32 * zl + 16, at] = low[part]
            out_ref[32 * zl + 16 : 32 * zl + 32, at] = high[part]


def lay(core, own, other, rows, tile=1024):
    parts, width = own.shape
    block = pl.BlockSpec((parts, tile), lambda j: (0, j))
    return pl.pallas_call(
        lay_kernel,
        grid=(width // tile,),
        in_specs=[pl.BlockSpec(memory_space=pltpu.SMEM), block, block],
        out_specs=pl.BlockSpec((rows, PROJ * width), lambda j: (0, 0)),
        out_shape=jax.ShapeDtypeStruct((rows, PROJ * width), jnp.bfloat16),
        compiler_params=pltpu.CompilerParams(vmem_limit_bytes=40 * 2**20),
        cost_estimate=pl.CostEstimate(
            flops=4 * 256 * parts * width, bytes_accessed=8 * parts * width, transcendentals=0
        ),
        name="lay",
    )(core, own, other)


def shards(x_in, attn_out, grads_out, master, moment, second):
    width = x_in.shape[1]
    swap = [(0, 1), (1, 0)]
    core = lax.axis_index("c").reshape(1).astype(jnp.int32)
    x_other = lax.ppermute(x_in, "c", swap)
    g_other = lax.ppermute(grads_out, "c", swap)
    a_other = lax.ppermute(attn_out, "c", swap)
    sent = terms(core, grads_out, g_other, x_in, x_other, attn_out, a_other)
    with jax.named_scope("plane_sum"):
        came = lax.all_to_all(
            sent.astype(jnp.float16).reshape(PLANE, NZL * PROJ, width), ("y", "x"), 0, 0, tiled=True
        )
        part = jnp.sum(came.astype(jnp.float32), axis=0) * (1.0 / SEND_SCALE)
    with jax.named_scope("depth_sum"):
        came = lax.all_to_all(part.reshape(NZL, PROJ, width), "zl", 0, 0, tiled=True)
        half = jnp.sum(came, axis=0)
        gradient = half + lax.ppermute(half, "zh", swap)
    with jax.named_scope("own_row"):
        row = lax.axis_index("y") * NX + lax.axis_index("x")

        def piece(a):
            return lax.dynamic_slice(a, (row, 0), (1, PROJ * width)).reshape(PROJ, width)

        stepped, _, _ = adam_update(gradient, piece(master), piece(moment), piece(second))
        scale = jnp.sqrt(jnp.sum(stepped * stepped, axis=1, keepdims=True) + 1e-06)
        unit = lax.reduce_precision(stepped / scale, 8, 7)
        unit = (unit * UNIT_SCALE).astype(jnp.float16)
        coarse = lax.reduce_precision(gradient, 8, 7)
        fine = (gradient - coarse).astype(jnp.float16)
        coarse = coarse.astype(jnp.float16)
    with jax.named_scope("depth_gather"):
        units = lax.all_to_all(
            jnp.broadcast_to(unit[None], (NZL, PROJ, width)), "zl", 0, 0, tiled=True
        )
    with jax.named_scope("plane_gather"):
        payload = jnp.concatenate([units.reshape(NZL * PROJ, width), coarse, fine], axis=0)
        own = lax.all_gather(payload, ("y", "x"), axis=0, tiled=True).astype(jnp.bfloat16)
    other = lax.ppermute(own, "c", swap)
    new_master, new_moment, new_second = step(own, master, moment, second)
    gathered = lay(core, own, other, NZL * NC * master.shape[0])
    return (new_master, new_moment, new_second, gathered)


def solution(mesh):
    fine = Mesh(mesh.devices.reshape(NY, NX, NZH, NZL, NC), REP + SHARD)
    tokens = P(REP + SHARD, None)
    rows = P(SHARD, None)
    return jax.shard_map(
        shards,
        mesh=fine,
        in_specs=(tokens, tokens, tokens, rows, rows, rows),
        out_specs=(rows, rows, rows, P()),
        check_vma=False,
    )
```

time: 709 us -> 158 us (0.22)
  waiting for transfers between devices: 647 us -> 11.2 us
  blocking collectives: 0 us -> 95.8 us
  local copies, waits for them, and re-layouts: 25.3 us -> 5.63 us
  Pallas kernels: 0 us -> 19.6 us
  starting transfers between devices: 0.12 us -> 17.2 us
  between operations: 13.8 us -> 0.75 us
  other arithmetic: 16.2 us -> 7.31 us
    psum x1 -> x0, waiting for transfers between devices: 417 us -> none  [shards(): gradient = lax.psum(partial_grad, 'rep')]
    reduce_scatter x1 -> x0, waiting for transfers between devices: 136 us -> none  [shards(): lax.psum_scatter(jnp.concatenate([triple.reshape(lax.axis_size('shard') *...]
    all_gather x1 -> x0, waiting for transfers between devices: 94.1 us -> none  [shards(): lax.all_gather(new_master.astype(jnp.bfloat16), 'shard', axis=0, tiled=True)]
    all_to_all x0 -> x3, blocking collectives: none -> 68 us  [the longest x1 43.6 us: shards(): lax.all_to_all(sent.astype(jnp.float16).reshape(PLANE, NZL * PROJ, width)...]
    all_gather x0 -> x1, blocking collectives: none -> 27.9 us  [shards(): lax.all_gather(payload, ('y', 'x'), axis=0, tiled=True).astype(jnp.bfloat16)]
    pallas_call x0 -> x3, Pallas kernels: none -> 19.6 us  [the longest x1 7.83 us: lay(): pl.pallas_call(lay_kernel, grid=(width // tile,), in_specs=[pl.BlockSpec(...]
    unnamed x16 -> x12, local copies, waits for them, and re-layouts: 22.2 us -> 4.27 us
    ppermute x0 -> x5, starting transfers between devices: none -> 17.2 us  [the longest x1 8.65 us: shards(): other = lax.ppermute(own, 'c', swap)]
  transfers between devices with their start and end apart: 3 -> 5, of which waited for: 3 -> 4; matrix products, arithmetic and copies ran while one was open for 0% -> 1% of each run, Pallas kernels for 0% -> 3%
where the time goes in v1:
time: 158 us
  blocking collectives  95.8 us (61%)
  Pallas kernels  19.6 us (12%)
  starting transfers between devices  17.2 us (11%)
  waiting for transfers between devices  11.2 us (7%)
  other arithmetic  7.31 us (5%)
  local copies, waits for them, and re-layouts  5.63 us (4%)
    all_to_all x1, blocking collectives, shards(): lax.all_to_all(sent.astype(jnp.float16).reshape(PLANE, NZL * PROJ, width)...  43.6 us
    all_gather x1, blocking collectives, shards(): lax.all_gather(payload, ('y', 'x'), axis=0, tiled=True).astype(jnp.bfloat16)  27.9 us
    all_to_all x1, blocking collectives, shards(): lax.all_to_all(part.reshape(NZL, PROJ, width), 'zl', 0, 0, tiled=True)  16 us
    ppermute x1, starting transfers between devices, shards(): other = lax.ppermute(own, 'c', swap)  8.65 us
    all_to_all x1, blocking collectives, shards(): lax.all_to_all(jnp.broadcast_to(unit[None], (NZL, PROJ, width)), 'zl', 0,...  8.35 us
    pallas_call x1, Pallas kernels, lay(): pl.pallas_call(lay_kernel, grid=(width // tile,), in_specs=[pl.BlockSpec(...  7.83 us
    pallas_call x1, Pallas kernels, terms(): pl.pallas_call(terms_kernel, grid=(width // tile,), in_specs=[pl.BlockSpe...  6.92 us
    ppermute x1, waiting for transfers between devices, shards(): g_other = lax.ppermute(grads_out, 'c', swap)  6.8 us
  transfers between devices with their start and end apart: 5, of which 4 were waited for; matrix products, arithmetic and copies ran while one was open for 1% of the time, Pallas kernels for 3%

profile of v1, /device:TPU:1, one launch (start us, length us, event | category | flops | bytes accessed | tf_op | source)
XLA Modules:
  0.0 157.5 jit_solution(4147121329290430579)
XLA Ops:
  0.6 3.3 %collective-permute-start.1 = (bf16[192,6144]{1,0:T(8,128)(2,1)}, bf16[192,6144]{1,0:T(8,128)(2,1)S(1)}, u32[]{:S(2)}, u32[]{:S(2)}) collective-permute-start(bf16[192,6144]{1,0:T(8,128)(2,1)} %x0_ref.1), channel_id=1, source_target_pairs={{0,1},{1,0},{2,3},{3,2},{4,5},{5,4},{6,7},{7,6},{8,9},{9,8},{10,11... | collective-permute-start | bytes 7077896 | tf_op jit(solution)/shard_map/ppermute | solution.py:170
  4.0 0.1 collective-permute-start.2
  4.1 0.4 collective-permute-start
  4.5 6.8 %collective-permute-done.g1_ref = bf16[192,512]{1,0:T(8,128)(2,1)S(1)} collective-permute-done((bf16[192,512]{1,0:T(8,128)(2,1)}, bf16[192,512]{1,0:T(8,128)(2,1)S(1)}, u32[]{:S(2)}, u32[]{:S(2)}) %collective-permute-start) | collective-permute-done | bytes 196640 | tf_op jit(solution)/shard_map/ppermute | solution.py:171
  11.3 0.8 collective-permute-done.2.a1_ref
  12.1 1.7 %copy-done = bf16[192,6144]{1,0:T(8,128)(2,1)S(1)} copy-done((bf16[192,6144]{1,0:T(8,128)(2,1)S(1)}, bf16[192,6144]{1,0:T(8,128)(2,1)}, u32[]{:S(2)}) %copy-start) | copy-done | bytes 2359320
  13.8 1.7 %copy-done.1 = bf16[192,6144]{1,0:T(8,128)(2,1)S(1)} copy-done((bf16[192,6144]{1,0:T(8,128)(2,1)S(1)}, bf16[192,6144]{1,0:T(8,128)(2,1)}, u32[]{:S(2)}) %copy-start.1) | copy-done | bytes 2359320
  15.5 0.9 copy-done.5
  16.4 6.9 %terms.1 = f32[256,6144]{1,0:T(8,128)S(1)} custom-call(s32[1]{0:T(128)} %bitcast.core_ref, bf16[192,512]{1,0:T(8,128)(2,1)S(1)} %copy-done.5, bf16[192,512]{1,0:T(8,128)(2,1)S(1)} %collective-permute-done.g1_ref, bf16[192,6144]{1,0:T(8,128)(2,1)S(1)} %copy-done, bf16[192,6144]{1,0:T(8,128)(2,1)S(1)} %collective-permute-done.1.x1_ref, ...), custom_call_target="tpu_custom_call" | custom-call | flops 2415919104 | bytes 11796480 | tf_op jit(solution)/shard_map/terms/pallas_call | solution.py:66
  23.3 0.4 convert_element_type.18
  23.7 43.6 %all_to_all.15 = f16[16,16,6144]{2,1,0:T(8,128)(2,1)S(1)} all-to-all(f16[16,16,6144]{2,1,0:T(8,128)(2,1)S(1)} %bitcast.2), channel_id=1, replica_groups=mesh['y'=4,'x'=4,'zh'=2,'zl'=4,'c'=2] {'y','x'}, dimensions={0} | all-to-all | bytes 6291456 | tf_op jit(solution)/shard_map/plane_sum/all_to_all | solution.py:175
  67.4 0.5 convert_reduce_fusion
  67.9 0.0 copy-start.2
  67.9 0.9 mul.67
  68.8 16.0 %all_to_all.16 = f32[4,4,6144]{2,1,0:T(4,128)S(1)} all-to-all(f32[4,4,6144]{2,1,0:T(4,128)} %mul.67), channel_id=1, replica_groups=mesh['y'=4,'x'=4,'zh'=2,'zl'=4,'c'=2] {'zl'}, dimensions={0} | all-to-all | bytes 786432 | tf_op jit(solution)/shard_map/depth_sum/all_to_all | solution.py:180
  84.7 0.7 reduce_sum.28
  85.5 4.7 %collective-permute-start.3 = (f32[4,6144]{1,0:T(4,128)}, f32[4,6144]{1,0:T(4,128)}, u32[]{:S(2)}, u32[]{:S(2)}) collective-permute-start(f32[4,6144]{1,0:T(4,128)} %reduce_sum.28), channel_id=1, source_target_pairs={{0,8},{8,0},{1,9},{9,1},{2,10},{10,2},{3,11},{11,3},{4,12},{12,4},... | collective-permute-start | bytes 294920 | tf_op jit(solution)/shard_map/depth_sum/ppermute | solution.py:182
  90.2 1.7 %multiply_reduce_fusion.1 = (f32[24576]{0:T(1024)S(1)}, f32[24576]{0:T(1024)S(1)}) fusion(f32[16,24576]{1,0:T(8,128)S(1)} %copy-done.3, s32[]{:T(128)S(6)} %select_n.2, f32[16,24576]{1,0:T(8,128)} %moment_ref.1), kind=kLoop, calls=%fused_computation.14 | loop fusion | flops 49152 | bytes 393220 | tf_op jit(solution)/shard_map/own_row/mul | solution.py:28
  92.0 0.3 dynamic-slice_reduce_fusion
  92.3 0.9 collective-permute-done.3
  93.2 1.9 %multiply_reduce_fusion = (f32[4]{0:T(128)S(1)}, f32[4,6144]{1,0:T(4,128)S(1)}, f16[4,6144]{1,0:T(4,128)(2,1)}, f16[4,6144]{1,0:T(4,128)(2,1)}) fusion(f32[4,6144]{1,0:T(4,128)S(1)} %reshape.37, f32[4,6144]{1,0:T(4,128)S(1)} %mul.74, f32[4,6144]{1,0:T(4,128)S(1)} %mul.64, f32[4,6144]{1,0:T(4,128)} %reduce_sum.28, f32[4,6144]{1,0:T(4,128)} %collective-permute-done.3), kind=kLoop, calls=%fused_computation.13 | loop fusion | flops 417788 | bytes 688144 | tf_op jit(solution)/shard_map/own_row/reduce_sum | solution.py:190
  95.1 0.1 multiply_convert_fusion
  95.2 0.1 broadcast_in_dim.2
  95.3 8.3 %all_to_all.17 = f16[4,4,6144]{2,1,0:T(4,128)(2,1)S(1)} all-to-all(f16[4,4,6144]{2,1,0:T(4,128)(2,1)S(1)} %broadcast_in_dim.2), channel_id=1, replica_groups=mesh['y'=4,'x'=4,'zh'=2,'zl'=4,'c'=2] {'zl'}, dimensions={0} | all-to-all | bytes 393216 | tf_op jit(solution)/shard_map/depth_gather/all_to_all | solution.py:197
  103.6 0.1 reshape.40
  103.7 0.9 pad_maximum_fusion
  104.6 27.9 %all-gather.1 = f16[384,6144]{1,0:T(8,128)(2,1)S(1)} all-gather(f16[24,6144]{1,0:T(8,128)(2,1)S(1)} %pad_maximum_fusion), channel_id=1, replica_groups=mesh['y'=4,'x'=4,'zh'=2,'zl'=4,'c'=2] {'y','x'}, dimensions={0}, use_global_device_ids=true | all-gather | bytes 5013504 | tf_op jit(solution)/shard_map/plane_gather/all_gather | solution.py:202
  132.5 1.0 convert_element_type.23.u_ref.own_ref
  133.5 8.7 %collective-permute-start.4 = (bf16[384,6144]{1,0:T(8,128)(2,1)S(1)}, bf16[384,6144]{1,0:T(8,128)(2,1)S(1)}, u32[]{:S(2)}, u32[]{:S(2)}) collective-permute-start(bf16[384,6144]{1,0:T(8,128)(2,1)S(1)} %convert_element_type.23.u_ref.own_ref), channel_id=1, source_target_pairs={{0,1},{1,0},{2,3},{3,2},{4,5},{5,4},{6,7},{7,6},{8,9},{9,8},{10,11... | collective-permute-start | bytes 14155784 | tf_op jit(solution)/shard_map/ppermute | solution.py:203
  142.2 4.9 %step.1 = (f32[16,24576]{1,0:T(8,128)}, f32[16,24576]{1,0:T(8,128)}, f32[16,24576]{1,0:T(8,128)}) custom-call(bf16[384,6144]{1,0:T(8,128)(2,1)S(1)} %convert_element_type.23.u_ref.own_ref, f32[16,24576]{1,0:T(8,128)S(1)} %copy-done.2, f32[16,24576]{1,0:T(8,128)S(1)} %copy-done.4, f32[16,24576]{1,0:T(8,128)S(1)} %copy-done.3), custom_call_target="tpu_custom_call" | custom-call | flops 301989888 | bytes 9437184 | tf_op jit(solution)/shard_map/step/pallas_call | solution.py:110
  147.1 2.6 %collective-permute-done.4.other_ref = bf16[384,6144]{1,0:T(8,128)(2,1)S(1)} collective-permute-done((bf16[384,6144]{1,0:T(8,128)(2,1)S(1)}, bf16[384,6144]{1,0:T(8,128)(2,1)S(1)}, u32[]{:S(2)}, u32[]{:S(2)}) %collective-permute-start.4) | collective-permute-done | bytes 4718624 | tf_op jit(solution)/shard_map/ppermute | solution.py:203
  149.7 7.8 %lay.1 = bf16[128,24576]{1,0:T(8,128)(2,1)} custom-call(s32[1]{0:T(128)} %bitcast.core_ref, bf16[384,6144]{1,0:T(8,128)(2,1)S(1)} %convert_element_type.23.u_ref.own_ref, bf16[384,6144]{1,0:T(8,128)(2,1)S(1)} %collective-permute-done.4.other_ref), custom_call_target="tpu_custom_call" | custom-call | flops 2415919104 | bytes 18874368 | tf_op jit(solution)/shard_map/lay/pallas_call | solution.py:152
  (14 shorter events, 0.2 us)
Async XLA Ops:
  0.6 10.6 %collective-permute-start.1 = (bf16[192,6144]{1,0:T(8,128)(2,1)}, bf16[192,6144]{1,0:T(8,128)(2,1)S(1)}, u32[]{:S(2)}, u32[]{:S(2)}) collective-permute-start(bf16[192,6144]{1,0:T(8,128)(2,1)} %x0_ref.1), channel_id=1, source_target_pairs={{0,1},{1,0},{2,3},{3,2},{4,5},{5,4},{6,7},{7,6},{8,9},{9,8},{10,11... | collective-permute-start | bytes 7077896 | tf_op jit(solution)/shard_map/ppermute | solution.py:170
  4.0 8.2 %collective-permute-start.2 = (bf16[192,6144]{1,0:T(8,128)(2,1)}, bf16[192,6144]{1,0:T(8,128)(2,1)}, u32[]{:S(2)}, u32[]{:S(2)}) collective-permute-start(bf16[192,6144]{1,0:T(8,128)(2,1)} %a0_ref.1), channel_id=1, source_target_pairs={{0,1},{1,0},{2,3},{3,2},{4,5},{5,4},{6,7},{7,6},{8,9},{9,8},{10,11... | collective-permute-start | bytes 7077896 | tf_op jit(solution)/shard_map/ppermute | solution.py:172
  4.1 7.2 %collective-permute-start = (bf16[192,512]{1,0:T(8,128)(2,1)}, bf16[192,512]{1,0:T(8,128)(2,1)S(1)}, u32[]{:S(2)}, u32[]{:S(2)}) collective-permute-start(bf16[192,512]{1,0:T(8,128)(2,1)} %g0_ref.1), channel_id=1, source_target_pairs={{0,1},{1,0},{2,3},{3,2},{4,5},{5,4},{6,7},{7,6},{8,9},{9,8},{10,11... | collective-permute-start | bytes 589832 | tf_op jit(solution)/shard_map/ppermute | solution.py:171
  12.1 1.7 %copy-start = (bf16[192,6144]{1,0:T(8,128)(2,1)S(1)}, bf16[192,6144]{1,0:T(8,128)(2,1)}, u32[]{:S(2)}) copy-start(bf16[192,6144]{1,0:T(8,128)(2,1)} %x0_ref.1) | copy-start | bytes 7077892
  13.8 1.7 %copy-start.1 = (bf16[192,6144]{1,0:T(8,128)(2,1)S(1)}, bf16[192,6144]{1,0:T(8,128)(2,1)}, u32[]{:S(2)}) copy-start(bf16[192,6144]{1,0:T(8,128)(2,1)} %a0_ref.1) | copy-start | bytes 7077892
  15.4 0.9 copy-start.5
  67.4 22.8 %copy-start.3 = (f32[16,24576]{1,0:T(8,128)S(1)}, f32[16,24576]{1,0:T(8,128)}, u32[]{:S(2)}) copy-start(f32[16,24576]{1,0:T(8,128)} %second_ref.1) | copy-start | bytes 4718596
  67.9 24.1 %copy-start.2 = (f32[16,24576]{1,0:T(8,128)S(1)}, f32[16,24576]{1,0:T(8,128)}, u32[]{:S(2)}) copy-start(f32[16,24576]{1,0:T(8,128)} %master_ref.1) | copy-start | bytes 4718596
  85.5 7.7 %collective-permute-start.3 = (f32[4,6144]{1,0:T(4,128)}, f32[4,6144]{1,0:T(4,128)}, u32[]{:S(2)}, u32[]{:S(2)}) collective-permute-start(f32[4,6144]{1,0:T(4,128)} %reduce_sum.28), channel_id=1, source_target_pairs={{0,8},{8,0},{1,9},{9,1},{2,10},{10,2},{3,11},{11,3},{4,12},{12,4},... | collective-permute-start | bytes 294920 | tf_op jit(solution)/shard_map/depth_sum/ppermute | solution.py:182
  132.5 9.7 %copy-start.4 = (f32[16,24576]{1,0:T(8,128)S(1)}, f32[16,24576]{1,0:T(8,128)}, u32[]{:S(2)}) copy-start(f32[16,24576]{1,0:T(8,128)} %moment_ref.1) | copy-start | bytes 4718596
  133.5 16.2 %collective-permute-start.4 = (bf16[384,6144]{1,0:T(8,128)(2,1)S(1)}, bf16[384,6144]{1,0:T(8,128)(2,1)S(1)}, u32[]{:S(2)}, u32[]{:S(2)}) collective-permute-start(bf16[384,6144]{1,0:T(8,128)(2,1)S(1)} %convert_element_type.23.u_ref.own_ref), channel_id=1, source_target_pairs={{0,1},{1,0},{2,3},{3,2},{4,5},{5,4},{6,7},{7,6},{8,9},{9,8},{10,11... | collective-permute-start | bytes 14155784 | tf_op jit(solution)/shard_map/ppermute | solution.py:203

commit v2 on v1

v2 whole, which is shorter than its diff:
```python
import functools

import jax
import jax.numpy as jnp
from jax import lax
from jax.experimental import pallas as pl
from jax.experimental.pallas import tpu as pltpu
from jax.sharding import Mesh
from jax.sharding import PartitionSpec as P

beta_one = 0.9
beta_two = 0.95
learn_rate = 0.002
bias_one = 1.0 - 0.9**10
bias_two = 1.0 - 0.95**10

REP = ("y", "x", "zh")
SHARD = ("zl", "c")
NY, NX, NZH, NZL, NC = 4, 4, 2, 4, 2
PLANE = NY * NX
PROJ = 4
SEND_SCALE = 128.0
UNIT_SCALE = 32768.0


def adam_update(gradient, master, moment, second):
    new_moment = beta_one * moment + (1.0 - beta_one) * gradient
    new_second = beta_two * second + (1.0 - beta_two) * gradient * gradient
    stepped = master - learn_rate * (new_moment / bias_one) / (
        jnp.sqrt(new_second / bias_two) + 1e-08
    )
    return (stepped, new_moment, new_second)


def pick_rows(place_ref, g_ref, left_ref, x_first):
    shape = (left_ref.shape[1], g_ref.shape[1])
    m = lax.broadcasted_iota(jnp.int32, shape, 0)
    j = lax.broadcasted_iota(jnp.int32, shape, 1)
    k = m & 3
    first, second = m >> 6, (m >> 4) & 3
    along_x, along_y = (first, second) if x_first else (second, first)
    i = 4 * ((place_ref[3] + along_y) & 3) + ((place_ref[2] + along_x) & 3)
    want = 128 * ((place_ref[1] + (m >> 2)) & 3) + 64 * place_ref[0] + 4 * i + k
    for at, mine in enumerate((k < 3, k == 3)):
        chosen = jnp.where((j == want) & mine, 1.0, 0.0).astype(jnp.bfloat16)
        left_ref[at] = lax.dot_general(
            chosen, g_ref[...], (((1,), (1,)), ((), ())), preferred_element_type=jnp.float32
        ).astype(jnp.bfloat16)


def two_dots(left_ref, x_ref, a_ref):
    total = jnp.dot(left_ref[0], x_ref[...], preferred_element_type=jnp.float32)
    return total + jnp.dot(left_ref[1], a_ref[...], preferred_element_type=jnp.float32)


def own_kernel(x_first, place_ref, g_ref, x_ref, a_ref, out_ref, left_ref):
    @pl.when(pl.program_id(0) == 0)
    def _():
        pick_rows(place_ref, g_ref, left_ref, x_first)

    out_ref[...] = two_dots(left_ref, x_ref, a_ref)


def other_kernel(x_first, place_ref, g_ref, x_ref, a_ref, base_ref, out_ref, left_ref):
    @pl.when(pl.program_id(0) == 0)
    def _():
        pick_rows(place_ref, g_ref, left_ref, x_first)

    out_ref[...] = (two_dots(left_ref, x_ref, a_ref) + base_ref[...]) * SEND_SCALE


def terms(x_first, place, g, x, a, base=None, tile=1024):
    tokens, width = x.shape
    width //= 2
    rows = g.shape[1] // NC
    skip = 0 if x_first else width // tile
    block = pl.BlockSpec((tokens, tile), lambda j: (0, skip + j))
    result = pl.BlockSpec((rows, tile), lambda j: (0, j))
    bases = [] if base is None else [base]
    return pl.pallas_call(
        functools.partial(own_kernel if base is None else other_kernel, x_first),
        grid=(width // tile,),
        in_specs=[
            pl.BlockSpec(memory_space=pltpu.SMEM),
            pl.BlockSpec(g.shape, lambda j: (0, 0)),
            block,
            block,
        ]
        + [result] * len(bases),
        out_specs=result,
        out_shape=jax.ShapeDtypeStruct((rows, width), jnp.float32),
        scratch_shapes=[pltpu.VMEM((2, rows, tokens), jnp.bfloat16)],
        compiler_params=pltpu.CompilerParams(vmem_limit_bytes=24 * 2**20),
        cost_estimate=pl.CostEstimate(
            flops=4 * rows * tokens * width, bytes_accessed=8 * tokens * width, transcendentals=0
        ),
        name="own_terms" if base is None else "pair_terms",
    )(place, g, x, a, *bases)


def step_kernel(u_ref, master_ref, moment_ref, second_ref, nm_ref, mo_ref, se_ref, grad_ref):
    k = pl.program_id(0)
    rows, width = master_ref.shape

    @pl.when(k == 0)
    def _():
        parts = u_ref.shape[0]
        m = lax.broadcasted_iota(jnp.int32, (PROJ * rows, parts), 0)
        j = lax.broadcasted_iota(jnp.int32, (PROJ * rows, parts), 1)
        first = (m & 15) * 2 * PROJ + (m >> 4)
        pick = jnp.where((j == first) | (j == first + PROJ), 1.0, 0.0).astype(jnp.bfloat16)
        grad_ref[...] = jnp.dot(
            pick, u_ref[...], preferred_element_type=jnp.float32
        )

    gradient = grad_ref[pl.ds(pl.multiple_of(k * rows, rows), rows), :]
    stepped, new_moment, new_second = adam_update(
        gradient, master_ref[...], moment_ref[...], second_ref[...]
    )
    mo_ref[...] = new_moment
    se_ref[...] = new_second
    scale = jnp.sqrt(jnp.sum(stepped * stepped, axis=1, keepdims=True) + 1e-06)
    nm_ref[...] = stepped / scale


def step(u, master, moment, second):
    rows, width = master.shape
    width //= PROJ
    block = pl.BlockSpec((rows, width), lambda k: (0, k))
    return pl.pallas_call(
        step_kernel,
        grid=(PROJ,),
        in_specs=[pl.BlockSpec(u.shape, lambda k: (0, 0)), block, block, block],
        out_specs=[block, block, block],
        out_shape=[jax.ShapeDtypeStruct(master.shape, jnp.float32)] * 3,
        scratch_shapes=[pltpu.VMEM((PROJ * rows, width), jnp.float32)],
        compiler_params=pltpu.CompilerParams(vmem_limit_bytes=40 * 2**20),
        cost_estimate=pl.CostEstimate(
            flops=2 * 64 * 128 * width, bytes_accessed=24 * rows * width * PROJ, transcendentals=0
        ),
        name="step",
    )(u, master, moment, second)


def lay_kernel(place_ref, own_ref, other_ref, out_ref, held_ref, sems):
    j = pl.program_id(0)
    last = pl.num_programs(0) - 1
    parts, tile = own_ref.shape
    width = tile * (last + 1)
    slot = lax.rem(j, 2)

    def copies(step, slot):
        for k in range(PROJ):
            at = pl.ds(pl.multiple_of(k * width + step * tile, 128), tile)
            yield pltpu.make_async_copy(held_ref.at[slot, k], out_ref.at[:, at], sems.at[slot, k])

    @pl.when(j >= 2)
    def _():
        for copy in copies(j - 2, slot):
            copy.wait()

    m = lax.broadcasted_iota(jnp.int32, (256, parts), 0)
    n = lax.broadcasted_iota(jnp.int32, (256, parts), 1)
    wanted = n == (m & 15) * 16 + ((m >> 4) & 3) * 4 + (m >> 6)
    pick = jnp.where(wanted, 1.0 / UNIT_SCALE, 0.0).astype(jnp.bfloat16)
    for ref, core in ((own_ref, place_ref[0]), (other_ref, 1 - place_ref[0])):
        rows = jnp.dot(pick, ref[...], preferred_element_type=jnp.float32).astype(out_ref.dtype)
        for k in range(PROJ):
            for zl in range(NZL):
                to = pl.ds(pl.multiple_of(32 * zl + 16 * core, 16), 16)
                held_ref[slot, k, to] = rows[64 * k + 16 * zl : 64 * k + 16 * zl + 16]
    for copy in copies(j, slot):
        copy.start()

    @pl.when(j == last)
    def _():
        for copy in copies(j - 1, 1 - slot):
            copy.wait()
        for copy in copies(j, slot):
            copy.wait()


def lay(place, own, other, rows, tile=1024):
    parts, width = own.shape
    block = pl.BlockSpec((parts, tile), lambda j: (0, j))
    return pl.pallas_call(
        lay_kernel,
        grid=(width // tile,),
        in_specs=[pl.BlockSpec(memory_space=pltpu.SMEM), block, block],
        out_specs=pl.BlockSpec(memory_space=pl.ANY),
        out_shape=jax.ShapeDtypeStruct((rows, PROJ * width), jnp.bfloat16),
        scratch_shapes=[
            pltpu.VMEM((2, PROJ, rows, tile), jnp.bfloat16),
            pltpu.SemaphoreType.DMA((2, PROJ)),
        ],
        compiler_params=pltpu.CompilerParams(vmem_limit_bytes=24 * 2**20),
        cost_estimate=pl.CostEstimate(
            flops=4 * 256 * parts * width, bytes_accessed=8 * parts * width, transcendentals=0
        ),
        name="lay",
    )(place, own, other)


def shards(x_in, attn_out, grads_out, master, moment, second):
    width = x_in.shape[1]
    swap = [(0, 1), (1, 0)]
    place = jnp.stack([lax.axis_index(name) for name in ("c", "zl", "x", "y")]).astype(jnp.int32)
    half = width // 2

    def along(a, axis, by):
        return lax.ppermute(a, axis, [(i, (i + by) % 4) for i in range(4)])

    def ahead(a, by):
        ring = NZH * NZL
        return lax.ppermute(a, ("zh", "zl"), [(z, (z + by) % ring) for z in range(ring)])

    def shared(blocks, axis, scale):
        sent = (blocks[1:] * scale).astype(jnp.float16)
        came = [along(sent[n - 1], axis, n).astype(jnp.float32) for n in (1, 3, 2)]
        return blocks[0] * scale + came[0] + came[1] + came[2]

    with jax.named_scope("pair"):
        g_other = lax.ppermute(grads_out, "c", swap)
        x_other = lax.ppermute(x_in, "c", swap)
        a_other = lax.ppermute(attn_out, "c", swap)
        first = terms(True, place, grads_out, x_in, attn_out)
        first, place = lax.optimization_barrier((first, place))
        second_half = terms(False, place, grads_out, x_in, attn_out)
        second_half, place = lax.optimization_barrier((second_half, place))
    with jax.named_scope("first"):
        first = terms(True, place, g_other, x_other, a_other, first)
        first, place_later = lax.optimization_barrier((first, place))
        first = shared(first.reshape(NX, -1, half), "x", 1.0)
        first = shared(first.reshape(NY, -1, half), "y", 0.25)
    with jax.named_scope("second"):
        second_half = terms(False, place_later, g_other, x_other, a_other, second_half)
        second_half = shared(second_half.reshape(NY, -1, half), "y", 1.0)
        second_half = shared(second_half.reshape(NX, -1, half), "x", 0.25)
    with jax.named_scope("depth_sum"):
        part = jnp.concatenate([first, second_half], axis=1) * (4.0 / SEND_SCALE)
        part = part.reshape(NZL, PROJ, width)
        part = part[0] + ahead(part[1], 1) + ahead(part[3], 7) + ahead(part[2], 2)
        gradient = part + lax.ppermute(part, "zh", swap)
    with jax.named_scope("own_row"):
        row = lax.axis_index("y") * NX + lax.axis_index("x")

        def piece(a):
            return lax.dynamic_slice(a, (row, 0), (1, PROJ * width)).reshape(PROJ, width)

        stepped, _, _ = adam_update(gradient, piece(master), piece(moment), piece(second))
        scale = jnp.sqrt(jnp.sum(stepped * stepped, axis=1, keepdims=True) + 1e-06)
        unit = lax.reduce_precision(stepped / scale, 8, 7)
        unit = (unit * UNIT_SCALE).astype(jnp.float16)
        coarse = lax.reduce_precision(gradient, 8, 7)
        fine = (gradient - coarse).astype(jnp.float16)
        coarse = coarse.astype(jnp.float16)
    with jax.named_scope("depth_gather"):
        units = lax.all_to_all(
            jnp.broadcast_to(unit[None], (NZL, PROJ, width)), "zl", 0, 0, tiled=True
        )
    with jax.named_scope("plane_gather"):
        payload = jnp.concatenate([units.reshape(NZL * PROJ, width), coarse, fine], axis=0)
        own = lax.all_gather(payload, ("y", "x"), axis=0, tiled=True).astype(jnp.bfloat16)
        own = own.reshape(PLANE, 24, width)
        grads = own[:, NZL * PROJ :].reshape(2 * PLANE * PROJ, width)
        own = own[:, : NZL * PROJ].reshape(PLANE * NZL * PROJ, width)
    other = lax.ppermute(own, "c", swap)
    new_master, new_moment, new_second = step(grads, master, moment, second)
    gathered = lay(place, own, other, NZL * NC * master.shape[0])
    return (new_master, new_moment, new_second, gathered)


def solution(mesh):
    fine = Mesh(mesh.devices.reshape(NY, NX, NZH, NZL, NC), REP + SHARD)
    tokens = P(REP + SHARD, None)
    rows = P(SHARD, None)
    return jax.shard_map(
        shards,
        mesh=fine,
        in_specs=(tokens, tokens, tokens, rows, rows, rows),
        out_specs=(rows, rows, rows, P()),
        check_vma=False,
    )
```

time: 158 us -> 142 us (0.90)
  blocking collectives: 95.8 us -> 36.1 us
  starting transfers between devices: 17.2 us -> 46 us
  waiting for transfers between devices: 11.2 us -> 23.8 us
  Pallas kernels: 19.6 us -> 21.7 us
    all_to_all x2 -> x0, blocking collectives: 59.6 us -> none  [the longest x1 43.6 us: shards(): lax.all_to_all(sent.astype(jnp.float16).reshape(PLANE, NZL * PROJ, width)...]
    ppermute x1 -> x16, waiting for transfers between devices: 0.87 us -> 23 us  [the longest x12 15.4 us: along(): return lax.ppermute(a, axis, [(i, (i + by) % 4) for i in range(4)])]
    ppermute x1 -> x16, starting transfers between devices: 4.74 us -> 26 us  [the longest x12 16.3 us: along(): return lax.ppermute(a, axis, [(i, (i + by) % 4) for i in range(4)])]
    ppermute x1, starting transfers between devices: 8.65 us -> 16.2 us  [shards(): other = lax.ppermute(own, 'c', swap)]
    ppermute x1, waiting for transfers between devices: 6.8 us -> 0.01 us  [shards(): g_other = lax.ppermute(grads_out, 'c', swap)]
    pallas_call x1 -> x4, Pallas kernels: 6.92 us -> 11.9 us  [terms(): pl.pallas_call(functools.partial(own_kernel if base is None else other_ke...]
    pallas_call x1, Pallas kernels: 7.83 us -> 5.44 us  [lay(): pl.pallas_call(lay_kernel, grid=(width // tile,), in_specs=[pl.BlockSpec(...]
    ppermute x1, waiting for transfers between devices: 2.64 us -> 0.79 us  [shards(): other = lax.ppermute(own, 'c', swap)]
  transfers between devices with their start and end apart: 5 -> 20, of which waited for: 4 -> 10; matrix products, arithmetic and copies ran while one was open for 1% -> 2% of each run, Pallas kernels for 3% -> 7%
where the time goes in v2:
time: 142 us
  starting transfers between devices  46 us (32%)
  blocking collectives  36.1 us (25%)
  waiting for transfers between devices  23.8 us (17%)
  Pallas kernels  21.7 us (15%)
  other arithmetic  7.11 us (5%)
  local copies, waits for them, and re-layouts  5.81 us (4%)
    all_gather x1, blocking collectives, shards(): lax.all_gather(payload, ('y', 'x'), axis=0, tiled=True).astype(jnp.bfloat16)  27.9 us
    ppermute x12, starting transfers between devices, along(): return lax.ppermute(a, axis, [(i, (i + by) % 4) for i in range(4)])  16.3 us
    ppermute x1, starting transfers between devices, shards(): other = lax.ppermute(own, 'c', swap)  16.2 us
    ppermute x12, waiting for transfers between devices, along(): return lax.ppermute(a, axis, [(i, (i + by) % 4) for i in range(4)])  15.4 us
    pallas_call x4, Pallas kernels, terms(): pl.pallas_call(functools.partial(own_kernel if base is None else other_ke...  11.9 us
    all_to_all x1, blocking collectives, shards(): lax.all_to_all(jnp.broadcast_to(unit[None], (NZL, PROJ, width)), 'zl', 0,...  8.19 us
    ppermute x3, starting transfers between devices, ahead(): lax.ppermute(a, ('zh', 'zl'), [(z, (z + by) % ring) for z in range(ring)])  5.89 us
    pallas_call x1, Pallas kernels, lay(): pl.pallas_call(lay_kernel, grid=(width // tile,), in_specs=[pl.BlockSpec(...  5.44 us
  transfers between devices with their start and end apart: 20, of which 10 were waited for; matrix products, arithmetic and copies ran while one was open for 2% of the time, Pallas kernels for 7%

profile of v2, /device:TPU:1, one launch (start us, length us, event | category | flops | bytes accessed | tf_op | source)
XLA Modules:
  0.0 141.6 jit_solution(9921590762124470198)
XLA Ops:
  0.6 3.3 %collective-permute-start.1 = (bf16[192,6144]{1,0:T(8,128)(2,1)}, bf16[192,6144]{1,0:T(8,128)(2,1)S(1)}, u32[]{:S(2)}, u32[]{:S(2)}) collective-permute-start(bf16[192,6144]{1,0:T(8,128)(2,1)} %x_ref.3), channel_id=1, source_target_pairs={{0,1},{1,0},{2,3},{3,2},{4,5},{5,4},{6,7},{7,6},{8,9},{9,8},{10,11... | collective-permute-start | bytes 7077896 | tf_op jit(solution)/shard_map/pair/ppermute | solution.py:224
  4.5 1.7 %copy-done = bf16[192,6144]{1,0:T(8,128)(2,1)S(1)} copy-done((bf16[192,6144]{1,0:T(8,128)(2,1)S(1)}, bf16[192,6144]{1,0:T(8,128)(2,1)}, u32[]{:S(2)}) %copy-start) | copy-done | bytes 2359320
  6.2 1.7 %copy-done.1 = bf16[192,6144]{1,0:T(8,128)(2,1)S(1)} copy-done((bf16[192,6144]{1,0:T(8,128)(2,1)S(1)}, bf16[192,6144]{1,0:T(8,128)(2,1)}, u32[]{:S(2)}) %copy-start.1) | copy-done | bytes 2359320
  8.8 2.5 %own_terms.2.base_ref = f32[256,3072]{1,0:T(8,128)S(1)} custom-call(s32[4]{0:T(128)S(1)} %pad_add_fusion.place_ref, bf16[192,512]{1,0:T(8,128)(2,1)S(1)} %copy-done.5, bf16[192,6144]{1,0:T(8,128)(2,1)S(1)} %copy-done, bf16[192,6144]{1,0:T(8,128)(2,1)S(1)} %copy-done.1), custom_call_target="tpu_custom_call" | custom-call | flops 603979776 | bytes 4718592 | tf_op jit(solution)/shard_map/pair/own_terms/pallas_call | solution.py:80
  11.3 2.5 %own_terms.3.base_ref = f32[256,3072]{1,0:T(8,128)S(1)} custom-call(s32[4]{0:T(128)S(1)} %pad_add_fusion.place_ref, bf16[192,512]{1,0:T(8,128)(2,1)S(1)} %copy-done.5, bf16[192,6144]{1,0:T(8,128)(2,1)S(1)} %copy-done, bf16[192,6144]{1,0:T(8,128)(2,1)S(1)} %copy-done.1), custom_call_target="tpu_custom_call" | custom-call | flops 603979776 | bytes 4718592 | tf_op jit(solution)/shard_map/pair/own_terms/pallas_call | solution.py:80
  13.9 3.4 %pair_terms.2 = f32[256,3072]{1,0:T(8,128)S(1)} custom-call(s32[4]{0:T(128)S(1)} %pad_add_fusion.place_ref, bf16[192,512]{1,0:T(8,128)(2,1)S(1)} %collective-permute-done.g_ref, bf16[192,6144]{1,0:T(8,128)(2,1)S(1)} %collective-permute-done.1.x_ref, bf16[192,6144]{1,0:T(8,128)(2,1)} %collective-permute-done.2.a_ref, f32[256,3072]{1,0:T(8,128)S(1)} %own_terms.2.base_ref), custom_call_target="tpu_custom_call" | custom-call | flops 603979776 | bytes 4718592 | tf_op jit(solution)/shard_map/first/pair_terms/pallas_call | solution.py:80
  17.3 3.4 %pair_terms.3 = f32[256,3072]{1,0:T(8,128)S(1)} custom-call(s32[4]{0:T(128)S(1)} %pad_add_fusion.place_ref, bf16[192,512]{1,0:T(8,128)(2,1)S(1)} %collective-permute-done.g_ref, bf16[192,6144]{1,0:T(8,128)(2,1)S(1)} %collective-permute-done.1.x_ref, bf16[192,6144]{1,0:T(8,128)(2,1)} %collective-permute-done.2.a_ref, f32[256,3072]{1,0:T(8,128)S(1)} %own_terms.3.base_ref), custom_call_target="tpu_custom_call" | custom-call | flops 603979776 | bytes 4718592 | tf_op jit(solution)/shard_map/second/pair_terms/pallas_call | solution.py:80
  21.3 2.2 %collective-permute-start.11 = (f16[64,3072]{1,0:T(8,128)(2,1)S(1)}, f16[64,3072]{1,0:T(8,128)(2,1)S(1)}, u32[]{:S(2)}, u32[]{:S(2)}) collective-permute-start(f16[64,3072]{1,0:T(8,128)(2,1)S(1)} %get-tuple-element.28), channel_id=1, source_target_pairs={{0,128},{64,192},{128,0},{192,64},{1,129},{65,193},{129,1},{193,65... | collective-permute-start | bytes 1179656 | tf_op jit(solution)/shard_map/second/ppermute | solution.py:211
  23.5 1.1 collective-permute-start.10
  25.0 1.3 collective-permute-start.3
  26.3 2.5 %collective-permute-start.5 = (f16[64,3072]{1,0:T(8,128)(2,1)S(1)}, f16[64,3072]{1,0:T(8,128)(2,1)S(1)}, u32[]{:S(2)}, u32[]{:S(2)}) collective-permute-start(f16[64,3072]{1,0:T(8,128)(2,1)S(1)} %get-tuple-element.25), channel_id=1, source_target_pairs={{0,32},{16,48},{32,0},{48,16},{1,33},{17,49},{33,1},{49,17},{2,34}... | collective-permute-start | bytes 1179656 | tf_op jit(solution)/shard_map/first/ppermute | solution.py:211
  28.8 4.9 %collective-permute-done.9 = f16[64,3072]{1,0:T(8,128)(2,1)S(1)} collective-permute-done((f16[64,3072]{1,0:T(8,128)(2,1)S(1)}, f16[64,3072]{1,0:T(8,128)(2,1)S(1)}, u32[]{:S(2)}, u32[]{:S(2)}) %collective-permute-start.9) | collective-permute-done | bytes 393248 | tf_op jit(solution)/shard_map/second/ppermute | solution.py:211
  34.0 7.1 %collective-permute-done.11 = f16[64,3072]{1,0:T(8,128)(2,1)S(1)} collective-permute-done((f16[64,3072]{1,0:T(8,128)(2,1)S(1)}, f16[64,3072]{1,0:T(8,128)(2,1)S(1)}, u32[]{:S(2)}, u32[]{:S(2)}) %collective-permute-start.11) | collective-permute-done | bytes 393248 | tf_op jit(solution)/shard_map/second/ppermute | solution.py:211
  42.7 2.5 %collective-permute-start.14 = (f16[16,3072]{1,0:T(8,128)(2,1)S(1)}, f16[16,3072]{1,0:T(8,128)(2,1)S(1)}, u32[]{:S(2)}, u32[]{:S(2)}) collective-permute-start(f16[16,3072]{1,0:T(8,128)(2,1)S(1)} %get-tuple-element.37), channel_id=1, source_target_pairs={{0,32},{16,48},{32,0},{48,16},{1,33},{17,49},{33,1},{49,17},{2,34}... | collective-permute-start | bytes 294920 | tf_op jit(solution)/shard_map/second/ppermute | solution.py:211
  45.2 1.1 collective-permute-start.13
  47.6 2.8 %collective-permute-start.8 = (f16[16,3072]{1,0:T(8,128)(2,1)S(1)}, f16[16,3072]{1,0:T(8,128)(2,1)S(1)}, u32[]{:S(2)}, u32[]{:S(2)}) collective-permute-start(f16[16,3072]{1,0:T(8,128)(2,1)S(1)} %get-tuple-element.34), channel_id=1, source_target_pairs={{0,128},{64,192},{128,0},{192,64},{1,129},{65,193},{129,1},{193,65... | collective-permute-start | bytes 294920 | tf_op jit(solution)/shard_map/first/ppermute | solution.py:211
  50.4 1.1 collective-permute-start.7
  51.6 1.8 %collective-permute-done.8 = f16[16,3072]{1,0:T(8,128)(2,1)S(1)} collective-permute-done((f16[16,3072]{1,0:T(8,128)(2,1)S(1)}, f16[16,3072]{1,0:T(8,128)(2,1)S(1)}, u32[]{:S(2)}, u32[]{:S(2)}) %collective-permute-start.8) | collective-permute-done | bytes 98336 | tf_op jit(solution)/shard_map/first/ppermute | solution.py:211
  54.2 1.8 %collective-permute-start.15 = (f32[4,6144]{1,0:T(4,128)S(1)}, f32[4,6144]{1,0:T(4,128)S(1)}, u32[]{:S(2)}, u32[]{:S(2)}) collective-permute-start(f32[4,6144]{1,0:T(4,128)S(1)} %get-tuple-element.30), channel_id=1, source_target_pairs={{0,2},{2,4},{4,6},{6,8},{8,10},{10,12},{12,14},{14,0},{1,3},{3,5},... | collective-permute-start | bytes 294920 | tf_op jit(solution)/shard_map/depth_sum/ppermute | solution.py:215
  56.0 3.0 %collective-permute-start.17 = (f32[4,6144]{1,0:T(4,128)S(1)}, f32[4,6144]{1,0:T(4,128)S(1)}, u32[]{:S(2)}, u32[]{:S(2)}) collective-permute-start(f32[4,6144]{1,0:T(4,128)S(1)} %get-tuple-element.31), channel_id=1, source_target_pairs={{0,4},{2,6},{4,8},{6,10},{8,12},{10,14},{12,0},{14,2},{1,5},{3,7},... | collective-permute-start | bytes 294920 | tf_op jit(solution)/shard_map/depth_sum/ppermute | solution.py:215
  59.0 1.1 collective-permute-start.16
  60.1 1.8 %collective-permute-done.15 = f32[4,6144]{1,0:T(4,128)S(1)} collective-permute-done((f32[4,6144]{1,0:T(4,128)S(1)}, f32[4,6144]{1,0:T(4,128)S(1)}, u32[]{:S(2)}, u32[]{:S(2)}) %collective-permute-start.15) | collective-permute-done | bytes 98336 | tf_op jit(solution)/shard_map/depth_sum/ppermute | solution.py:215
  61.9 2.9 %collective-permute-done.17 = f32[4,6144]{1,0:T(4,128)S(1)} collective-permute-done((f32[4,6144]{1,0:T(4,128)S(1)}, f32[4,6144]{1,0:T(4,128)S(1)}, u32[]{:S(2)}, u32[]{:S(2)}) %collective-permute-start.17) | collective-permute-done | bytes 98336 | tf_op jit(solution)/shard_map/depth_sum/ppermute | solution.py:215
  65.5 3.8 %collective-permute-start.18 = (f32[4,6144]{1,0:T(4,128)}, f32[4,6144]{1,0:T(4,128)}, u32[]{:S(2)}, u32[]{:S(2)}) collective-permute-start(f32[4,6144]{1,0:T(4,128)} %fusion.17), channel_id=1, source_target_pairs={{0,8},{8,0},{1,9},{9,1},{2,10},{10,2},{3,11},{11,3},{4,12},{12,4},... | collective-permute-start | bytes 294920 | tf_op jit(solution)/shard_map/depth_sum/ppermute | solution.py:243
  69.7 1.7 %multiply_reduce_fusion.1 = (f32[24576]{0:T(1024)S(1)}, f32[24576]{0:T(1024)S(1)}) fusion(f32[16,24576]{1,0:T(8,128)S(1)} %copy-done.3, s32[]{:T(128)S(6)} %select_n.2, f32[16,24576]{1,0:T(8,128)} %moment_ref.1), kind=kLoop, calls=%fused_computation.33 | loop fusion | flops 49152 | bytes 393220 | tf_op jit(solution)/shard_map/own_row/mul | solution.py:28
  71.5 2.9 %collective-permute-done.18 = f32[4,6144]{1,0:T(4,128)} collective-permute-done((f32[4,6144]{1,0:T(4,128)}, f32[4,6144]{1,0:T(4,128)}, u32[]{:S(2)}, u32[]{:S(2)}) %collective-permute-start.18) | collective-permute-done | bytes 98336 | tf_op jit(solution)/shard_map/depth_sum/ppermute | solution.py:243
  74.4 1.9 %multiply_reduce_fusion = (f32[4]{0:T(128)S(1)}, f32[4,6144]{1,0:T(4,128)S(1)}, f16[4,6144]{1,0:T(4,128)(2,1)}, f16[4,6144]{1,0:T(4,128)(2,1)}) fusion(f32[4,6144]{1,0:T(4,128)S(1)} %reshape.93, f32[4,6144]{1,0:T(4,128)S(1)} %mul.87, f32[4,6144]{1,0:T(4,128)S(1)} %mul.74, f32[4,6144]{1,0:T(4,128)} %fusion.17, f32[4,6144]{1,0:T(4,128)} %collective-permute-done.18), kind=kLoop, calls=%fused_computation.32 | loop fusion | flops 417788 | bytes 688144 | tf_op jit(solution)/shard_map/own_row/reduce_sum | solution.py:251
  76.5 8.2 %all_to_all.5 = f16[4,4,6144]{2,1,0:T(4,128)(2,1)S(1)} all-to-all(f16[4,4,6144]{2,1,0:T(4,128)(2,1)S(1)} %broadcast_in_dim.2), channel_id=1, replica_groups=mesh['y'=4,'x'=4,'zh'=2,'zl'=4,'c'=2] {'zl'}, dimensions={0} | all-to-all | bytes 393216 | tf_op jit(solution)/shard_map/depth_gather/all_to_all | solution.py:258
  85.7 27.9 %all-gather.1 = f16[384,6144]{1,0:T(8,128)(2,1)S(1)} all-gather(f16[24,6144]{1,0:T(8,128)(2,1)S(1)} %pad_maximum_fusion), channel_id=1, replica_groups=mesh['y'=4,'x'=4,'zh'=2,'zl'=4,'c'=2] {'y','x'}, dimensions={0}, use_global_device_ids=true | all-gather | bytes 5013504 | tf_op jit(solution)/shard_map/plane_gather/all_gather | solution.py:263
  114.5 16.2 %collective-permute-start.19 = (bf16[256,6144]{1,0:T(8,128)(2,1)S(1)}, bf16[256,6144]{1,0:T(8,128)(2,1)S(1)}, u32[]{:S(2)}, u32[]{:S(2)}) collective-permute-start(bf16[256,6144]{1,0:T(8,128)(2,1)S(1)} %bitcast.8), channel_id=1, source_target_pairs={{0,1},{1,0},{2,3},{3,2},{4,5},{5,4},{6,7},{7,6},{8,9},{9,8},{10,11... | collective-permute-start | bytes 9437192 | tf_op jit(solution)/shard_map/ppermute | solution.py:267
  130.9 4.3 %step.1 = (f32[16,24576]{1,0:T(8,128)}, f32[16,24576]{1,0:T(8,128)}, f32[16,24576]{1,0:T(8,128)}) custom-call(bf16[128,6144]{1,0:T(8,128)(2,1)S(1)} %slice_bitcast_fusion.u_ref, f32[16,24576]{1,0:T(8,128)S(1)} %copy-done.2, f32[16,24576]{1,0:T(8,128)S(1)} %copy-done.4, f32[16,24576]{1,0:T(8,128)S(1)} %copy-done.3), custom_call_target="tpu_custom_call" | custom-call | flops 100663296 | bytes 9437184 | tf_op jit(solution)/shard_map/step/pallas_call | solution.py:130
  136.0 5.4 %lay.1 = bf16[128,24576]{1,0:T(8,128)(2,1)} custom-call(s32[4]{0:T(128)S(1)} %pad_add_fusion.place_ref, bf16[256,6144]{1,0:T(8,128)(2,1)S(1)} %bitcast.9, bf16[256,6144]{1,0:T(8,128)(2,1)S(1)} %collective-permute-done.19.other_ref), custom_call_target="tpu_custom_call" | custom-call | flops 1610612736 | bytes 12582912 | tf_op jit(solution)/shard_map/lay/pallas_call | solution.py:186
  (58 shorter events, 10.6 us)
Async XLA Ops:
  0.6 13.2 %collective-permute-start.1 = (bf16[192,6144]{1,0:T(8,128)(2,1)}, bf16[192,6144]{1,0:T(8,128)(2,1)S(1)}, u32[]{:S(2)}, u32[]{:S(2)}) collective-permute-start(bf16[192,6144]{1,0:T(8,128)(2,1)} %x_ref.3), channel_id=1, source_target_pairs={{0,1},{1,0},{2,3},{3,2},{4,5},{5,4},{6,7},{7,6},{8,9},{9,8},{10,11... | collective-permute-start | bytes 7077896 | tf_op jit(solution)/shard_map/pair/ppermute | solution.py:224
  4.0 9.9 %collective-permute-start.2 = (bf16[192,6144]{1,0:T(8,128)(2,1)}, bf16[192,6144]{1,0:T(8,128)(2,1)}, u32[]{:S(2)}, u32[]{:S(2)}) collective-permute-start(bf16[192,6144]{1,0:T(8,128)(2,1)} %a_ref.3), channel_id=1, source_target_pairs={{0,1},{1,0},{2,3},{3,2},{4,5},{5,4},{6,7},{7,6},{8,9},{9,8},{10,11... | collective-permute-start | bytes 7077896 | tf_op jit(solution)/shard_map/pair/ppermute | solution.py:225
  4.1 9.8 %collective-permute-start = (bf16[192,512]{1,0:T(8,128)(2,1)}, bf16[192,512]{1,0:T(8,128)(2,1)S(1)}, u32[]{:S(2)}, u32[]{:S(2)}) collective-permute-start(bf16[192,512]{1,0:T(8,128)(2,1)} %g_ref.3), channel_id=1, source_target_pairs={{0,1},{1,0},{2,3},{3,2},{4,5},{5,4},{6,7},{7,6},{8,9},{9,8},{10,11... | collective-permute-start | bytes 589832 | tf_op jit(solution)/shard_map/pair/ppermute | solution.py:223
  4.5 1.7 %copy-start = (bf16[192,6144]{1,0:T(8,128)(2,1)S(1)}, bf16[192,6144]{1,0:T(8,128)(2,1)}, u32[]{:S(2)}) copy-start(bf16[192,6144]{1,0:T(8,128)(2,1)} %x_ref.3) | copy-start | bytes 7077892
  6.2 1.7 %copy-start.1 = (bf16[192,6144]{1,0:T(8,128)(2,1)S(1)}, bf16[192,6144]{1,0:T(8,128)(2,1)}, u32[]{:S(2)}) copy-start(bf16[192,6144]{1,0:T(8,128)(2,1)} %a_ref.3) | copy-start | bytes 7077892
  7.9 0.9 copy-start.5
  21.2 12.4 %collective-permute-start.9 = (f16[64,3072]{1,0:T(8,128)(2,1)S(1)}, f16[64,3072]{1,0:T(8,128)(2,1)S(1)}, u32[]{:S(2)}, u32[]{:S(2)}) collective-permute-start(f16[64,3072]{1,0:T(8,128)(2,1)S(1)} %get-tuple-element.27), channel_id=1, source_target_pairs={{0,64},{64,128},{128,192},{192,0},{1,65},{65,129},{129,193},{193,1... | collective-permute-start | bytes 1179656 | tf_op jit(solution)/shard_map/second/ppermute | solution.py:211
  21.3 19.9 %collective-permute-start.11 = (f16[64,3072]{1,0:T(8,128)(2,1)S(1)}, f16[64,3072]{1,0:T(8,128)(2,1)S(1)}, u32[]{:S(2)}, u32[]{:S(2)}) collective-permute-start(f16[64,3072]{1,0:T(8,128)(2,1)S(1)} %get-tuple-element.28), channel_id=1, source_target_pairs={{0,128},{64,192},{128,0},{192,64},{1,129},{65,193},{129,1},{193,65... | collective-permute-start | bytes 1179656 | tf_op jit(solution)/shard_map/second/ppermute | solution.py:211
  23.5 18.4 %collective-permute-start.10 = (f16[64,3072]{1,0:T(8,128)(2,1)S(1)}, f16[64,3072]{1,0:T(8,128)(2,1)S(1)}, u32[]{:S(2)}, u32[]{:S(2)}) collective-permute-start(f16[64,3072]{1,0:T(8,128)(2,1)S(1)} %get-tuple-element.29), channel_id=1, source_target_pairs={{0,192},{64,0},{128,64},{192,128},{1,193},{65,1},{129,65},{193,129... | collective-permute-start | bytes 1179656 | tf_op jit(solution)/shard_map/second/ppermute | solution.py:211
  25.0 20.2 %collective-permute-start.3 = (f16[64,3072]{1,0:T(8,128)(2,1)S(1)}, f16[64,3072]{1,0:T(8,128)(2,1)S(1)}, u32[]{:S(2)}, u32[]{:S(2)}) collective-permute-start(f16[64,3072]{1,0:T(8,128)(2,1)S(1)} %get-tuple-element.24), channel_id=1, source_target_pairs={{0,16},{16,32},{32,48},{48,0},{1,17},{17,33},{33,49},{49,1},{2,18}... | collective-permute-start | bytes 1179656 | tf_op jit(solution)/shard_map/first/ppermute | solution.py:211
  26.3 20.0 %collective-permute-start.5 = (f16[64,3072]{1,0:T(8,128)(2,1)S(1)}, f16[64,3072]{1,0:T(8,128)(2,1)S(1)}, u32[]{:S(2)}, u32[]{:S(2)}) collective-permute-start(f16[64,3072]{1,0:T(8,128)(2,1)S(1)} %get-tuple-element.25), channel_id=1, source_target_pairs={{0,32},{16,48},{32,0},{48,16},{1,33},{17,49},{33,1},{49,17},{2,34}... | collective-permute-start | bytes 1179656 | tf_op jit(solution)/shard_map/first/ppermute | solution.py:211
  33.7 12.7 %collective-permute-start.4 = (f16[64,3072]{1,0:T(8,128)(2,1)S(1)}, f16[64,3072]{1,0:T(8,128)(2,1)S(1)}, u32[]{:S(2)}, u32[]{:S(2)}) collective-permute-start(f16[64,3072]{1,0:T(8,128)(2,1)S(1)} %get-tuple-element.26), channel_id=1, source_target_pairs={{0,48},{16,0},{32,16},{48,32},{1,49},{17,1},{33,17},{49,33},{2,50}... | collective-permute-start | bytes 1179656 | tf_op jit(solution)/shard_map/first/ppermute | solution.py:211
  42.2 8.1 %collective-permute-start.12 = (f16[16,3072]{1,0:T(8,128)(2,1)S(1)}, f16[16,3072]{1,0:T(8,128)(2,1)S(1)}, u32[]{:S(2)}, u32[]{:S(2)}) collective-permute-start(f16[16,3072]{1,0:T(8,128)(2,1)S(1)} %get-tuple-element.36), channel_id=1, source_target_pairs={{0,16},{16,32},{32,48},{48,0},{1,17},{17,33},{33,49},{49,1},{2,18}... | collective-permute-start | bytes 294920 | tf_op jit(solution)/shard_map/second/ppermute | solution.py:211
  42.7 8.7 %collective-permute-start.14 = (f16[16,3072]{1,0:T(8,128)(2,1)S(1)}, f16[16,3072]{1,0:T(8,128)(2,1)S(1)}, u32[]{:S(2)}, u32[]{:S(2)}) collective-permute-start(f16[16,3072]{1,0:T(8,128)(2,1)S(1)} %get-tuple-element.37), channel_id=1, source_target_pairs={{0,32},{16,48},{32,0},{48,16},{1,33},{17,49},{33,1},{49,17},{2,34}... | collective-permute-start | bytes 294920 | tf_op jit(solution)/shard_map/second/ppermute | solution.py:211
  45.2 6.2 %collective-permute-start.13 = (f16[16,3072]{1,0:T(8,128)(2,1)S(1)}, f16[16,3072]{1,0:T(8,128)(2,1)S(1)}, u32[]{:S(2)}, u32[]{:S(2)}) collective-permute-start(f16[16,3072]{1,0:T(8,128)(2,1)S(1)} %get-tuple-element.38), channel_id=1, source_target_pairs={{0,48},{16,0},{32,16},{48,32},{1,49},{17,1},{33,17},{49,33},{2,50}... | collective-permute-start | bytes 294920 | tf_op jit(solution)/shard_map/second/ppermute | solution.py:211
  46.5 22.8 %copy-start.2 = (f32[16,24576]{1,0:T(8,128)S(1)}, f32[16,24576]{1,0:T(8,128)}, u32[]{:S(2)}) copy-start(f32[16,24576]{1,0:T(8,128)} %master_ref.1) | copy-start | bytes 4718596
  46.6 23.1 %copy-start.3 = (f32[16,24576]{1,0:T(8,128)S(1)}, f32[16,24576]{1,0:T(8,128)}, u32[]{:S(2)}) copy-start(f32[16,24576]{1,0:T(8,128)} %second_ref.1) | copy-start | bytes 4718596
  46.7 4.9 %collective-permute-start.6 = (f16[16,3072]{1,0:T(8,128)(2,1)S(1)}, f16[16,3072]{1,0:T(8,128)(2,1)S(1)}, u32[]{:S(2)}, u32[]{:S(2)}) collective-permute-start(f16[16,3072]{1,0:T(8,128)(2,1)S(1)} %get-tuple-element.33), channel_id=1, source_target_pairs={{0,64},{64,128},{128,192},{192,0},{1,65},{65,129},{129,193},{193,1... | collective-permute-start | bytes 294920 | tf_op jit(solution)/shard_map/first/ppermute | solution.py:211
  47.6 5.9 %collective-permute-start.8 = (f16[16,3072]{1,0:T(8,128)(2,1)S(1)}, f16[16,3072]{1,0:T(8,128)(2,1)S(1)}, u32[]{:S(2)}, u32[]{:S(2)}) collective-permute-start(f16[16,3072]{1,0:T(8,128)(2,1)S(1)} %get-tuple-element.34), channel_id=1, source_target_pairs={{0,128},{64,192},{128,0},{192,64},{1,129},{65,193},{129,1},{193,65... | collective-permute-start | bytes 294920 | tf_op jit(solution)/shard_map/first/ppermute | solution.py:211
  50.4 3.7 %collective-permute-start.7 = (f16[16,3072]{1,0:T(8,128)(2,1)S(1)}, f16[16,3072]{1,0:T(8,128)(2,1)S(1)}, u32[]{:S(2)}, u32[]{:S(2)}) collective-permute-start(f16[16,3072]{1,0:T(8,128)(2,1)S(1)} %get-tuple-element.35), channel_id=1, source_target_pairs={{0,192},{64,0},{128,64},{192,128},{1,193},{65,1},{129,65},{193,129... | collective-permute-start | bytes 294920 | tf_op jit(solution)/shard_map/first/ppermute | solution.py:211
  54.2 7.7 %collective-permute-start.15 = (f32[4,6144]{1,0:T(4,128)S(1)}, f32[4,6144]{1,0:T(4,128)S(1)}, u32[]{:S(2)}, u32[]{:S(2)}) collective-permute-start(f32[4,6144]{1,0:T(4,128)S(1)} %get-tuple-element.30), channel_id=1, source_target_pairs={{0,2},{2,4},{4,6},{6,8},{8,10},{10,12},{12,14},{14,0},{1,3},{3,5},... | collective-permute-start | bytes 294920 | tf_op jit(solution)/shard_map/depth_sum/ppermute | solution.py:215
  56.0 8.8 %collective-permute-start.17 = (f32[4,6144]{1,0:T(4,128)S(1)}, f32[4,6144]{1,0:T(4,128)S(1)}, u32[]{:S(2)}, u32[]{:S(2)}) collective-permute-start(f32[4,6144]{1,0:T(4,128)S(1)} %get-tuple-element.31), channel_id=1, source_target_pairs={{0,4},{2,6},{4,8},{6,10},{8,12},{10,14},{12,0},{14,2},{1,5},{3,7},... | collective-permute-start | bytes 294920 | tf_op jit(solution)/shard_map/depth_sum/ppermute | solution.py:215
  59.0 5.9 %collective-permute-start.16 = (f32[4,6144]{1,0:T(4,128)S(1)}, f32[4,6144]{1,0:T(4,128)S(1)}, u32[]{:S(2)}, u32[]{:S(2)}) collective-permute-start(f32[4,6144]{1,0:T(4,128)S(1)} %get-tuple-element.32), channel_id=1, source_target_pairs={{0,14},{2,0},{4,2},{6,4},{8,6},{10,8},{12,10},{14,12},{1,15},{3,1}... | collective-permute-start | bytes 294920 | tf_op jit(solution)/shard_map/depth_sum/ppermute | solution.py:215
  65.5 8.9 %collective-permute-start.18 = (f32[4,6144]{1,0:T(4,128)}, f32[4,6144]{1,0:T(4,128)}, u32[]{:S(2)}, u32[]{:S(2)}) collective-permute-start(f32[4,6144]{1,0:T(4,128)} %fusion.17), channel_id=1, source_target_pairs={{0,8},{8,0},{1,9},{9,1},{2,10},{10,2},{3,11},{11,3},{4,12},{12,4},... | collective-permute-start | bytes 294920 | tf_op jit(solution)/shard_map/depth_sum/ppermute | solution.py:243
  114.5 16.4 %copy-start.4 = (f32[16,24576]{1,0:T(8,128)S(1)}, f32[16,24576]{1,0:T(8,128)}, u32[]{:S(2)}) copy-start(f32[16,24576]{1,0:T(8,128)} %moment_ref.1) | copy-start | bytes 4718596
  114.5 21.5 %collective-permute-start.19 = (bf16[256,6144]{1,0:T(8,128)(2,1)S(1)}, bf16[256,6144]{1,0:T(8,128)(2,1)S(1)}, u32[]{:S(2)}, u32[]{:S(2)}) collective-permute-start(bf16[256,6144]{1,0:T(8,128)(2,1)S(1)} %bitcast.8), channel_id=1, source_target_pairs={{0,1},{1,0},{2,3},{3,2},{4,5},{5,4},{6,7},{7,6},{8,9},{9,8},{10,11... | collective-permute-start | bytes 9437192 | tf_op jit(solution)/shard_map/ppermute | solution.py:267

commit v3 on v2

v3 whole, which is shorter than its diff:
```python
import functools

import jax
import jax.numpy as jnp
from jax import lax
from jax.experimental import pallas as pl
from jax.experimental.pallas import tpu as pltpu
from jax.sharding import Mesh
from jax.sharding import PartitionSpec as P

beta_one = 0.9
beta_two = 0.95
learn_rate = 0.002
bias_one = 1.0 - 0.9**10
bias_two = 1.0 - 0.95**10

REP = ("y", "x", "zh")
SHARD = ("zl", "c")
NY, NX, NZH, NZL, NC = 4, 4, 2, 4, 2
PLANE = NY * NX
PROJ = 4
SEND_SCALE = 128.0
UNIT_SCALE = 32768.0


def adam_update(gradient, master, moment, second):
    new_moment = beta_one * moment + (1.0 - beta_one) * gradient
    new_second = beta_two * second + (1.0 - beta_two) * gradient * gradient
    stepped = master - learn_rate * (new_moment / bias_one) / (
        jnp.sqrt(new_second / bias_two) + 1e-08
    )
    return (stepped, new_moment, new_second)


def lefts_kernel(place_ref, g_ref, own_ref, send_ref):
    shape = (own_ref.shape[0], g_ref.shape[1])
    m = lax.broadcasted_iota(jnp.int32, shape, 0)
    j = lax.broadcasted_iota(jnp.int32, shape, 1)
    core, depth, x, y = (place_ref[n] for n in range(4))
    first, second = m >> 7, (m >> 5) & 3
    start = 128 * ((depth + (m >> 3)) & 3) + 64 * ((m >> 2) & 1) + (m & 3)
    for out_ref, order in ((own_ref, core), (send_ref, 1 - core)):
        turn = order * (second - first)
        i = 4 * ((y + second - turn) & 3) + ((x + first + turn) & 3)
        chosen = jnp.where(j == start + 4 * i, 1.0, 0.0).astype(jnp.bfloat16)
        out_ref[...] = lax.dot_general(
            chosen, g_ref[...], (((1,), (1,)), ((), ())), preferred_element_type=jnp.float32
        ).astype(jnp.bfloat16)


def lefts(place, g):
    shape = jax.ShapeDtypeStruct((g.shape[1], g.shape[0]), g.dtype)
    return pl.pallas_call(
        lefts_kernel,
        in_specs=[pl.BlockSpec(memory_space=pltpu.SMEM), pl.BlockSpec(memory_space=pltpu.VMEM)],
        out_specs=[pl.BlockSpec(memory_space=pltpu.VMEM)] * 2,
        out_shape=[shape] * 2,
        compiler_params=pltpu.CompilerParams(vmem_limit_bytes=16 * 2**20),
        cost_estimate=pl.CostEstimate(flops=4 * g.size * g.shape[1], bytes_accessed=6 * g.size, transcendentals=0),
        name="lefts",
    )(place, g)


def mask_rows(left_ref, rows, masked_ref):
    left = left_ref[rows]
    k = lax.broadcasted_iota(jnp.int32, left.shape, 0) & 3
    masked_ref[0] = jnp.where(k < 3, left.astype(jnp.float32), 0.0).astype(left.dtype)
    masked_ref[1] = jnp.where(k == 3, left.astype(jnp.float32), 0.0).astype(left.dtype)


def two_dots(left_ref, x_ref, a_ref):
    total = jnp.dot(left_ref[0], x_ref[...], preferred_element_type=jnp.float32)
    return total + jnp.dot(left_ref[1], a_ref[...], preferred_element_type=jnp.float32)


def terms_kernel(rows, sides, *refs):
    inputs, (base_refs, out_ref, masked) = refs[: 3 * sides], (refs[3 * sides : -1 - sides], refs[-1 - sides], refs[-sides:])
    groups = [inputs[3 * n : 3 * n + 3] for n in range(sides)]

    @pl.when(pl.program_id(0) == 0)
    def _():
        for (left_ref, _, _), masked_ref in zip(groups, masked):
            mask_rows(left_ref, rows, masked_ref)

    total = base_refs[0][...] if base_refs else 0.0
    for (_, x_ref, a_ref), masked_ref in zip(groups, masked):
        total += two_dots(masked_ref, x_ref, a_ref)
    out_ref[...] = total


def terms(rows, *sides, base=None, tile=512):
    tokens, width = sides[0][1].shape
    count = rows.stop - rows.start
    left = pl.BlockSpec(sides[0][0].shape, lambda j: (0, 0))
    block = pl.BlockSpec((tokens, tile), lambda j: (0, j))
    result = pl.BlockSpec((count, tile), lambda j: (0, j))
    bases = [] if base is None else [base]
    return pl.pallas_call(
        functools.partial(terms_kernel, rows, len(sides)),
        grid=(width // tile,),
        in_specs=[left, block, block] * len(sides) + [result] * len(bases),
        out_specs=result,
        out_shape=jax.ShapeDtypeStruct((count, width), jnp.float32),
        scratch_shapes=[pltpu.VMEM((2, count, tokens), jnp.bfloat16)] * len(sides),
        compiler_params=pltpu.CompilerParams(vmem_limit_bytes=24 * 2**20),
        cost_estimate=pl.CostEstimate(
            flops=4 * len(sides) * count * tokens * width,
            bytes_accessed=8 * tokens * width,
            transcendentals=0,
        ),
        name="terms",
    )(*(a for side in sides for a in side), *bases)


def step_kernel(g_ref, master_ref, moment_ref, second_ref, nm_ref, mo_ref, se_ref, grad_ref):
    k = pl.program_id(0)
    rows, width = master_ref.shape

    @pl.when(k == 0)
    def _():
        shape = (PROJ * rows, g_ref.shape[0])
        m = lax.broadcasted_iota(jnp.int32, shape, 0)
        j = lax.broadcasted_iota(jnp.int32, shape, 1)
        coarse = g_ref[...].astype(jnp.bfloat16)
        fine = (g_ref[...] - coarse.astype(jnp.float32)).astype(jnp.bfloat16)
        for at in range(2):
            wanted = j == 2 * PROJ * (m & 15) + PROJ * at + (m >> 4)
            pick = jnp.where(wanted, 1.0, 0.0).astype(jnp.bfloat16)
            total = jnp.dot(pick, coarse, preferred_element_type=jnp.float32)
            total += jnp.dot(pick, fine, preferred_element_type=jnp.float32)
            grad_ref[:, at * width // 2 : (at + 1) * width // 2] = total

    gradient = grad_ref[pl.ds(pl.multiple_of(k * rows, rows), rows), :]
    stepped, new_moment, new_second = adam_update(
        gradient, master_ref[...], moment_ref[...], second_ref[...]
    )
    mo_ref[...] = new_moment
    se_ref[...] = new_second
    scale = jnp.sqrt(jnp.sum(stepped * stepped, axis=1, keepdims=True) + 1e-06)
    nm_ref[...] = stepped / scale


def step(u, master, moment, second):
    rows, width = master.shape
    width //= PROJ
    block = pl.BlockSpec((rows, width), lambda k: (0, k))
    return pl.pallas_call(
        step_kernel,
        grid=(PROJ,),
        in_specs=[pl.BlockSpec(u.shape, lambda k: (0, 0)), block, block, block],
        out_specs=[block, block, block],
        out_shape=[jax.ShapeDtypeStruct(master.shape, jnp.float32)] * 3,
        scratch_shapes=[pltpu.VMEM((PROJ * rows, width), jnp.float32)],
        compiler_params=pltpu.CompilerParams(vmem_limit_bytes=40 * 2**20),
        cost_estimate=pl.CostEstimate(
            flops=2 * 64 * 128 * width, bytes_accessed=24 * rows * width * PROJ, transcendentals=0
        ),
        name="step",
    )(u, master, moment, second)


def lay_kernel(place_ref, own_ref, other_ref, out_ref, held_ref, sems):
    j = pl.program_id(0)
    last = pl.num_programs(0) - 1
    parts, tile = own_ref.shape
    width = tile * (last + 1)
    slot = lax.rem(j, 2)

    def copies(step, slot):
        for k in range(PROJ):
            at = pl.ds(pl.multiple_of(k * width + step * tile, 128), tile)
            yield pltpu.make_async_copy(held_ref.at[slot, k], out_ref.at[:, at], sems.at[slot, k])

    @pl.when(j >= 2)
    def _():
        for copy in copies(j - 2, slot):
            copy.wait()

    m = lax.broadcasted_iota(jnp.int32, (256, parts), 0)
    n = lax.broadcasted_iota(jnp.int32, (256, parts), 1)
    wanted = n == (m & 15) * 16 + ((m >> 4) & 3) * 4 + (m >> 6)
    pick = jnp.where(wanted, 1.0 / UNIT_SCALE, 0.0).astype(jnp.bfloat16)
    for ref, core in ((own_ref, place_ref[0]), (other_ref, 1 - place_ref[0])):
        rows = jnp.dot(pick, ref[...], preferred_element_type=jnp.float32).astype(out_ref.dtype)
        for k in range(PROJ):
            for zl in range(NZL):
                to = pl.ds(pl.multiple_of(32 * zl + 16 * core, 16), 16)
                held_ref[slot, k, to] = rows[64 * k + 16 * zl : 64 * k + 16 * zl + 16]
    for copy in copies(j, slot):
        copy.start()

    @pl.when(j == last)
    def _():
        for copy in copies(j - 1, 1 - slot):
            copy.wait()
        for copy in copies(j, slot):
            copy.wait()


def lay(place, own, other, rows, tile=1536):
    parts, half = own.shape[0] // 2, own.shape[1]
    width = 2 * half
    block = pl.BlockSpec((parts, tile), lambda j: (j // (half // tile), j % (half // tile)))
    return pl.pallas_call(
        lay_kernel,
        grid=(width // tile,),
        in_specs=[pl.BlockSpec(memory_space=pltpu.SMEM), block, block],
        out_specs=pl.BlockSpec(memory_space=pl.ANY),
        out_shape=jax.ShapeDtypeStruct((rows, PROJ * width), jnp.bfloat16),
        scratch_shapes=[
            pltpu.VMEM((2, PROJ, rows, tile), jnp.bfloat16),
            pltpu.SemaphoreType.DMA((2, PROJ)),
        ],
        compiler_params=pltpu.CompilerParams(vmem_limit_bytes=24 * 2**20),
        cost_estimate=pl.CostEstimate(
            flops=4 * 256 * parts * width, bytes_accessed=8 * parts * width, transcendentals=0
        ),
        name="lay",
    )(place, own, other)


def shards(x_in, attn_out, grads_out, master, moment, second):
    width = x_in.shape[1]
    swap = [(0, 1), (1, 0)]
    core = lax.axis_index("c")
    place = jnp.stack([lax.axis_index(name) for name in ("c", "zl", "x", "y")]).astype(jnp.int32)
    half = width // 2

    def ahead(a, by):
        ring = NZH * NZL
        return lax.ppermute(a, ("zh", "zl"), [(z, (z + by) % ring) for z in range(ring)])

    def onward(a, by, turned):
        pairs = []
        for n in range(PLANE * NC):
            y, x, core = n // (NX * NC), n // NC % NX, n % NC
            to_y, to_x = ((y + by) % NY, x) if core != turned else (y, (x + by) % NX)
            pairs.append((n, (to_y * NX + to_x) * NC + core))
        return lax.ppermute(a, ("y", "x", "c"), pairs)

    def shared(kept, rows, turned):
        blocks = rows.astype(jnp.float16).reshape(3, -1, half)
        came = [onward(blocks[n - 1], n, turned).astype(jnp.float32) for n in (1, 3, 2)]
        return kept + came[0] + came[1] + came[2]

    def columns(a, which):
        return lax.dynamic_slice_in_dim(a, which * half, half, axis=1)

    with jax.named_scope("pair"):
        left, left_send = lefts(place, grads_out)
        left_other = lax.ppermute(left_send, "c", swap)
        x_other = lax.ppermute(columns(x_in, 1 - core), "c", swap)
        a_other = lax.ppermute(columns(attn_out, 1 - core), "c", swap)
        own = (left, columns(x_in, core), columns(attn_out, core))
        other = (left_other, x_other, a_other)
        block = grads_out.shape[1] // 4
        going, staying = slice(block, 4 * block), slice(0, block)
        sent = terms(going, other, base=terms(going, own))
    with jax.named_scope("plane_sum"):
        part = shared(terms(staying, own, other) * SEND_SCALE, sent * SEND_SCALE, 0)
        part = part * 0.25
        part = shared(part[: block // 4], part[block // 4 :], 1)
    with jax.named_scope("depth_sum"):
        part = (part * (4.0 / SEND_SCALE)).reshape(NZL, NC * PROJ, half)
        part = part[0] + ahead(part[1], 1) + ahead(part[3], 7) + ahead(part[2], 2)
        part = part + lax.ppermute(part, "zh", swap)
        came = lax.ppermute(part, "c", swap)
        gradient = jnp.where(
            core == 0,
            jnp.concatenate([part[:PROJ], came[:PROJ]], axis=1),
            jnp.concatenate([came[PROJ:], part[PROJ:]], axis=1),
        )
    with jax.named_scope("own_row"):
        row = lax.axis_index("y") * NX + lax.axis_index("x")

        def piece(a):
            return lax.dynamic_slice(a, (row, 0), (1, PROJ * width)).reshape(PROJ, width)

        stepped, _, _ = adam_update(gradient, piece(master), piece(moment), piece(second))
        scale = jnp.sqrt(jnp.sum(stepped * stepped, axis=1, keepdims=True) + 1e-06)
        unit = lax.reduce_precision(stepped / scale, 8, 7)
        unit = (unit * UNIT_SCALE).astype(jnp.float16)
    with jax.named_scope("depth_gather"):
        units = lax.all_to_all(
            jnp.broadcast_to(unit[None], (NZL, PROJ, width)), "zl", 0, 0, tiled=True
        )
    with jax.named_scope("plane_gather"):
        units = units.reshape(NZL * PROJ, width)
        small = gradient.astype(jnp.float16)
        halves = [a[:, n * half : (n + 1) * half] for a in (units, small) for n in range(2)]
        came = lax.all_gather(jnp.concatenate(halves, axis=0), ("y", "x"), axis=0, tiled=True)
        came = came.reshape(PLANE, 2 * (NZL + 1) * PROJ, half)
        grads = came[:, 2 * NZL * PROJ :].astype(jnp.float32).reshape(2 * PLANE * PROJ, half)
        own = came[:, : 2 * NZL * PROJ].astype(jnp.bfloat16)
        own = jnp.swapaxes(own.reshape(PLANE, 2, NZL * PROJ, half), 0, 1)
        own = own.reshape(2 * PLANE * NZL * PROJ, half)
    other = lax.ppermute(own, "c", swap)
    new_master, new_moment, new_second = step(grads, master, moment, second)
    gathered = lay(place, own, other, NZL * NC * master.shape[0])
    return (new_master, new_moment, new_second, gathered)


def solution(mesh):
    fine = Mesh(mesh.devices.reshape(NY, NX, NZH, NZL, NC), REP + SHARD)
    tokens = P(REP + SHARD, None)
    rows = P(SHARD, None)
    return jax.shard_map(
        shards,
        mesh=fine,
        in_specs=(tokens, tokens, tokens, rows, rows, rows),
        out_specs=(rows, rows, rows, P()),
        check_vma=False,
    )
```

time: 142 us -> 134 us (0.944)
  starting transfers between devices: 46 us -> 32.8 us
  waiting for transfers between devices: 23.8 us -> 32.9 us
  blocking collectives: 36.1 us -> 28.4 us
  local copies, waits for them, and re-layouts: 5.81 us -> 8.55 us
    ppermute x1, starting transfers between devices: 16.2 us -> 5.19 us  [shards(): other = lax.ppermute(own, 'c', swap)]
    all_to_all x1 -> x0, blocking collectives: 8.19 us -> none  [shards(): lax.all_to_all(jnp.broadcast_to(unit[None], (NZL, PROJ, width)), 'zl', 0,...]
    ppermute x16 -> x11, starting transfers between devices: 23.9 us -> 19.1 us  [the longest x6 6.24 us: onward(): return lax.ppermute(a, ('y', 'x', 'c'), pairs)]
    all_to_all x0 -> x1, waiting for transfers between devices: none -> 4.37 us  [shards(): lax.all_to_all(jnp.broadcast_to(unit[None], (NZL, PROJ, width)), 'zl', 0,...]
    dynamic_slice x0 -> x2, local copies, waits for them, and re-layouts: none -> 4.11 us  [columns(): return lax.dynamic_slice_in_dim(a, which * half, half, axis=1)]
    ppermute x16 -> x11, waiting for transfers between devices: 18.3 us -> 21.7 us  [the longest x6 19.4 us: onward(): return lax.ppermute(a, ('y', 'x', 'c'), pairs)]
    all_to_all x0 -> x1, starting transfers between devices: none -> 3.37 us  [shards(): lax.all_to_all(jnp.broadcast_to(unit[None], (NZL, PROJ, width)), 'zl', 0,...]
    unnamed x12 -> x10, local copies, waits for them, and re-layouts: 4.28 us -> 0.95 us
  transfers between devices with their start and end apart: 20 -> 16, of which waited for: 10 -> 11; matrix products, arithmetic and copies ran while one was open for 2% -> 4% of each run, Pallas kernels for 7% -> 10%
where the time goes in v3:
time: 134 us; the launch traced here: 133 us
  waiting for transfers between devices  32.9 us (25%)
  starting transfers between devices  32.8 us (24%)
  blocking collectives  28.4 us (21%)
  Pallas kernels  22.4 us (17%)
  local copies, waits for them, and re-layouts  8.55 us (6%)
  other arithmetic  7.24 us (5%)
    all_gather x1, blocking collectives, shards(): lax.all_gather(jnp.concatenate(halves, axis=0), ('y', 'x'), axis=0, tiled...  28.4 us
    ppermute x6, waiting for transfers between devices, onward(): return lax.ppermute(a, ('y', 'x', 'c'), pairs)  19.4 us
    pallas_call x3, Pallas kernels, terms(): pl.pallas_call(functools.partial(terms_kernel, rows, len(sides)), grid=(w...  11.8 us
    ppermute x3, waiting for transfers between devices, ahead(): lax.ppermute(a, ('zh', 'zl'), [(z, (z + by) % ring) for z in range(ring)])  6.3 us
    ppermute x6, starting transfers between devices, onward(): return lax.ppermute(a, ('y', 'x', 'c'), pairs)  6.24 us
    ppermute x1, starting transfers between devices, shards(): other = lax.ppermute(own, 'c', swap)  5.19 us
    ppermute x3, starting transfers between devices, ahead(): lax.ppermute(a, ('zh', 'zl'), [(z, (z + by) % ring) for z in range(ring)])  5.15 us
    ppermute x1, starting transfers between devices, shards(): came = lax.ppermute(part, 'c', swap)  4.89 us
  transfers between devices with their start and end apart: 16, of which 11 were waited for; matrix products, arithmetic and copies ran while one was open for 4% of the time, Pallas kernels for 10%

profile of v3, /device:TPU:1, one launch (start us, length us, event | category | flops | bytes accessed | tf_op | source)
XLA Modules:
  0.0 133.4 jit_solution(2732939113890413780)
XLA Ops:
  0.6 2.9 %constant_dynamic-slice_fusion.3 = (bf16[192,3072]{1,0:T(8,128)(2,1)S(1)}, bf16[192,3072]{1,0:T(8,128)(2,1)}) fusion(bf16[192,6144]{1,0:T(8,128)(2,1)} %param.6, s32[]{:T(128)S(6)} %select_n.31, s32[]{:T(128)S(6)} %select_n.32), kind=kLoop, calls=%fused_computation.29 | loop fusion | bytes 4718600 | tf_op jit(solution)/shard_map/pair/dynamic_slice | solution.py:247
  3.6 3.2 %collective-permute-start.1 = (bf16[192,3072]{1,0:T(8,128)(2,1)}, bf16[192,3072]{1,0:T(8,128)(2,1)S(1)}, u32[]{:S(2)}, u32[]{:S(2)}) collective-permute-start(bf16[192,3072]{1,0:T(8,128)(2,1)} %get-tuple-element.24), channel_id=1, source_target_pairs={{0,1},{1,0},{2,3},{3,2},{4,5},{5,4},{6,7},{7,6},{8,9},{9,8},{10,11... | collective-permute-start | bytes 3538952 | tf_op jit(solution)/shard_map/pair/ppermute | solution.py:252
  6.8 1.2 constant_dynamic-slice_fusion.2
  8.1 0.9 copy-done.3
  9.0 1.2 lefts.1
  10.8 2.7 %terms.4.refs_3_ = f32[384,3072]{1,0:T(8,128)S(1)} custom-call(bf16[512,192]{1,0:T(8,128)(2,1)S(1)} %get-tuple-element.9.refs_0_, bf16[192,3072]{1,0:T(8,128)(2,1)S(1)} %get-tuple-element.23.refs_1_, bf16[192,3072]{1,0:T(8,128)(2,1)S(1)} %get-tuple-element.21.refs_2_), custom_call_target="tpu_custom_call" | custom-call | flops 905969664 | bytes 4718592 | tf_op jit(solution)/shard_map/pair/terms/pallas_call | solution.py:98
  13.6 4.7 %terms.5 = f32[384,3072]{1,0:T(8,128)S(1)} custom-call(bf16[512,192]{1,0:T(8,128)(2,1)S(1)} %collective-permute-done.refs_3_.refs_0_, bf16[192,3072]{1,0:T(8,128)(2,1)S(1)} %collective-permute-done.1.refs_4_.refs_1_, bf16[192,3072]{1,0:T(8,128)(2,1)} %collective-permute-done.2.refs_5_.refs_2_, f32[384,3072]{1,0:T(8,128)S(1)} %terms.4.refs_3_), custom_call_target="tpu_custom_call" | custom-call | flops 905969664 | bytes 4718592 | tf_op jit(solution)/shard_map/pair/terms/pallas_call | solution.py:98
  19.2 2.7 %collective-permute-start.4 = (f16[128,3072]{1,0:T(8,128)(2,1)S(1)}, f16[128,3072]{1,0:T(8,128)(2,1)S(1)}, u32[]{:S(2)}, u32[]{:S(2)}) collective-permute-start(f16[128,3072]{1,0:T(8,128)(2,1)S(1)} %get-tuple-element.20), channel_id=1, source_target_pairs={{0,48},{1,193},{16,0},{17,209},{32,16},{33,225},{48,32},{49,241},{... | collective-permute-start | bytes 2359304 | tf_op jit(solution)/shard_map/plane_sum/ppermute | solution.py:239
  21.9 4.3 %terms.3 = f32[128,3072]{1,0:T(8,128)S(1)} custom-call(bf16[512,192]{1,0:T(8,128)(2,1)S(1)} %get-tuple-element.9.refs_0_, bf16[192,3072]{1,0:T(8,128)(2,1)S(1)} %get-tuple-element.23.refs_1_, bf16[192,3072]{1,0:T(8,128)(2,1)S(1)} %get-tuple-element.21.refs_2_, bf16[512,192]{1,0:T(8,128)(2,1)S(1)} %collective-permute-done.refs_3_.refs_0_, ...), custom_call_target="tpu_custom_call" | custom-call | flops 603979776 | bytes 4718592 | tf_op jit(solution)/shard_map/plane_sum/terms/pallas_call | solution.py:98
  26.2 13.8 %collective-permute-done.3 = f16[128,3072]{1,0:T(8,128)(2,1)S(1)} collective-permute-done((f16[128,3072]{1,0:T(8,128)(2,1)S(1)}, f16[128,3072]{1,0:T(8,128)(2,1)S(1)}, u32[]{:S(2)}, u32[]{:S(2)}) %collective-permute-start.3) | collective-permute-done | bytes 786464 | tf_op jit(solution)/shard_map/plane_sum/ppermute | solution.py:239
  41.1 2.3 %collective-permute-start.7 = (f16[32,3072]{1,0:T(8,128)(2,1)S(1)}, f16[32,3072]{1,0:T(8,128)(2,1)S(1)}, u32[]{:S(2)}, u32[]{:S(2)}) collective-permute-start(f16[32,3072]{1,0:T(8,128)(2,1)S(1)} %get-tuple-element.27), channel_id=1, source_target_pairs={{0,192},{1,49},{16,208},{17,1},{32,224},{33,17},{48,240},{49,33},{... | collective-permute-start | bytes 589832 | tf_op jit(solution)/shard_map/plane_sum/ppermute | solution.py:239
  44.1 2.6 %collective-permute-done.6 = f16[32,3072]{1,0:T(8,128)(2,1)S(1)} collective-permute-done((f16[32,3072]{1,0:T(8,128)(2,1)S(1)}, f16[32,3072]{1,0:T(8,128)(2,1)S(1)}, u32[]{:S(2)}, u32[]{:S(2)}) %collective-permute-start.6) | collective-permute-done | bytes 196640 | tf_op jit(solution)/shard_map/plane_sum/ppermute | solution.py:239
  46.7 1.4 %collective-permute-done.7 = f16[32,3072]{1,0:T(8,128)(2,1)S(1)} collective-permute-done((f16[32,3072]{1,0:T(8,128)(2,1)S(1)}, f16[32,3072]{1,0:T(8,128)(2,1)S(1)}, u32[]{:S(2)}, u32[]{:S(2)}) %collective-permute-start.7) | collective-permute-done | bytes 196640 | tf_op jit(solution)/shard_map/plane_sum/ppermute | solution.py:239
  48.1 1.6 %collective-permute-done.8 = f16[32,3072]{1,0:T(8,128)(2,1)S(1)} collective-permute-done((f16[32,3072]{1,0:T(8,128)(2,1)S(1)}, f16[32,3072]{1,0:T(8,128)(2,1)S(1)}, u32[]{:S(2)}, u32[]{:S(2)}) %collective-permute-start.8) | collective-permute-done | bytes 196640 | tf_op jit(solution)/shard_map/plane_sum/ppermute | solution.py:239
  49.9 5.1 %collective-permute-start.10 = (f32[8,3072]{1,0:T(8,128)S(1)}, f32[8,3072]{1,0:T(8,128)S(1)}, u32[]{:S(2)}, u32[]{:S(2)}) collective-permute-start(f32[8,3072]{1,0:T(8,128)S(1)} %get-tuple-element.30), channel_id=1, source_target_pairs={{0,14},{2,0},{4,2},{6,4},{8,6},{10,8},{12,10},{14,12},{1,15},{3,1}... | collective-permute-start | bytes 294920 | tf_op jit(solution)/shard_map/depth_sum/ppermute | solution.py:231
  55.0 1.6 %collective-permute-done.10 = f32[8,3072]{1,0:T(8,128)S(1)} collective-permute-done((f32[8,3072]{1,0:T(8,128)S(1)}, f32[8,3072]{1,0:T(8,128)S(1)}, u32[]{:S(2)}, u32[]{:S(2)}) %collective-permute-start.10) | collective-permute-done | bytes 98336 | tf_op jit(solution)/shard_map/depth_sum/ppermute | solution.py:231
  56.7 4.5 %collective-permute-done.11 = f32[8,3072]{1,0:T(8,128)S(1)} collective-permute-done((f32[8,3072]{1,0:T(8,128)S(1)}, f32[8,3072]{1,0:T(8,128)S(1)}, u32[]{:S(2)}, u32[]{:S(2)}) %collective-permute-start.11) | collective-permute-done | bytes 98336 | tf_op jit(solution)/shard_map/depth_sum/ppermute | solution.py:231
  62.0 4.2 %collective-permute-start.12 = (f32[8,3072]{1,0:T(8,128)}, f32[8,3072]{1,0:T(8,128)}, u32[]{:S(2)}, u32[]{:S(2)}) collective-permute-start(f32[8,3072]{1,0:T(8,128)} %fusion.10), channel_id=1, source_target_pairs={{0,8},{8,0},{1,9},{9,1},{2,10},{10,2},{3,11},{11,3},{4,12},{12,4},... | collective-permute-start | bytes 294920 | tf_op jit(solution)/shard_map/depth_sum/ppermute | solution.py:266
  66.1 1.7 %multiply_reduce_fusion.1 = (f32[24576]{0:T(1024)S(1)}, f32[24576]{0:T(1024)S(1)}) fusion(f32[16,24576]{1,0:T(8,128)S(1)} %copy-done.1, s32[]{:T(128)S(6)} %select_n.29, f32[16,24576]{1,0:T(8,128)} %moment_ref.1), kind=kLoop, calls=%fused_computation.22 | loop fusion | flops 49152 | bytes 393220 | tf_op jit(solution)/shard_map/own_row/mul | solution.py:28
  68.3 1.4 %collective-permute-done.12 = f32[8,3072]{1,0:T(8,128)} collective-permute-done((f32[8,3072]{1,0:T(8,128)}, f32[8,3072]{1,0:T(8,128)}, u32[]{:S(2)}, u32[]{:S(2)}) %collective-permute-start.12) | collective-permute-done | bytes 98336 | tf_op jit(solution)/shard_map/depth_sum/ppermute | solution.py:266
  69.7 1.0 add.103
  70.6 4.9 %collective-permute-start.13 = (f32[8,3072]{1,0:T(8,128)S(1)}, f32[8,3072]{1,0:T(8,128)S(1)}, u32[]{:S(2)}, u32[]{:S(2)}) collective-permute-start(f32[8,3072]{1,0:T(8,128)S(1)} %add.103), channel_id=1, source_target_pairs={{0,1},{1,0},{2,3},{3,2},{4,5},{5,4},{6,7},{7,6},{8,9},{9,8},{10,11... | collective-permute-start | bytes 294920 | tf_op jit(solution)/shard_map/depth_sum/ppermute | solution.py:267
  75.5 0.9 collective-permute-done.13
  76.5 0.9 multiply_reduce_fusion
  78.3 3.4 %all-to-all-start = ((f16[4,4,6144]{2,1,0:T(4,128)(2,1)}), f16[4,4,6144]{2,1,0:T(4,128)(2,1)S(1)}, u32[]{:S(2)}, u32[]{:S(2)}) async-start(f16[4,4,6144]{2,1,0:T(4,128)(2,1)} %broadcast_in_dim.2), calls=%async_computation | async-start | bytes 393216 | tf_op jit(solution)/shard_map/depth_gather/all_to_all | solution.py:284
  81.6 1.4 %fusion.21 = (f16[4,3072]{1,0:T(4,128)(2,1)}, f16[4,3072]{1,0:T(4,128)(2,1)}) fusion(f16[4,6144]{1,0:T(4,128)(2,1)} %get-tuple-element.33), kind=kLoop, calls=%fused_computation.40 | loop fusion | bytes 98304 | tf_op jit(solution)/shard_map/plane_gather/slice | solution.py:290
  83.0 4.4 %all-to-all-done = f16[4,4,6144]{2,1,0:T(4,128)(2,1)S(1)} async-done(((f16[4,4,6144]{2,1,0:T(4,128)(2,1)}), f16[4,4,6144]{2,1,0:T(4,128)(2,1)S(1)}, u32[]{:S(2)}, u32[]{:S(2)}) %all-to-all-start) | async-done | bytes 196640 | tf_op jit(solution)/shard_map/depth_gather/all_to_all | solution.py:284
  87.5 0.9 pad_maximum_fusion
  88.4 28.4 %all-gather.1 = f16[640,3072]{1,0:T(8,128)(2,1)S(1)} all-gather(f16[40,3072]{1,0:T(8,128)(2,1)S(1)} %pad_maximum_fusion), channel_id=1, replica_groups=mesh['y'=4,'x'=4,'zh'=2,'zl'=4,'c'=2] {'y','x'}, dimensions={0}, use_global_device_ids=true | all-gather | bytes 4177920 | tf_op jit(solution)/shard_map/plane_gather/all_gather | solution.py:291
  117.9 5.2 %collective-permute-start.14 = (bf16[512,3072]{1,0:T(8,128)(2,1)S(1)}, bf16[512,3072]{1,0:T(8,128)(2,1)S(1)}, u32[]{:S(2)}, u32[]{:S(2)}) collective-permute-start(bf16[512,3072]{1,0:T(8,128)(2,1)S(1)} %bitcast.14), channel_id=1, source_target_pairs={{0,1},{1,0},{2,3},{3,2},{4,5},{5,4},{6,7},{7,6},{8,9},{9,8},{10,11... | collective-permute-start | bytes 9437192 | tf_op jit(solution)/shard_map/ppermute | solution.py:297
  123.2 4.6 %step.1 = (f32[16,24576]{1,0:T(8,128)}, f32[16,24576]{1,0:T(8,128)}, f32[16,24576]{1,0:T(8,128)}) custom-call(f32[128,3072]{1,0:T(8,128)S(1)} %fusion.g_ref, f32[16,24576]{1,0:T(8,128)S(1)} %copy-done, f32[16,24576]{1,0:T(8,128)S(1)} %copy-done.2, f32[16,24576]{1,0:T(8,128)S(1)} %copy-done.1), custom_call_target="tpu_custom_call" | custom-call | flops 100663296 | bytes 9437184 | tf_op jit(solution)/shard_map/step/pallas_call | solution.py:147
  128.4 4.9 %lay.1 = bf16[128,24576]{1,0:T(8,128)(2,1)} custom-call(s32[4]{0:T(128)S(1)} %pad_add_fusion.place_ref, bf16[512,3072]{1,0:T(8,128)(2,1)S(1)} %bitcast.15, bf16[512,3072]{1,0:T(8,128)(2,1)S(1)} %collective-permute-done.14.other_ref), custom_call_target="tpu_custom_call" | custom-call | flops 1610612736 | bytes 12582912 | tf_op jit(solution)/shard_map/lay/pallas_call | solution.py:204
  (46 shorter events, 7.6 us)
Async XLA Ops:
  0.6 6.2 %copy-start.4 = (bf16[192,6144]{1,0:T(8,128)(2,1)S(1)}, bf16[192,6144]{1,0:T(8,128)(2,1)}, u32[]{:S(2)}) copy-start(bf16[192,6144]{1,0:T(8,128)(2,1)} %param.7) | copy-start | bytes 7077892
  3.6 10.0 %collective-permute-start.1 = (bf16[192,3072]{1,0:T(8,128)(2,1)}, bf16[192,3072]{1,0:T(8,128)(2,1)S(1)}, u32[]{:S(2)}, u32[]{:S(2)}) collective-permute-start(bf16[192,3072]{1,0:T(8,128)(2,1)} %get-tuple-element.24), channel_id=1, source_target_pairs={{0,1},{1,0},{2,3},{3,2},{4,5},{5,4},{6,7},{7,6},{8,9},{9,8},{10,11... | collective-permute-start | bytes 3538952 | tf_op jit(solution)/shard_map/pair/ppermute | solution.py:252
  8.0 5.6 %collective-permute-start.2 = (bf16[192,3072]{1,0:T(8,128)(2,1)}, bf16[192,3072]{1,0:T(8,128)(2,1)}, u32[]{:S(2)}, u32[]{:S(2)}) collective-permute-start(bf16[192,3072]{1,0:T(8,128)(2,1)} %get-tuple-element.22), channel_id=1, source_target_pairs={{0,1},{1,0},{2,3},{3,2},{4,5},{5,4},{6,7},{7,6},{8,9},{9,8},{10,11... | collective-permute-start | bytes 3538952 | tf_op jit(solution)/shard_map/pair/ppermute | solution.py:253
  8.1 0.9 copy-start.3
  10.2 3.3 %collective-permute-start = (bf16[512,192]{1,0:T(8,128)(2,1)S(1)}, bf16[512,192]{1,0:T(8,128)(2,1)S(1)}, u32[]{:S(2)}, u32[]{:S(2)}) collective-permute-start(bf16[512,192]{1,0:T(8,128)(2,1)S(1)} %get-tuple-element.10), channel_id=1, source_target_pairs={{0,1},{1,0},{2,3},{3,2},{4,5},{5,4},{6,7},{7,6},{8,9},{9,8},{10,11... | collective-permute-start | bytes 589832 | tf_op jit(solution)/shard_map/pair/ppermute | solution.py:251
  19.1 20.8 %collective-permute-start.3 = (f16[128,3072]{1,0:T(8,128)(2,1)S(1)}, f16[128,3072]{1,0:T(8,128)(2,1)S(1)}, u32[]{:S(2)}, u32[]{:S(2)}) collective-permute-start(f16[128,3072]{1,0:T(8,128)(2,1)S(1)} %get-tuple-element.18), channel_id=1, source_target_pairs={{0,16},{1,65},{16,32},{17,81},{32,48},{33,97},{48,0},{49,113},{64,... | collective-permute-start | bytes 2359304 | tf_op jit(solution)/shard_map/plane_sum/ppermute | solution.py:239
  19.2 20.8 %collective-permute-start.4 = (f16[128,3072]{1,0:T(8,128)(2,1)S(1)}, f16[128,3072]{1,0:T(8,128)(2,1)S(1)}, u32[]{:S(2)}, u32[]{:S(2)}) collective-permute-start(f16[128,3072]{1,0:T(8,128)(2,1)S(1)} %get-tuple-element.20), channel_id=1, source_target_pairs={{0,48},{1,193},{16,0},{17,209},{32,16},{33,225},{48,32},{49,241},{... | collective-permute-start | bytes 2359304 | tf_op jit(solution)/shard_map/plane_sum/ppermute | solution.py:239
  21.9 18.1 %collective-permute-start.5 = (f16[128,3072]{1,0:T(8,128)(2,1)S(1)}, f16[128,3072]{1,0:T(8,128)(2,1)S(1)}, u32[]{:S(2)}, u32[]{:S(2)}) collective-permute-start(f16[128,3072]{1,0:T(8,128)(2,1)S(1)} %get-tuple-element.19), channel_id=1, source_target_pairs={{0,32},{1,129},{16,48},{17,145},{32,0},{33,161},{48,16},{49,177},{... | collective-permute-start | bytes 2359304 | tf_op jit(solution)/shard_map/plane_sum/ppermute | solution.py:239
  40.5 25.6 %copy-start.1 = (f32[16,24576]{1,0:T(8,128)S(1)}, f32[16,24576]{1,0:T(8,128)}, u32[]{:S(2)}) copy-start(f32[16,24576]{1,0:T(8,128)} %second_ref.1) | copy-start | bytes 4718596
  40.6 6.1 %collective-permute-start.6 = (f16[32,3072]{1,0:T(8,128)(2,1)S(1)}, f16[32,3072]{1,0:T(8,128)(2,1)S(1)}, u32[]{:S(2)}, u32[]{:S(2)}) collective-permute-start(f16[32,3072]{1,0:T(8,128)(2,1)S(1)} %get-tuple-element.25), channel_id=1, source_target_pairs={{0,64},{1,17},{16,80},{17,33},{32,96},{33,49},{48,112},{49,1},{64,... | collective-permute-start | bytes 589832 | tf_op jit(solution)/shard_map/plane_sum/ppermute | solution.py:239
  41.1 7.0 %collective-permute-start.7 = (f16[32,3072]{1,0:T(8,128)(2,1)S(1)}, f16[32,3072]{1,0:T(8,128)(2,1)S(1)}, u32[]{:S(2)}, u32[]{:S(2)}) collective-permute-start(f16[32,3072]{1,0:T(8,128)(2,1)S(1)} %get-tuple-element.27), channel_id=1, source_target_pairs={{0,192},{1,49},{16,208},{17,1},{32,224},{33,17},{48,240},{49,33},{... | collective-permute-start | bytes 589832 | tf_op jit(solution)/shard_map/plane_sum/ppermute | solution.py:239
  43.4 6.3 %collective-permute-start.8 = (f16[32,3072]{1,0:T(8,128)(2,1)S(1)}, f16[32,3072]{1,0:T(8,128)(2,1)S(1)}, u32[]{:S(2)}, u32[]{:S(2)}) collective-permute-start(f16[32,3072]{1,0:T(8,128)(2,1)S(1)} %get-tuple-element.26), channel_id=1, source_target_pairs={{0,128},{1,33},{16,144},{17,49},{32,160},{33,1},{48,176},{49,17},{... | collective-permute-start | bytes 589832 | tf_op jit(solution)/shard_map/plane_sum/ppermute | solution.py:239
  49.7 18.2 %copy-start = (f32[16,24576]{1,0:T(8,128)S(1)}, f32[16,24576]{1,0:T(8,128)}, u32[]{:S(2)}) copy-start(f32[16,24576]{1,0:T(8,128)} %master_ref.1) | copy-start | bytes 4718596
  49.9 6.8 %collective-permute-start.10 = (f32[8,3072]{1,0:T(8,128)S(1)}, f32[8,3072]{1,0:T(8,128)S(1)}, u32[]{:S(2)}, u32[]{:S(2)}) collective-permute-start(f32[8,3072]{1,0:T(8,128)S(1)} %get-tuple-element.30), channel_id=1, source_target_pairs={{0,14},{2,0},{4,2},{6,4},{8,6},{10,8},{12,10},{14,12},{1,15},{3,1}... | collective-permute-start | bytes 294920 | tf_op jit(solution)/shard_map/depth_sum/ppermute | solution.py:231
  55.0 6.1 %collective-permute-start.11 = (f32[8,3072]{1,0:T(8,128)S(1)}, f32[8,3072]{1,0:T(8,128)S(1)}, u32[]{:S(2)}, u32[]{:S(2)}) collective-permute-start(f32[8,3072]{1,0:T(8,128)S(1)} %get-tuple-element.29), channel_id=1, source_target_pairs={{0,4},{2,6},{4,8},{6,10},{8,12},{10,14},{12,0},{14,2},{1,5},{3,7},... | collective-permute-start | bytes 294920 | tf_op jit(solution)/shard_map/depth_sum/ppermute | solution.py:231
  55.0 6.3 %collective-permute-start.9 = (f32[8,3072]{1,0:T(8,128)S(1)}, f32[8,3072]{1,0:T(8,128)S(1)}, u32[]{:S(2)}, u32[]{:S(2)}) collective-permute-start(f32[8,3072]{1,0:T(8,128)S(1)} %get-tuple-element.28), channel_id=1, source_target_pairs={{0,2},{2,4},{4,6},{6,8},{8,10},{10,12},{12,14},{14,0},{1,3},{3,5},... | collective-permute-start | bytes 294920 | tf_op jit(solution)/shard_map/depth_sum/ppermute | solution.py:231
  62.0 7.7 %collective-permute-start.12 = (f32[8,3072]{1,0:T(8,128)}, f32[8,3072]{1,0:T(8,128)}, u32[]{:S(2)}, u32[]{:S(2)}) collective-permute-start(f32[8,3072]{1,0:T(8,128)} %fusion.10), channel_id=1, source_target_pairs={{0,8},{8,0},{1,9},{9,1},{2,10},{10,2},{3,11},{11,3},{4,12},{12,4},... | collective-permute-start | bytes 294920 | tf_op jit(solution)/shard_map/depth_sum/ppermute | solution.py:266
  70.6 5.8 %collective-permute-start.13 = (f32[8,3072]{1,0:T(8,128)S(1)}, f32[8,3072]{1,0:T(8,128)S(1)}, u32[]{:S(2)}, u32[]{:S(2)}) collective-permute-start(f32[8,3072]{1,0:T(8,128)S(1)} %add.103), channel_id=1, source_target_pairs={{0,1},{1,0},{2,3},{3,2},{4,5},{5,4},{6,7},{7,6},{8,9},{9,8},{10,11... | collective-permute-start | bytes 294920 | tf_op jit(solution)/shard_map/depth_sum/ppermute | solution.py:267
  78.3 9.1 %all-to-all-start = ((f16[4,4,6144]{2,1,0:T(4,128)(2,1)}), f16[4,4,6144]{2,1,0:T(4,128)(2,1)S(1)}, u32[]{:S(2)}, u32[]{:S(2)}) async-start(f16[4,4,6144]{2,1,0:T(4,128)(2,1)} %broadcast_in_dim.2), calls=%async_computation | async-start | bytes 393216 | tf_op jit(solution)/shard_map/depth_gather/all_to_all | solution.py:284
  117.9 5.3 %copy-start.2 = (f32[16,24576]{1,0:T(8,128)S(1)}, f32[16,24576]{1,0:T(8,128)}, u32[]{:S(2)}) copy-start(f32[16,24576]{1,0:T(8,128)} %moment_ref.1) | copy-start | bytes 4718596
  117.9 10.5 %collective-permute-start.14 = (bf16[512,3072]{1,0:T(8,128)(2,1)S(1)}, bf16[512,3072]{1,0:T(8,128)(2,1)S(1)}, u32[]{:S(2)}, u32[]{:S(2)}) collective-permute-start(bf16[512,3072]{1,0:T(8,128)(2,1)S(1)} %bitcast.14), channel_id=1, source_target_pairs={{0,1},{1,0},{2,3},{3,2},{4,5},{5,4},{6,7},{7,6},{8,9},{9,8},{10,11... | collective-permute-start | bytes 9437192 | tf_op jit(solution)/shard_map/ppermute | solution.py:297

commit v4 on v3

--- a/solution.py
+++ b/solution.py
@@ -26,8 +26,8 @@
 def adam_update(gradient, master, moment, second):
     new_moment = beta_one * moment + (1.0 - beta_one) * gradient
     new_second = beta_two * second + (1.0 - beta_two) * gradient * gradient
-    stepped = master - learn_rate * (new_moment / bias_one) / (
-        jnp.sqrt(new_second / bias_two) + 1e-08
+    stepped = master - (learn_rate / bias_one) * new_moment / (
+        jnp.sqrt(new_second * (1.0 / bias_two)) + 1e-08
     )
     return (stepped, new_moment, new_second)
 
@@ -68,152 +68,153 @@
     masked_ref[1] = jnp.where(k == 3, left.astype(jnp.float32), 0.0).astype(left.dtype)
 
 
-def two_dots(left_ref, x_ref, a_ref):
-    total = jnp.dot(left_ref[0], x_ref[...], preferred_element_type=jnp.float32)
-    return total + jnp.dot(left_ref[1], a_ref[...], preferred_element_type=jnp.float32)
-
-
-def terms_kernel(rows, sides, *refs):
-    inputs, (base_refs, out_ref, masked) = refs[: 3 * sides], (refs[3 * sides : -1 - sides], refs[-1 - sides], refs[-sides:])
+def terms_kernel(rows, sides, tile, *refs):
+    inputs, rest = refs[: 3 * sides], refs[3 * sides :]
+    bases, out_ref, masked = rest[: -1 - sides], rest[-1 - sides], rest[-sides:]
     groups = [inputs[3 * n : 3 * n + 3] for n in range(sides)]
-
-    @pl.when(pl.program_id(0) == 0)
-    def _():
-        for (left_ref, _, _), masked_ref in zip(groups, masked):
-            mask_rows(left_ref, rows, masked_ref)
-
-    total = base_refs[0][...] if base_refs else 0.0
-    for (_, x_ref, a_ref), masked_ref in zip(groups, masked):
-        total += two_dots(masked_ref, x_ref, a_ref)
-    out_ref[...] = total
+    for (left_ref, _, _), masked_ref in zip(groups, masked):
+        mask_rows(left_ref, rows, masked_ref)
+
+    @pl.loop(0, out_ref.shape[1] // tile)
+    def _(j):
+        at = pl.ds(pl.multiple_of(j * tile, tile), tile)
+        total = bases[0][:, at] if bases else 0.0
+        for (_, x_ref, a_ref), masked_ref in zip(groups, masked):
+            total += jnp.dot(masked_ref[0], x_ref[:, at], preferred_element_type=jnp.float32)
+            total += jnp.dot(masked_ref[1], a_ref[:, at], preferred_element_type=jnp.float32)
+        out_ref[:, at] = total
 
 
 def terms(rows, *sides, base=None, tile=512):
     tokens, width = sides[0][1].shape
     count = rows.stop - rows.start
-    left = pl.BlockSpec(sides[0][0].shape, lambda j: (0, 0))
-    block = pl.BlockSpec((tokens, tile), lambda j: (0, j))
-    result = pl.BlockSpec((count, tile), lambda j: (0, j))
-    bases = [] if base is None else [base]
+    operands = [a for side in sides for a in side] + ([] if base is None else [base])
     return pl.pallas_call(
-        functools.partial(terms_kernel, rows, len(sides)),
-        grid=(width // tile,),
-        in_specs=[left, block, block] * len(sides) + [result] * len(bases),
-        out_specs=result,
+        functools.partial(terms_kernel, rows, len(sides), tile),
+        in_specs=[pl.BlockSpec(memory_space=pltpu.VMEM)] * len(operands),
+        out_specs=pl.BlockSpec(memory_space=pltpu.VMEM),
         out_shape=jax.ShapeDtypeStruct((count, width), jnp.float32),
         scratch_shapes=[pltpu.VMEM((2, count, tokens), jnp.bfloat16)] * len(sides),
-        compiler_params=pltpu.CompilerParams(vmem_limit_bytes=24 * 2**20),
+        compiler_params=pltpu.CompilerParams(vmem_limit_bytes=32 * 2**20),
         cost_estimate=pl.CostEstimate(
             flops=4 * len(sides) * count * tokens * width,
             bytes_accessed=8 * tokens * width,
             transcendentals=0,
         ),
         name="terms",
-    )(*(a for side in sides for a in side), *bases)
-
-
-def step_kernel(g_ref, master_ref, moment_ref, second_ref, nm_ref, mo_ref, se_ref, grad_ref):
-    k = pl.program_id(0)
-    rows, width = master_ref.shape
-
-    @pl.when(k == 0)
-    def _():
-        shape = (PROJ * rows, g_ref.shape[0])
-        m = lax.broadcasted_iota(jnp.int32, shape, 0)
-        j = lax.broadcasted_iota(jnp.int32, shape, 1)
-        coarse = g_ref[...].astype(jnp.bfloat16)
-        fine = (g_ref[...] - coarse.astype(jnp.float32)).astype(jnp.bfloat16)
-        for at in range(2):
-            wanted = j == 2 * PROJ * (m & 15) + PROJ * at + (m >> 4)
-            pick = jnp.where(wanted, 1.0, 0.0).astype(jnp.bfloat16)
-            total = jnp.dot(pick, coarse, preferred_element_type=jnp.float32)
-            total += jnp.dot(pick, fine, preferred_element_type=jnp.float32)
-            grad_ref[:, at * width // 2 : (at + 1) * width // 2] = total
-
-    gradient = grad_ref[pl.ds(pl.multiple_of(k * rows, rows), rows), :]
-    stepped, new_moment, new_second = adam_update(
-        gradient, master_ref[...], moment_ref[...], second_ref[...]
-    )
-    mo_ref[...] = new_moment
-    se_ref[...] = new_second
-    scale = jnp.sqrt(jnp.sum(stepped * stepped, axis=1, keepdims=True) + 1e-06)
-    nm_ref[...] = stepped / scale
-
-
-def step(u, master, moment, second):
+    )(*operands)
+
+
+def step_kernel(g_ref, *refs):
+    state_refs, out_refs, (made, grad_ref, out_sems) = refs[:3], refs[3:6], refs[6:]
+    rows, width = grad_ref.shape[0] // PROJ, grad_ref.shape[1]
+
+    def part(k):
+        return slice(None), slice(k * width, (k + 1) * width)
+
+    def leaving(n, k):
+        return pltpu.make_async_copy(made.at[n, k], out_refs[n].at[part(k)], out_sems.at[n, k])
+
+    shape = (PROJ * rows, g_ref.shape[0])
+    m = lax.broadcasted_iota(jnp.int32, shape, 0)
+    j = lax.broadcasted_iota(jnp.int32, shape, 1)
+    coarse = g_ref[...].astype(jnp.bfloat16)
+    fine = (g_ref[...] - coarse.astype(jnp.float32)).astype(jnp.bfloat16)
+    for at in range(2):
+        wanted = j == 2 * PROJ * (m & 15) + PROJ * at + (m >> 4)
+        pick = jnp.where(wanted, 1.0, 0.0).astype(jnp.bfloat16)
+        total = jnp.dot(pick, coarse, preferred_element_type=jnp.float32)
+        total += jnp.dot(pick, fine, preferred_element_type=jnp.float32)
+        grad_ref[:, at * width // 2 : (at + 1) * width // 2] = total
+    for k in range(PROJ):
+        gradient = grad_ref[k * rows : (k + 1) * rows]
+        stepped, new_moment, new_second = adam_update(
+            gradient, *(ref[part(k)] for ref in state_refs)
+        )
+        made[1, k] = new_moment
+        leaving(1, k).start()
+        made[2, k] = new_second
+        leaving(2, k).start()
+        scale = jnp.sqrt(jnp.sum(stepped * stepped, axis=1, keepdims=True) + 1e-06)
+        made[0, k] = stepped * (1.0 / scale)
+        leaving(0, k).start()
+    for k in range(PROJ):
+        for n in range(3):
+            leaving(n, k).wait()
+
+
+def step(g, master, moment, second):
     rows, width = master.shape
     width //= PROJ
-    block = pl.BlockSpec((rows, width), lambda k: (0, k))
+    anywhere = pl.BlockSpec(memory_space=pl.ANY)
     return pl.pallas_call(
         step_kernel,
-        grid=(PROJ,),
-        in_specs=[pl.BlockSpec(u.shape, lambda k: (0, 0)), block, block, block],
-        out_specs=[block, block, block],
+        in_specs=[pl.BlockSpec(memory_space=pltpu.VMEM)] * 4,
+        out_specs=[anywhere] * 3,
         out_shape=[jax.ShapeDtypeStruct(master.shape, jnp.float32)] * 3,
-        scratch_shapes=[pltpu.VMEM((PROJ * rows, width), jnp.float32)],
-        compiler_params=pltpu.CompilerParams(vmem_limit_bytes=40 * 2**20),
+        scratch_shapes=[
+            pltpu.VMEM((3, PROJ, rows, width), jnp.float32),
+            pltpu.VMEM((PROJ * rows, width), jnp.float32),
+            pltpu.SemaphoreType.DMA((3, PROJ)),
+        ],
+        compiler_params=pltpu.CompilerParams(vmem_limit_bytes=28 * 2**20),
         cost_estimate=pl.CostEstimate(
-            flops=2 * 64 * 128 * width, bytes_accessed=24 * rows * width * PROJ, transcendentals=0
+            flops=20 * 64 * width, bytes_accessed=24 * rows * width * PROJ, transcendentals=0
         ),
         name="step",
-    )(u, master, moment, second)
+    )(g, master, moment, second)
 
 
 def lay_kernel(place_ref, own_ref, other_ref, out_ref, held_ref, sems):
-    j = pl.program_id(0)
-    last = pl.num_programs(0) - 1
-    parts, tile = own_ref.shape
-    width = tile * (last + 1)
-    slot = lax.rem(j, 2)
-
-    def copies(step, slot):
-        for k in range(PROJ):
-            at = pl.ds(pl.multiple_of(k * width + step * tile, 128), tile)
-            yield pltpu.make_async_copy(held_ref.at[slot, k], out_ref.at[:, at], sems.at[slot, k])
-
-    @pl.when(j >= 2)
-    def _():
-        for copy in copies(j - 2, slot):
-            copy.wait()
-
-    m = lax.broadcasted_iota(jnp.int32, (256, parts), 0)
-    n = lax.broadcasted_iota(jnp.int32, (256, parts), 1)
+    slots, tile = sems.shape[0], held_ref.shape[3]
+    parts, half = own_ref.shape[0] // 2, own_ref.shape[1]
+    m = lax.broadcasted_iota(jnp.int32, (parts, parts), 0)
+    n = lax.broadcasted_iota(jnp.int32, (parts, parts), 1)
     wanted = n == (m & 15) * 16 + ((m >> 4) & 3) * 4 + (m >> 6)
     pick = jnp.where(wanted, 1.0 / UNIT_SCALE, 0.0).astype(jnp.bfloat16)
-    for ref, core in ((own_ref, place_ref[0]), (other_ref, 1 - place_ref[0])):
-        rows = jnp.dot(pick, ref[...], preferred_element_type=jnp.float32).astype(out_ref.dtype)
+
+    def leaving(j, k):
+        at = slice(k * 2 * half + j * tile, k * 2 * half + (j + 1) * tile)
+        return pltpu.make_async_copy(
+            held_ref.at[j % slots, k], out_ref.at[:, at], sems.at[j % slots, k]
+        )
+
+    steps = 2 * half // tile
+    for j in range(steps):
+        if j >= slots:
+            for k in range(PROJ):
+                leaving(j - slots, k).wait()
+        side, at = divmod(j * tile, half)
+        for ref, core in ((own_ref, place_ref[0]), (other_ref, 1 - place_ref[0])):
+            values = ref[side * parts : (side + 1) * parts, at : at + tile]
+            rows = jnp.dot(pick, values, preferred_element_type=jnp.float32).astype(out_ref.dtype)
+            for k in range(PROJ):
+                for zl in range(NZL):
+                    to = pl.ds(pl.multiple_of(32 * zl + 16 * core, 16), 16)
+                    start = 64 * k + 16 * zl
+                    held_ref[j % slots, k, to] = rows[start : start + 16]
         for k in range(PROJ):
-            for zl in range(NZL):
-                to = pl.ds(pl.multiple_of(32 * zl + 16 * core, 16), 16)
-                held_ref[slot, k, to] = rows[64 * k + 16 * zl : 64 * k + 16 * zl + 16]
-    for copy in copies(j, slot):
-        copy.start()
-
-    @pl.when(j == last)
-    def _():
-        for copy in copies(j - 1, 1 - slot):
-            copy.wait()
-        for copy in copies(j, slot):
-            copy.wait()
-
-
-def lay(place, own, other, rows, tile=1536):
-    parts, half = own.shape[0] // 2, own.shape[1]
-    width = 2 * half
-    block = pl.BlockSpec((parts, tile), lambda j: (j // (half // tile), j % (half // tile)))
+            leaving(j, k).start()
+    for j in range(max(steps - slots, 0), steps):
+        for k in range(PROJ):
+            leaving(j, k).wait()
+
+
+def lay(place, own, other, rows, tile=768, slots=4):
+    width = 2 * own.shape[1]
     return pl.pallas_call(
         lay_kernel,
-        grid=(width // tile,),
-        in_specs=[pl.BlockSpec(memory_space=pltpu.SMEM), block, block],
+        in_specs=[pl.BlockSpec(memory_space=pltpu.SMEM)]
+        + [pl.BlockSpec(memory_space=pltpu.VMEM)] * 2,
         out_specs=pl.BlockSpec(memory_space=pl.ANY),
         out_shape=jax.ShapeDtypeStruct((rows, PROJ * width), jnp.bfloat16),
         scratch_shapes=[
-            pltpu.VMEM((2, PROJ, rows, tile), jnp.bfloat16),
-            pltpu.SemaphoreType.DMA((2, PROJ)),
+            pltpu.VMEM((slots, PROJ, rows, tile), jnp.bfloat16),
+            pltpu.SemaphoreType.DMA((slots, PROJ)),
         ],
-        compiler_params=pltpu.CompilerParams(vmem_limit_bytes=24 * 2**20),
+        compiler_params=pltpu.CompilerParams(vmem_limit_bytes=28 * 2**20),
         cost_estimate=pl.CostEstimate(
-            flops=4 * 256 * parts * width, bytes_accessed=8 * parts * width, transcendentals=0
+            flops=2 * 256 * own.size, bytes_accessed=4 * own.size, transcendentals=0
         ),
         name="lay",
     )(place, own, other)

time: 134 us -> 132 us (0.985)
  Pallas kernels: 22.4 us -> 18.3 us
  waiting for transfers between devices: 32.9 us -> 34.8 us
    pallas_call x5, Pallas kernels: 21.3 us -> 17.2 us  [the longest x3 8.91 us: terms(): pl.pallas_call(functools.partial(terms_kernel, rows, len(sides), tile), i...]
  transfers between devices with their start and end apart: 16 -> 16, of which waited for: 11 -> 11; matrix products, arithmetic and copies ran while one was open for 4% -> 4% of each run, Pallas kernels for 10% -> 8%
where the time goes in v4:
time: 132 us; the launch traced here: 131 us
  waiting for transfers between devices  34.8 us (26%)
  starting transfers between devices  32.7 us (25%)
  blocking collectives  28.4 us (22%)
  Pallas kernels  18.3 us (14%)
  local copies, waits for them, and re-layouts  8.55 us (6%)
  other arithmetic  7.24 us (5%)
    all_gather x1, blocking collectives, shards(): lax.all_gather(jnp.concatenate(halves, axis=0), ('y', 'x'), axis=0, tiled...  28.4 us
    ppermute x6, waiting for transfers between devices, onward(): return lax.ppermute(a, ('y', 'x', 'c'), pairs)  20.5 us
    pallas_call x3, Pallas kernels, terms(): pl.pallas_call(functools.partial(terms_kernel, rows, len(sides), tile), i...  8.91 us
    ppermute x3, waiting for transfers between devices, ahead(): lax.ppermute(a, ('zh', 'zl'), [(z, (z + by) % ring) for z in range(ring)])  6.3 us
    ppermute x6, starting transfers between devices, onward(): return lax.ppermute(a, ('y', 'x', 'c'), pairs)  6.24 us
    ppermute x3, starting transfers between devices, ahead(): lax.ppermute(a, ('zh', 'zl'), [(z, (z + by) % ring) for z in range(ring)])  5.15 us
    ppermute x1, starting transfers between devices, shards(): other = lax.ppermute(own, 'c', swap)  5.07 us
    ppermute x1, starting transfers between devices, shards(): came = lax.ppermute(part, 'c', swap)  4.89 us
  transfers between devices with their start and end apart: 16, of which 11 were waited for; matrix products, arithmetic and copies ran while one was open for 4% of the time, Pallas kernels for 8%

profile of v4, /device:TPU:1, one launch (start us, length us, event | category | flops | bytes accessed | tf_op | source)
XLA Modules:
  0.0 131.1 jit_solution(7649238519302732389)
XLA Ops:
  0.6 2.9 %constant_dynamic-slice_fusion.3 = (bf16[192,3072]{1,0:T(8,128)(2,1)S(1)}, bf16[192,3072]{1,0:T(8,128)(2,1)}) fusion(bf16[192,6144]{1,0:T(8,128)(2,1)} %param.6, s32[]{:T(128)S(6)} %select_n.31, s32[]{:T(128)S(6)} %select_n.32), kind=kLoop, calls=%fused_computation.29 | loop fusion | bytes 4718600 | tf_op jit(solution)/shard_map/pair/dynamic_slice | solution.py:248
  3.6 3.2 %collective-permute-start.1 = (bf16[192,3072]{1,0:T(8,128)(2,1)}, bf16[192,3072]{1,0:T(8,128)(2,1)S(1)}, u32[]{:S(2)}, u32[]{:S(2)}) collective-permute-start(bf16[192,3072]{1,0:T(8,128)(2,1)} %get-tuple-element.24), channel_id=1, source_target_pairs={{0,1},{1,0},{2,3},{3,2},{4,5},{5,4},{6,7},{7,6},{8,9},{9,8},{10,11... | collective-permute-start | bytes 3538952 | tf_op jit(solution)/shard_map/pair/ppermute | solution.py:253
  6.8 1.2 constant_dynamic-slice_fusion.2
  8.1 0.9 copy-done.3
  9.0 1.2 lefts.1
  10.8 2.2 %terms.4.refs_3_ = f32[384,3072]{1,0:T(8,128)S(1)} custom-call(bf16[512,192]{1,0:T(8,128)(2,1)S(1)} %get-tuple-element.9.refs_0_, bf16[192,3072]{1,0:T(8,128)(2,1)S(1)} %get-tuple-element.23.refs_1_, bf16[192,3072]{1,0:T(8,128)(2,1)S(1)} %get-tuple-element.21.refs_2_), custom_call_target="tpu_custom_call" | custom-call | flops 905969664 | bytes 4718592 | tf_op jit(solution)/shard_map/pair/terms/pallas_call | solution.py:92
  13.1 3.5 %terms.5 = f32[384,3072]{1,0:T(8,128)S(1)} custom-call(bf16[512,192]{1,0:T(8,128)(2,1)S(1)} %collective-permute-done.refs_3_.refs_0_, bf16[192,3072]{1,0:T(8,128)(2,1)S(1)} %collective-permute-done.1.refs_4_.refs_1_, bf16[192,3072]{1,0:T(8,128)(2,1)} %collective-permute-done.2.refs_5_.refs_2_, f32[384,3072]{1,0:T(8,128)S(1)} %terms.4.refs_3_), custom_call_target="tpu_custom_call" | custom-call | flops 905969664 | bytes 4718592 | tf_op jit(solution)/shard_map/pair/terms/pallas_call | solution.py:92
  17.5 2.7 %collective-permute-start.4 = (f16[128,3072]{1,0:T(8,128)(2,1)S(1)}, f16[128,3072]{1,0:T(8,128)(2,1)S(1)}, u32[]{:S(2)}, u32[]{:S(2)}) collective-permute-start(f16[128,3072]{1,0:T(8,128)(2,1)S(1)} %get-tuple-element.20), channel_id=1, source_target_pairs={{0,48},{1,193},{16,0},{17,209},{32,16},{33,225},{48,32},{49,241},{... | collective-permute-start | bytes 2359304 | tf_op jit(solution)/shard_map/plane_sum/ppermute | solution.py:240
  20.2 3.1 %terms.3 = f32[128,3072]{1,0:T(8,128)S(1)} custom-call(bf16[512,192]{1,0:T(8,128)(2,1)S(1)} %get-tuple-element.9.refs_0_, bf16[192,3072]{1,0:T(8,128)(2,1)S(1)} %get-tuple-element.23.refs_1_, bf16[192,3072]{1,0:T(8,128)(2,1)S(1)} %get-tuple-element.21.refs_2_, bf16[512,192]{1,0:T(8,128)(2,1)S(1)} %collective-permute-done.refs_3_.refs_0_, ...), custom_call_target="tpu_custom_call" | custom-call | flops 603979776 | bytes 4718592 | tf_op jit(solution)/shard_map/plane_sum/terms/pallas_call | solution.py:92
  23.4 14.9 %collective-permute-done.3 = f16[128,3072]{1,0:T(8,128)(2,1)S(1)} collective-permute-done((f16[128,3072]{1,0:T(8,128)(2,1)S(1)}, f16[128,3072]{1,0:T(8,128)(2,1)S(1)}, u32[]{:S(2)}, u32[]{:S(2)}) %collective-permute-start.3) | collective-permute-done | bytes 786464 | tf_op jit(solution)/shard_map/plane_sum/ppermute | solution.py:240
  39.4 2.3 %collective-permute-start.7 = (f16[32,3072]{1,0:T(8,128)(2,1)S(1)}, f16[32,3072]{1,0:T(8,128)(2,1)S(1)}, u32[]{:S(2)}, u32[]{:S(2)}) collective-permute-start(f16[32,3072]{1,0:T(8,128)(2,1)S(1)} %get-tuple-element.27), channel_id=1, source_target_pairs={{0,192},{1,49},{16,208},{17,1},{32,224},{33,17},{48,240},{49,33},{... | collective-permute-start | bytes 589832 | tf_op jit(solution)/shard_map/plane_sum/ppermute | solution.py:240
  42.4 2.6 %collective-permute-done.6 = f16[32,3072]{1,0:T(8,128)(2,1)S(1)} collective-permute-done((f16[32,3072]{1,0:T(8,128)(2,1)S(1)}, f16[32,3072]{1,0:T(8,128)(2,1)S(1)}, u32[]{:S(2)}, u32[]{:S(2)}) %collective-permute-start.6) | collective-permute-done | bytes 196640 | tf_op jit(solution)/shard_map/plane_sum/ppermute | solution.py:240
  45.1 1.4 %collective-permute-done.7 = f16[32,3072]{1,0:T(8,128)(2,1)S(1)} collective-permute-done((f16[32,3072]{1,0:T(8,128)(2,1)S(1)}, f16[32,3072]{1,0:T(8,128)(2,1)S(1)}, u32[]{:S(2)}, u32[]{:S(2)}) %collective-permute-start.7) | collective-permute-done | bytes 196640 | tf_op jit(solution)/shard_map/plane_sum/ppermute | solution.py:240
  46.4 1.6 %collective-permute-done.8 = f16[32,3072]{1,0:T(8,128)(2,1)S(1)} collective-permute-done((f16[32,3072]{1,0:T(8,128)(2,1)S(1)}, f16[32,3072]{1,0:T(8,128)(2,1)S(1)}, u32[]{:S(2)}, u32[]{:S(2)}) %collective-permute-start.8) | collective-permute-done | bytes 196640 | tf_op jit(solution)/shard_map/plane_sum/ppermute | solution.py:240
  48.2 5.1 %collective-permute-start.10 = (f32[8,3072]{1,0:T(8,128)S(1)}, f32[8,3072]{1,0:T(8,128)S(1)}, u32[]{:S(2)}, u32[]{:S(2)}) collective-permute-start(f32[8,3072]{1,0:T(8,128)S(1)} %get-tuple-element.30), channel_id=1, source_target_pairs={{0,14},{2,0},{4,2},{6,4},{8,6},{10,8},{12,10},{14,12},{1,15},{3,1}... | collective-permute-start | bytes 294920 | tf_op jit(solution)/shard_map/depth_sum/ppermute | solution.py:232
  53.3 1.6 %collective-permute-done.10 = f32[8,3072]{1,0:T(8,128)S(1)} collective-permute-done((f32[8,3072]{1,0:T(8,128)S(1)}, f32[8,3072]{1,0:T(8,128)S(1)}, u32[]{:S(2)}, u32[]{:S(2)}) %collective-permute-start.10) | collective-permute-done | bytes 98336 | tf_op jit(solution)/shard_map/depth_sum/ppermute | solution.py:232
  55.0 4.5 %collective-permute-done.11 = f32[8,3072]{1,0:T(8,128)S(1)} collective-permute-done((f32[8,3072]{1,0:T(8,128)S(1)}, f32[8,3072]{1,0:T(8,128)S(1)}, u32[]{:S(2)}, u32[]{:S(2)}) %collective-permute-start.11) | collective-permute-done | bytes 98336 | tf_op jit(solution)/shard_map/depth_sum/ppermute | solution.py:232
  60.3 4.1 %collective-permute-start.12 = (f32[8,3072]{1,0:T(8,128)}, f32[8,3072]{1,0:T(8,128)}, u32[]{:S(2)}, u32[]{:S(2)}) collective-permute-start(f32[8,3072]{1,0:T(8,128)} %fusion.10), channel_id=1, source_target_pairs={{0,8},{8,0},{1,9},{9,1},{2,10},{10,2},{3,11},{11,3},{4,12},{12,4},... | collective-permute-start | bytes 294920 | tf_op jit(solution)/shard_map/depth_sum/ppermute | solution.py:267
  64.5 1.7 %multiply_reduce_fusion.1 = (f32[24576]{0:T(1024)S(1)}, f32[24576]{0:T(1024)S(1)}) fusion(f32[16,24576]{1,0:T(8,128)S(1)} %copy-done.1, s32[]{:T(128)S(6)} %select_n.29, f32[16,24576]{1,0:T(8,128)} %refs_1_.1), kind=kLoop, calls=%fused_computation.22 | loop fusion | flops 49152 | bytes 393220 | tf_op jit(solution)/shard_map/own_row/mul | solution.py:28
  66.6 1.4 %collective-permute-done.12 = f32[8,3072]{1,0:T(8,128)} collective-permute-done((f32[8,3072]{1,0:T(8,128)}, f32[8,3072]{1,0:T(8,128)}, u32[]{:S(2)}, u32[]{:S(2)}) %collective-permute-start.12) | collective-permute-done | bytes 98336 | tf_op jit(solution)/shard_map/depth_sum/ppermute | solution.py:267
  68.0 1.0 add.103
  69.0 4.9 %collective-permute-start.13 = (f32[8,3072]{1,0:T(8,128)S(1)}, f32[8,3072]{1,0:T(8,128)S(1)}, u32[]{:S(2)}, u32[]{:S(2)}) collective-permute-start(f32[8,3072]{1,0:T(8,128)S(1)} %add.103), channel_id=1, source_target_pairs={{0,1},{1,0},{2,3},{3,2},{4,5},{5,4},{6,7},{7,6},{8,9},{9,8},{10,11... | collective-permute-start | bytes 294920 | tf_op jit(solution)/shard_map/depth_sum/ppermute | solution.py:268
  73.9 0.9 collective-permute-done.13
  74.8 0.9 multiply_reduce_fusion
  76.6 3.4 %all-to-all-start = ((f16[4,4,6144]{2,1,0:T(4,128)(2,1)}), f16[4,4,6144]{2,1,0:T(4,128)(2,1)S(1)}, u32[]{:S(2)}, u32[]{:S(2)}) async-start(f16[4,4,6144]{2,1,0:T(4,128)(2,1)} %broadcast_in_dim.2), calls=%async_computation | async-start | bytes 393216 | tf_op jit(solution)/shard_map/depth_gather/all_to_all | solution.py:285
  79.9 1.4 %fusion.21 = (f16[4,3072]{1,0:T(4,128)(2,1)}, f16[4,3072]{1,0:T(4,128)(2,1)}) fusion(f16[4,6144]{1,0:T(4,128)(2,1)} %get-tuple-element.33), kind=kLoop, calls=%fused_computation.40 | loop fusion | bytes 98304 | tf_op jit(solution)/shard_map/plane_gather/slice | solution.py:291
  81.3 4.4 %all-to-all-done = f16[4,4,6144]{2,1,0:T(4,128)(2,1)S(1)} async-done(((f16[4,4,6144]{2,1,0:T(4,128)(2,1)}), f16[4,4,6144]{2,1,0:T(4,128)(2,1)S(1)}, u32[]{:S(2)}, u32[]{:S(2)}) %all-to-all-start) | async-done | bytes 196640 | tf_op jit(solution)/shard_map/depth_gather/all_to_all | solution.py:285
  86.7 28.4 %all-gather.1 = f16[640,3072]{1,0:T(8,128)(2,1)S(1)} all-gather(f16[40,3072]{1,0:T(8,128)(2,1)S(1)} %pad_maximum_fusion), channel_id=1, replica_groups=mesh['y'=4,'x'=4,'zh'=2,'zl'=4,'c'=2] {'y','x'}, dimensions={0}, use_global_device_ids=true | all-gather | bytes 4177920 | tf_op jit(solution)/shard_map/plane_gather/all_gather | solution.py:292
  116.2 5.1 %collective-permute-start.14 = (bf16[512,3072]{1,0:T(8,128)(2,1)S(1)}, bf16[512,3072]{1,0:T(8,128)(2,1)S(1)}, u32[]{:S(2)}, u32[]{:S(2)}) collective-permute-start(bf16[512,3072]{1,0:T(8,128)(2,1)S(1)} %bitcast.14), channel_id=1, source_target_pairs={{0,1},{1,0},{2,3},{3,2},{4,5},{5,4},{6,7},{7,6},{8,9},{9,8},{10,11... | collective-permute-start | bytes 9437192 | tf_op jit(solution)/shard_map/ppermute | solution.py:298
  121.4 3.9 %step.1 = (f32[16,24576]{1,0:T(8,128)}, f32[16,24576]{1,0:T(8,128)}, f32[16,24576]{1,0:T(8,128)}) custom-call(f32[128,3072]{1,0:T(8,128)S(1)} %fusion.g_ref, f32[16,24576]{1,0:T(8,128)S(1)} %copy-done, f32[16,24576]{1,0:T(8,128)S(1)} %copy-done.2, f32[16,24576]{1,0:T(8,128)S(1)} %copy-done.1), custom_call_target="tpu_custom_call" | custom-call | flops 7864320 | bytes 9437184 | tf_op jit(solution)/shard_map/step/pallas_call | solution.py:150
  125.3 1.2 collective-permute-done.14.other_ref
  126.6 4.3 %lay.1 = bf16[128,24576]{1,0:T(8,128)(2,1)} custom-call(s32[4]{0:T(128)S(1)} %pad_add_fusion.place_ref, bf16[512,3072]{1,0:T(8,128)(2,1)S(1)} %bitcast.15, bf16[512,3072]{1,0:T(8,128)(2,1)S(1)} %collective-permute-done.14.other_ref), custom_call_target="tpu_custom_call" | custom-call | flops 805306368 | bytes 6291456 | tf_op jit(solution)/shard_map/lay/pallas_call | solution.py:205
  (46 shorter events, 8.0 us)
Async XLA Ops:
  0.6 6.2 %copy-start.4 = (bf16[192,6144]{1,0:T(8,128)(2,1)S(1)}, bf16[192,6144]{1,0:T(8,128)(2,1)}, u32[]{:S(2)}) copy-start(bf16[192,6144]{1,0:T(8,128)(2,1)} %param.7) | copy-start | bytes 7077892
  3.6 9.4 %collective-permute-start.1 = (bf16[192,3072]{1,0:T(8,128)(2,1)}, bf16[192,3072]{1,0:T(8,128)(2,1)S(1)}, u32[]{:S(2)}, u32[]{:S(2)}) collective-permute-start(bf16[192,3072]{1,0:T(8,128)(2,1)} %get-tuple-element.24), channel_id=1, source_target_pairs={{0,1},{1,0},{2,3},{3,2},{4,5},{5,4},{6,7},{7,6},{8,9},{9,8},{10,11... | collective-permute-start | bytes 3538952 | tf_op jit(solution)/shard_map/pair/ppermute | solution.py:253
  8.0 5.1 %collective-permute-start.2 = (bf16[192,3072]{1,0:T(8,128)(2,1)}, bf16[192,3072]{1,0:T(8,128)(2,1)}, u32[]{:S(2)}, u32[]{:S(2)}) collective-permute-start(bf16[192,3072]{1,0:T(8,128)(2,1)} %get-tuple-element.22), channel_id=1, source_target_pairs={{0,1},{1,0},{2,3},{3,2},{4,5},{5,4},{6,7},{7,6},{8,9},{9,8},{10,11... | collective-permute-start | bytes 3538952 | tf_op jit(solution)/shard_map/pair/ppermute | solution.py:254
  8.1 0.9 copy-start.3
  10.2 2.8 %collective-permute-start = (bf16[512,192]{1,0:T(8,128)(2,1)S(1)}, bf16[512,192]{1,0:T(8,128)(2,1)S(1)}, u32[]{:S(2)}, u32[]{:S(2)}) collective-permute-start(bf16[512,192]{1,0:T(8,128)(2,1)S(1)} %get-tuple-element.10), channel_id=1, source_target_pairs={{0,1},{1,0},{2,3},{3,2},{4,5},{5,4},{6,7},{7,6},{8,9},{9,8},{10,11... | collective-permute-start | bytes 589832 | tf_op jit(solution)/shard_map/pair/ppermute | solution.py:252
  17.4 20.8 %collective-permute-start.3 = (f16[128,3072]{1,0:T(8,128)(2,1)S(1)}, f16[128,3072]{1,0:T(8,128)(2,1)S(1)}, u32[]{:S(2)}, u32[]{:S(2)}) collective-permute-start(f16[128,3072]{1,0:T(8,128)(2,1)S(1)} %get-tuple-element.18), channel_id=1, source_target_pairs={{0,16},{1,65},{16,32},{17,81},{32,48},{33,97},{48,0},{49,113},{64,... | collective-permute-start | bytes 2359304 | tf_op jit(solution)/shard_map/plane_sum/ppermute | solution.py:240
  17.5 20.8 %collective-permute-start.4 = (f16[128,3072]{1,0:T(8,128)(2,1)S(1)}, f16[128,3072]{1,0:T(8,128)(2,1)S(1)}, u32[]{:S(2)}, u32[]{:S(2)}) collective-permute-start(f16[128,3072]{1,0:T(8,128)(2,1)S(1)} %get-tuple-element.20), channel_id=1, source_target_pairs={{0,48},{1,193},{16,0},{17,209},{32,16},{33,225},{48,32},{49,241},{... | collective-permute-start | bytes 2359304 | tf_op jit(solution)/shard_map/plane_sum/ppermute | solution.py:240
  20.2 18.1 %collective-permute-start.5 = (f16[128,3072]{1,0:T(8,128)(2,1)S(1)}, f16[128,3072]{1,0:T(8,128)(2,1)S(1)}, u32[]{:S(2)}, u32[]{:S(2)}) collective-permute-start(f16[128,3072]{1,0:T(8,128)(2,1)S(1)} %get-tuple-element.19), channel_id=1, source_target_pairs={{0,32},{1,129},{16,48},{17,145},{32,0},{33,161},{48,16},{49,177},{... | collective-permute-start | bytes 2359304 | tf_op jit(solution)/shard_map/plane_sum/ppermute | solution.py:240
  38.8 25.6 %copy-start.1 = (f32[16,24576]{1,0:T(8,128)S(1)}, f32[16,24576]{1,0:T(8,128)}, u32[]{:S(2)}) copy-start(f32[16,24576]{1,0:T(8,128)} %refs_2_.1) | copy-start | bytes 4718596
  39.0 6.1 %collective-permute-start.6 = (f16[32,3072]{1,0:T(8,128)(2,1)S(1)}, f16[32,3072]{1,0:T(8,128)(2,1)S(1)}, u32[]{:S(2)}, u32[]{:S(2)}) collective-permute-start(f16[32,3072]{1,0:T(8,128)(2,1)S(1)} %get-tuple-element.25), channel_id=1, source_target_pairs={{0,64},{1,17},{16,80},{17,33},{32,96},{33,49},{48,112},{49,1},{64,... | collective-permute-start | bytes 589832 | tf_op jit(solution)/shard_map/plane_sum/ppermute | solution.py:240
  39.4 7.0 %collective-permute-start.7 = (f16[32,3072]{1,0:T(8,128)(2,1)S(1)}, f16[32,3072]{1,0:T(8,128)(2,1)S(1)}, u32[]{:S(2)}, u32[]{:S(2)}) collective-permute-start(f16[32,3072]{1,0:T(8,128)(2,1)S(1)} %get-tuple-element.27), channel_id=1, source_target_pairs={{0,192},{1,49},{16,208},{17,1},{32,224},{33,17},{48,240},{49,33},{... | collective-permute-start | bytes 589832 | tf_op jit(solution)/shard_map/plane_sum/ppermute | solution.py:240
  41.7 6.3 %collective-permute-start.8 = (f16[32,3072]{1,0:T(8,128)(2,1)S(1)}, f16[32,3072]{1,0:T(8,128)(2,1)S(1)}, u32[]{:S(2)}, u32[]{:S(2)}) collective-permute-start(f16[32,3072]{1,0:T(8,128)(2,1)S(1)} %get-tuple-element.26), channel_id=1, source_target_pairs={{0,128},{1,33},{16,144},{17,49},{32,160},{33,1},{48,176},{49,17},{... | collective-permute-start | bytes 589832 | tf_op jit(solution)/shard_map/plane_sum/ppermute | solution.py:240
  48.0 18.2 %copy-start = (f32[16,24576]{1,0:T(8,128)S(1)}, f32[16,24576]{1,0:T(8,128)}, u32[]{:S(2)}) copy-start(f32[16,24576]{1,0:T(8,128)} %refs_0_.1) | copy-start | bytes 4718596
  48.2 6.8 %collective-permute-start.10 = (f32[8,3072]{1,0:T(8,128)S(1)}, f32[8,3072]{1,0:T(8,128)S(1)}, u32[]{:S(2)}, u32[]{:S(2)}) collective-permute-start(f32[8,3072]{1,0:T(8,128)S(1)} %get-tuple-element.30), channel_id=1, source_target_pairs={{0,14},{2,0},{4,2},{6,4},{8,6},{10,8},{12,10},{14,12},{1,15},{3,1}... | collective-permute-start | bytes 294920 | tf_op jit(solution)/shard_map/depth_sum/ppermute | solution.py:232
  53.3 6.1 %collective-permute-start.11 = (f32[8,3072]{1,0:T(8,128)S(1)}, f32[8,3072]{1,0:T(8,128)S(1)}, u32[]{:S(2)}, u32[]{:S(2)}) collective-permute-start(f32[8,3072]{1,0:T(8,128)S(1)} %get-tuple-element.29), channel_id=1, source_target_pairs={{0,4},{2,6},{4,8},{6,10},{8,12},{10,14},{12,0},{14,2},{1,5},{3,7},... | collective-permute-start | bytes 294920 | tf_op jit(solution)/shard_map/depth_sum/ppermute | solution.py:232
  53.3 6.3 %collective-permute-start.9 = (f32[8,3072]{1,0:T(8,128)S(1)}, f32[8,3072]{1,0:T(8,128)S(1)}, u32[]{:S(2)}, u32[]{:S(2)}) collective-permute-start(f32[8,3072]{1,0:T(8,128)S(1)} %get-tuple-element.28), channel_id=1, source_target_pairs={{0,2},{2,4},{4,6},{6,8},{8,10},{10,12},{12,14},{14,0},{1,3},{3,5},... | collective-permute-start | bytes 294920 | tf_op jit(solution)/shard_map/depth_sum/ppermute | solution.py:232
  60.3 7.7 %collective-permute-start.12 = (f32[8,3072]{1,0:T(8,128)}, f32[8,3072]{1,0:T(8,128)}, u32[]{:S(2)}, u32[]{:S(2)}) collective-permute-start(f32[8,3072]{1,0:T(8,128)} %fusion.10), channel_id=1, source_target_pairs={{0,8},{8,0},{1,9},{9,1},{2,10},{10,2},{3,11},{11,3},{4,12},{12,4},... | collective-permute-start | bytes 294920 | tf_op jit(solution)/shard_map/depth_sum/ppermute | solution.py:267
  69.0 5.8 %collective-permute-start.13 = (f32[8,3072]{1,0:T(8,128)S(1)}, f32[8,3072]{1,0:T(8,128)S(1)}, u32[]{:S(2)}, u32[]{:S(2)}) collective-permute-start(f32[8,3072]{1,0:T(8,128)S(1)} %add.103), channel_id=1, source_target_pairs={{0,1},{1,0},{2,3},{3,2},{4,5},{5,4},{6,7},{7,6},{8,9},{9,8},{10,11... | collective-permute-start | bytes 294920 | tf_op jit(solution)/shard_map/depth_sum/ppermute | solution.py:268
  76.6 9.1 %all-to-all-start = ((f16[4,4,6144]{2,1,0:T(4,128)(2,1)}), f16[4,4,6144]{2,1,0:T(4,128)(2,1)S(1)}, u32[]{:S(2)}, u32[]{:S(2)}) async-start(f16[4,4,6144]{2,1,0:T(4,128)(2,1)} %broadcast_in_dim.2), calls=%async_computation | async-start | bytes 393216 | tf_op jit(solution)/shard_map/depth_gather/all_to_all | solution.py:285
  116.2 5.2 %copy-start.2 = (f32[16,24576]{1,0:T(8,128)S(1)}, f32[16,24576]{1,0:T(8,128)}, u32[]{:S(2)}) copy-start(f32[16,24576]{1,0:T(8,128)} %refs_1_.1) | copy-start | bytes 4718596
  116.2 10.4 %collective-permute-start.14 = (bf16[512,3072]{1,0:T(8,128)(2,1)S(1)}, bf16[512,3072]{1,0:T(8,128)(2,1)S(1)}, u32[]{:S(2)}, u32[]{:S(2)}) collective-permute-start(bf16[512,3072]{1,0:T(8,128)(2,1)S(1)} %bitcast.14), channel_id=1, source_target_pairs={{0,1},{1,0},{2,3},{3,2},{4,5},{5,4},{6,7},{7,6},{8,9},{9,8},{10,11... | collective-permute-start | bytes 9437192 | tf_op jit(solution)/shard_map/ppermute | solution.py:298

commit v5 on v4

--- a/solution.py
+++ b/solution.py
@@ -2,6 +2,7 @@
 
 import jax
 import jax.numpy as jnp
+import numpy as np
 from jax import lax
 from jax.experimental import pallas as pl
 from jax.experimental.pallas import tpu as pltpu
@@ -170,7 +171,8 @@
     parts, half = own_ref.shape[0] // 2, own_ref.shape[1]
     m = lax.broadcasted_iota(jnp.int32, (parts, parts), 0)
     n = lax.broadcasted_iota(jnp.int32, (parts, parts), 1)
-    wanted = n == (m & 15) * 16 + ((m >> 4) & 3) * 4 + (m >> 6)
+    ahead = ((m >> 4) - place_ref[1]) & 3
+    wanted = n == (m & 15) * 16 + ahead * 4 + (m >> 6)
     pick = jnp.where(wanted, 1.0 / UNIT_SCALE, 0.0).astype(jnp.bfloat16)
 
     def leaving(j, k):
@@ -279,17 +281,18 @@
 
         stepped, _, _ = adam_update(gradient, piece(master), piece(moment), piece(second))
         scale = jnp.sqrt(jnp.sum(stepped * stepped, axis=1, keepdims=True) + 1e-06)
-        unit = lax.reduce_precision(stepped / scale, 8, 7)
-        unit = (unit * UNIT_SCALE).astype(jnp.float16)
+        unit = (stepped / scale).astype(jnp.bfloat16)
+        unit, small = (
+            jnp.concatenate([a[:, :half], a[:, half:]], axis=0) for a in (unit, gradient)
+        )
     with jax.named_scope("depth_gather"):
-        units = lax.all_to_all(
-            jnp.broadcast_to(unit[None], (NZL, PROJ, width)), "zl", 0, 0, tiled=True
-        )
+        units = [unit, ahead(unit, 7), ahead(unit, 2), ahead(unit, 1)]
     with jax.named_scope("plane_gather"):
-        units = units.reshape(NZL * PROJ, width)
-        small = gradient.astype(jnp.float16)
-        halves = [a[:, n * half : (n + 1) * half] for a in (units, small) for n in range(2)]
-        came = lax.all_gather(jnp.concatenate(halves, axis=0), ("y", "x"), axis=0, tiled=True)
+        order = np.arange(2 * NZL * PROJ).reshape(NZL, 2, PROJ).swapaxes(0, 1).reshape(-1)
+        turn = jnp.asarray(np.eye(2 * NZL * PROJ)[order] * UNIT_SCALE, jnp.bfloat16)
+        units = jnp.dot(turn, jnp.concatenate(units, axis=0), preferred_element_type=jnp.float32)
+        payload = jnp.concatenate([units, small], axis=0).astype(jnp.float16)
+        came = lax.all_gather(payload, ("y", "x"), axis=0, tiled=True)
         came = came.reshape(PLANE, 2 * (NZL + 1) * PROJ, half)
         grads = came[:, 2 * NZL * PROJ :].astype(jnp.float32).reshape(2 * PLANE * PROJ, half)
         own = came[:, : 2 * NZL * PROJ].astype(jnp.bfloat16)

time: 132 us -> 127 us (0.962)
  local copies, waits for them, and re-layouts: 8.55 us -> 6.4 us
  waiting for transfers between devices: 34.8 us -> 33.1 us
  other arithmetic: 7.24 us -> 5.89 us
    all_to_all x1 -> x0, waiting for transfers between devices: 4.37 us -> none  [shards(): lax.all_to_all(jnp.broadcast_to(unit[None], (NZL, PROJ, width)), 'zl', 0,...]
    all_to_all x1 -> x0, starting transfers between devices: 3.37 us -> none  [shards(): lax.all_to_all(jnp.broadcast_to(unit[None], (NZL, PROJ, width)), 'zl', 0,...]
    ppermute x3 -> x6, starting transfers between devices: 5.15 us -> 8.14 us  [ahead(): lax.ppermute(a, ('zh', 'zl'), [(z, (z + by) % ring) for z in range(ring)])]
    ppermute x3 -> x6, waiting for transfers between devices: 6.3 us -> 9.01 us  [ahead(): lax.ppermute(a, ('zh', 'zl'), [(z, (z + by) % ring) for z in range(ring)])]
    slice x2, local copies, waits for them, and re-layouts: 1.43 us -> 0.04 us  [shards(): a[:, :half]]
  transfers between devices with their start and end apart: 16 -> 18, of which waited for: 11 -> 12; matrix products, arithmetic and copies ran while one was open for 4% -> 3% of each run, Pallas kernels for 8% -> 8%
where the time goes in v5:
time: 127 us
  waiting for transfers between devices  33.1 us (26%)
  starting transfers between devices  32.4 us (26%)
  blocking collectives  28.5 us (22%)
  Pallas kernels  18.3 us (14%)
  local copies, waits for them, and re-layouts  6.4 us (5%)
  other arithmetic  5.89 us (5%)
    all_gather x1, blocking collectives, shards(): came = lax.all_gather(payload, ('y', 'x'), axis=0, tiled=True)  28.5 us
    ppermute x6, waiting for transfers between devices, onward(): return lax.ppermute(a, ('y', 'x', 'c'), pairs)  20.5 us
    ppermute x6, waiting for transfers between devices, ahead(): lax.ppermute(a, ('zh', 'zl'), [(z, (z + by) % ring) for z in range(ring)])  9.01 us
    pallas_call x3, Pallas kernels, terms(): pl.pallas_call(functools.partial(terms_kernel, rows, len(sides), tile), i...  8.91 us
    ppermute x6, starting transfers between devices, ahead(): lax.ppermute(a, ('zh', 'zl'), [(z, (z + by) % ring) for z in range(ring)])  8.14 us
    ppermute x6, starting transfers between devices, onward(): return lax.ppermute(a, ('y', 'x', 'c'), pairs)  6.24 us
    ppermute x1, starting transfers between devices, shards(): other = lax.ppermute(own, 'c', swap)  5.15 us
    ppermute x1, starting transfers between devices, shards(): came = lax.ppermute(part, 'c', swap)  4.89 us
  transfers between devices with their start and end apart: 18, of which 12 were waited for; matrix products, arithmetic and copies ran while one was open for 3% of the time, Pallas kernels for 8%

profile of v5, /device:TPU:1, one launch (start us, length us, event | category | flops | bytes accessed | tf_op | source)
XLA Modules:
  0.0 126.7 jit_solution(12100677104454782956)
XLA Ops:
  0.6 2.9 %constant_dynamic-slice_fusion.3 = (bf16[192,3072]{1,0:T(8,128)(2,1)S(1)}, bf16[192,3072]{1,0:T(8,128)(2,1)}) fusion(bf16[192,6144]{1,0:T(8,128)(2,1)} %param.7, s32[]{:T(128)S(6)} %select_n.27, s32[]{:T(128)S(6)} %select_n.28), kind=kLoop, calls=%fused_computation.36 | loop fusion | bytes 4718600 | tf_op jit(solution)/shard_map/pair/dynamic_slice | solution.py:250
  3.6 3.2 %collective-permute-start.1 = (bf16[192,3072]{1,0:T(8,128)(2,1)}, bf16[192,3072]{1,0:T(8,128)(2,1)S(1)}, u32[]{:S(2)}, u32[]{:S(2)}) collective-permute-start(bf16[192,3072]{1,0:T(8,128)(2,1)} %get-tuple-element.24), channel_id=1, source_target_pairs={{0,1},{1,0},{2,3},{3,2},{4,5},{5,4},{6,7},{7,6},{8,9},{9,8},{10,11... | collective-permute-start | bytes 3538952 | tf_op jit(solution)/shard_map/pair/ppermute | solution.py:255
  6.8 1.2 constant_dynamic-slice_fusion.2
  8.1 0.9 copy-done.3
  9.0 1.2 lefts.1
  10.8 2.2 %terms.4.refs_3_ = f32[384,3072]{1,0:T(8,128)S(1)} custom-call(bf16[512,192]{1,0:T(8,128)(2,1)S(1)} %get-tuple-element.9.refs_0_, bf16[192,3072]{1,0:T(8,128)(2,1)S(1)} %get-tuple-element.23.refs_1_, bf16[192,3072]{1,0:T(8,128)(2,1)S(1)} %get-tuple-element.21.refs_2_), custom_call_target="tpu_custom_call" | custom-call | flops 905969664 | bytes 4718592 | tf_op jit(solution)/shard_map/pair/terms/pallas_call | solution.py:93
  13.1 3.5 %terms.5 = f32[384,3072]{1,0:T(8,128)S(1)} custom-call(bf16[512,192]{1,0:T(8,128)(2,1)S(1)} %collective-permute-done.refs_3_.refs_0_, bf16[192,3072]{1,0:T(8,128)(2,1)S(1)} %collective-permute-done.1.refs_4_.refs_1_, bf16[192,3072]{1,0:T(8,128)(2,1)} %collective-permute-done.2.refs_5_.refs_2_, f32[384,3072]{1,0:T(8,128)S(1)} %terms.4.refs_3_), custom_call_target="tpu_custom_call" | custom-call | flops 905969664 | bytes 4718592 | tf_op jit(solution)/shard_map/pair/terms/pallas_call | solution.py:93
  17.5 2.7 %collective-permute-start.4 = (f16[128,3072]{1,0:T(8,128)(2,1)S(1)}, f16[128,3072]{1,0:T(8,128)(2,1)S(1)}, u32[]{:S(2)}, u32[]{:S(2)}) collective-permute-start(f16[128,3072]{1,0:T(8,128)(2,1)S(1)} %get-tuple-element.20), channel_id=1, source_target_pairs={{0,48},{1,193},{16,0},{17,209},{32,16},{33,225},{48,32},{49,241},{... | collective-permute-start | bytes 2359304 | tf_op jit(solution)/shard_map/plane_sum/ppermute | solution.py:242
  20.2 3.1 %terms.3 = f32[128,3072]{1,0:T(8,128)S(1)} custom-call(bf16[512,192]{1,0:T(8,128)(2,1)S(1)} %get-tuple-element.9.refs_0_, bf16[192,3072]{1,0:T(8,128)(2,1)S(1)} %get-tuple-element.23.refs_1_, bf16[192,3072]{1,0:T(8,128)(2,1)S(1)} %get-tuple-element.21.refs_2_, bf16[512,192]{1,0:T(8,128)(2,1)S(1)} %collective-permute-done.refs_3_.refs_0_, ...), custom_call_target="tpu_custom_call" | custom-call | flops 603979776 | bytes 4718592 | tf_op jit(solution)/shard_map/plane_sum/terms/pallas_call | solution.py:93
  23.4 14.9 %collective-permute-done.3 = f16[128,3072]{1,0:T(8,128)(2,1)S(1)} collective-permute-done((f16[128,3072]{1,0:T(8,128)(2,1)S(1)}, f16[128,3072]{1,0:T(8,128)(2,1)S(1)}, u32[]{:S(2)}, u32[]{:S(2)}) %collective-permute-start.3) | collective-permute-done | bytes 786464 | tf_op jit(solution)/shard_map/plane_sum/ppermute | solution.py:242
  39.4 2.3 %collective-permute-start.7 = (f16[32,3072]{1,0:T(8,128)(2,1)S(1)}, f16[32,3072]{1,0:T(8,128)(2,1)S(1)}, u32[]{:S(2)}, u32[]{:S(2)}) collective-permute-start(f16[32,3072]{1,0:T(8,128)(2,1)S(1)} %get-tuple-element.27), channel_id=1, source_target_pairs={{0,192},{1,49},{16,208},{17,1},{32,224},{33,17},{48,240},{49,33},{... | collective-permute-start | bytes 589832 | tf_op jit(solution)/shard_map/plane_sum/ppermute | solution.py:242
  42.4 2.6 %collective-permute-done.6 = f16[32,3072]{1,0:T(8,128)(2,1)S(1)} collective-permute-done((f16[32,3072]{1,0:T(8,128)(2,1)S(1)}, f16[32,3072]{1,0:T(8,128)(2,1)S(1)}, u32[]{:S(2)}, u32[]{:S(2)}) %collective-permute-start.6) | collective-permute-done | bytes 196640 | tf_op jit(solution)/shard_map/plane_sum/ppermute | solution.py:242
  45.1 1.4 %collective-permute-done.7 = f16[32,3072]{1,0:T(8,128)(2,1)S(1)} collective-permute-done((f16[32,3072]{1,0:T(8,128)(2,1)S(1)}, f16[32,3072]{1,0:T(8,128)(2,1)S(1)}, u32[]{:S(2)}, u32[]{:S(2)}) %collective-permute-start.7) | collective-permute-done | bytes 196640 | tf_op jit(solution)/shard_map/plane_sum/ppermute | solution.py:242
  46.4 1.6 %collective-permute-done.8 = f16[32,3072]{1,0:T(8,128)(2,1)S(1)} collective-permute-done((f16[32,3072]{1,0:T(8,128)(2,1)S(1)}, f16[32,3072]{1,0:T(8,128)(2,1)S(1)}, u32[]{:S(2)}, u32[]{:S(2)}) %collective-permute-start.8) | collective-permute-done | bytes 196640 | tf_op jit(solution)/shard_map/plane_sum/ppermute | solution.py:242
  48.2 5.1 %collective-permute-start.10 = (f32[8,3072]{1,0:T(8,128)S(1)}, f32[8,3072]{1,0:T(8,128)S(1)}, u32[]{:S(2)}, u32[]{:S(2)}) collective-permute-start(f32[8,3072]{1,0:T(8,128)S(1)} %get-tuple-element.30), channel_id=1, source_target_pairs={{0,14},{2,0},{4,2},{6,4},{8,6},{10,8},{12,10},{14,12},{1,15},{3,1}... | collective-permute-start | bytes 294920 | tf_op jit(solution)/shard_map/depth_sum/ppermute | solution.py:234
  53.3 1.6 %collective-permute-done.10 = f32[8,3072]{1,0:T(8,128)S(1)} collective-permute-done((f32[8,3072]{1,0:T(8,128)S(1)}, f32[8,3072]{1,0:T(8,128)S(1)}, u32[]{:S(2)}, u32[]{:S(2)}) %collective-permute-start.10) | collective-permute-done | bytes 98336 | tf_op jit(solution)/shard_map/depth_sum/ppermute | solution.py:234
  55.0 4.5 %collective-permute-done.11 = f32[8,3072]{1,0:T(8,128)S(1)} collective-permute-done((f32[8,3072]{1,0:T(8,128)S(1)}, f32[8,3072]{1,0:T(8,128)S(1)}, u32[]{:S(2)}, u32[]{:S(2)}) %collective-permute-start.11) | collective-permute-done | bytes 98336 | tf_op jit(solution)/shard_map/depth_sum/ppermute | solution.py:234
  60.3 4.1 %collective-permute-start.12 = (f32[8,3072]{1,0:T(8,128)}, f32[8,3072]{1,0:T(8,128)}, u32[]{:S(2)}, u32[]{:S(2)}) collective-permute-start(f32[8,3072]{1,0:T(8,128)} %fusion.14), channel_id=1, source_target_pairs={{0,8},{8,0},{1,9},{9,1},{2,10},{10,2},{3,11},{11,3},{4,12},{12,4},... | collective-permute-start | bytes 294920 | tf_op jit(solution)/shard_map/depth_sum/ppermute | solution.py:269
  64.5 1.7 %multiply_reduce_fusion.1 = (f32[24576]{0:T(1024)S(1)}, f32[24576]{0:T(1024)S(1)}) fusion(f32[16,24576]{1,0:T(8,128)S(1)} %copy-done.1, s32[]{:T(128)S(6)} %select_n.25, f32[16,24576]{1,0:T(8,128)} %refs_1_.1), kind=kLoop, calls=%fused_computation.27 | loop fusion | flops 49152 | bytes 393220 | tf_op jit(solution)/shard_map/own_row/mul | solution.py:29
  66.6 1.4 %collective-permute-done.12 = f32[8,3072]{1,0:T(8,128)} collective-permute-done((f32[8,3072]{1,0:T(8,128)}, f32[8,3072]{1,0:T(8,128)}, u32[]{:S(2)}, u32[]{:S(2)}) %collective-permute-start.12) | collective-permute-done | bytes 98336 | tf_op jit(solution)/shard_map/depth_sum/ppermute | solution.py:269
  68.0 1.0 add.91
  69.0 4.9 %collective-permute-start.13 = (f32[8,3072]{1,0:T(8,128)S(1)}, f32[8,3072]{1,0:T(8,128)S(1)}, u32[]{:S(2)}, u32[]{:S(2)}) collective-permute-start(f32[8,3072]{1,0:T(8,128)S(1)} %add.91), channel_id=1, source_target_pairs={{0,1},{1,0},{2,3},{3,2},{4,5},{5,4},{6,7},{7,6},{8,9},{9,8},{10,11... | collective-permute-start | bytes 294920 | tf_op jit(solution)/shard_map/depth_sum/ppermute | solution.py:270
  73.9 0.9 collective-permute-done.13
  76.0 2.3 %collective-permute-start.14 = (bf16[8,3072]{1,0:T(8,128)(2,1)S(1)}, bf16[8,3072]{1,0:T(8,128)(2,1)S(1)}, u32[]{:S(2)}, u32[]{:S(2)}) collective-permute-start(bf16[8,3072]{1,0:T(8,128)(2,1)S(1)} %pad_maximum_fusion.1), channel_id=1, source_target_pairs={{0,14},{2,0},{4,2},{6,4},{8,6},{10,8},{12,10},{14,12},{1,15},{3,1}... | collective-permute-start | bytes 147464 | tf_op jit(solution)/shard_map/depth_gather/ppermute | solution.py:234
  78.7 1.8 %collective-permute-done.15 = bf16[8,3072]{1,0:T(8,128)(2,1)S(1)} collective-permute-done((bf16[8,3072]{1,0:T(8,128)(2,1)S(1)}, bf16[8,3072]{1,0:T(8,128)(2,1)S(1)}, u32[]{:S(2)}, u32[]{:S(2)}) %collective-permute-start.15) | collective-permute-done | bytes 49184 | tf_op jit(solution)/shard_map/depth_gather/ppermute | solution.py:234
  80.7 0.9 collective-permute-done.16
  82.1 28.5 %all-gather.1 = f16[640,3072]{1,0:T(8,128)(2,1)S(1)} all-gather(f16[40,3072]{1,0:T(8,128)(2,1)S(1)} %pad_maximum_fusion), channel_id=1, replica_groups=mesh['y'=4,'x'=4,'zh'=2,'zl'=4,'c'=2] {'y','x'}, dimensions={0}, use_global_device_ids=true | all-gather | bytes 4177920 | tf_op jit(solution)/shard_map/plane_gather/all_gather | solution.py:295
  110.6 0.8 slice_convert_fusion
  111.7 5.1 %collective-permute-start.17 = (bf16[512,3072]{1,0:T(8,128)(2,1)S(1)}, bf16[512,3072]{1,0:T(8,128)(2,1)S(1)}, u32[]{:S(2)}, u32[]{:S(2)}) collective-permute-start(bf16[512,3072]{1,0:T(8,128)(2,1)S(1)} %bitcast.24), channel_id=1, source_target_pairs={{0,1},{1,0},{2,3},{3,2},{4,5},{5,4},{6,7},{7,6},{8,9},{9,8},{10,11... | collective-permute-start | bytes 9437192 | tf_op jit(solution)/shard_map/ppermute | solution.py:301
  117.0 3.9 %step.1 = (f32[16,24576]{1,0:T(8,128)}, f32[16,24576]{1,0:T(8,128)}, f32[16,24576]{1,0:T(8,128)}) custom-call(f32[128,3072]{1,0:T(8,128)S(1)} %fusion.4.g_ref, f32[16,24576]{1,0:T(8,128)S(1)} %copy-done, f32[16,24576]{1,0:T(8,128)S(1)} %copy-done.2, f32[16,24576]{1,0:T(8,128)S(1)} %copy-done.1), custom_call_target="tpu_custom_call" | custom-call | flops 7864320 | bytes 9437184 | tf_op jit(solution)/shard_map/step/pallas_call | solution.py:151
  120.9 1.2 collective-permute-done.17.other_ref
  122.2 4.3 %lay.1 = bf16[128,24576]{1,0:T(8,128)(2,1)} custom-call(s32[4]{0:T(128)S(1)} %pad_add_fusion.place_ref, bf16[512,3072]{1,0:T(8,128)(2,1)S(1)} %bitcast.25, bf16[512,3072]{1,0:T(8,128)(2,1)S(1)} %collective-permute-done.17.other_ref), custom_call_target="tpu_custom_call" | custom-call | flops 805306368 | bytes 6291456 | tf_op jit(solution)/shard_map/lay/pallas_call | solution.py:207
  (64 shorter events, 7.5 us)
Async XLA Ops:
  0.6 6.2 %copy-start.4 = (bf16[192,6144]{1,0:T(8,128)(2,1)S(1)}, bf16[192,6144]{1,0:T(8,128)(2,1)}, u32[]{:S(2)}) copy-start(bf16[192,6144]{1,0:T(8,128)(2,1)} %param.8) | copy-start | bytes 7077892
  3.6 9.4 %collective-permute-start.1 = (bf16[192,3072]{1,0:T(8,128)(2,1)}, bf16[192,3072]{1,0:T(8,128)(2,1)S(1)}, u32[]{:S(2)}, u32[]{:S(2)}) collective-permute-start(bf16[192,3072]{1,0:T(8,128)(2,1)} %get-tuple-element.24), channel_id=1, source_target_pairs={{0,1},{1,0},{2,3},{3,2},{4,5},{5,4},{6,7},{7,6},{8,9},{9,8},{10,11... | collective-permute-start | bytes 3538952 | tf_op jit(solution)/shard_map/pair/ppermute | solution.py:255
  8.0 5.1 %collective-permute-start.2 = (bf16[192,3072]{1,0:T(8,128)(2,1)}, bf16[192,3072]{1,0:T(8,128)(2,1)}, u32[]{:S(2)}, u32[]{:S(2)}) collective-permute-start(bf16[192,3072]{1,0:T(8,128)(2,1)} %get-tuple-element.22), channel_id=1, source_target_pairs={{0,1},{1,0},{2,3},{3,2},{4,5},{5,4},{6,7},{7,6},{8,9},{9,8},{10,11... | collective-permute-start | bytes 3538952 | tf_op jit(solution)/shard_map/pair/ppermute | solution.py:256
  8.1 0.9 copy-start.3
  10.2 2.8 %collective-permute-start = (bf16[512,192]{1,0:T(8,128)(2,1)S(1)}, bf16[512,192]{1,0:T(8,128)(2,1)S(1)}, u32[]{:S(2)}, u32[]{:S(2)}) collective-permute-start(bf16[512,192]{1,0:T(8,128)(2,1)S(1)} %get-tuple-element.10), channel_id=1, source_target_pairs={{0,1},{1,0},{2,3},{3,2},{4,5},{5,4},{6,7},{7,6},{8,9},{9,8},{10,11... | collective-permute-start | bytes 589832 | tf_op jit(solution)/shard_map/pair/ppermute | solution.py:254
  17.4 20.8 %collective-permute-start.3 = (f16[128,3072]{1,0:T(8,128)(2,1)S(1)}, f16[128,3072]{1,0:T(8,128)(2,1)S(1)}, u32[]{:S(2)}, u32[]{:S(2)}) collective-permute-start(f16[128,3072]{1,0:T(8,128)(2,1)S(1)} %get-tuple-element.18), channel_id=1, source_target_pairs={{0,16},{1,65},{16,32},{17,81},{32,48},{33,97},{48,0},{49,113},{64,... | collective-permute-start | bytes 2359304 | tf_op jit(solution)/shard_map/plane_sum/ppermute | solution.py:242
  17.5 20.8 %collective-permute-start.4 = (f16[128,3072]{1,0:T(8,128)(2,1)S(1)}, f16[128,3072]{1,0:T(8,128)(2,1)S(1)}, u32[]{:S(2)}, u32[]{:S(2)}) collective-permute-start(f16[128,3072]{1,0:T(8,128)(2,1)S(1)} %get-tuple-element.20), channel_id=1, source_target_pairs={{0,48},{1,193},{16,0},{17,209},{32,16},{33,225},{48,32},{49,241},{... | collective-permute-start | bytes 2359304 | tf_op jit(solution)/shard_map/plane_sum/ppermute | solution.py:242
  20.2 18.1 %collective-permute-start.5 = (f16[128,3072]{1,0:T(8,128)(2,1)S(1)}, f16[128,3072]{1,0:T(8,128)(2,1)S(1)}, u32[]{:S(2)}, u32[]{:S(2)}) collective-permute-start(f16[128,3072]{1,0:T(8,128)(2,1)S(1)} %get-tuple-element.19), channel_id=1, source_target_pairs={{0,32},{1,129},{16,48},{17,145},{32,0},{33,161},{48,16},{49,177},{... | collective-permute-start | bytes 2359304 | tf_op jit(solution)/shard_map/plane_sum/ppermute | solution.py:242
  38.8 25.6 %copy-start.1 = (f32[16,24576]{1,0:T(8,128)S(1)}, f32[16,24576]{1,0:T(8,128)}, u32[]{:S(2)}) copy-start(f32[16,24576]{1,0:T(8,128)} %refs_2_.1) | copy-start | bytes 4718596
  39.0 6.1 %collective-permute-start.6 = (f16[32,3072]{1,0:T(8,128)(2,1)S(1)}, f16[32,3072]{1,0:T(8,128)(2,1)S(1)}, u32[]{:S(2)}, u32[]{:S(2)}) collective-permute-start(f16[32,3072]{1,0:T(8,128)(2,1)S(1)} %get-tuple-element.25), channel_id=1, source_target_pairs={{0,64},{1,17},{16,80},{17,33},{32,96},{33,49},{48,112},{49,1},{64,... | collective-permute-start | bytes 589832 | tf_op jit(solution)/shard_map/plane_sum/ppermute | solution.py:242
  39.4 7.0 %collective-permute-start.7 = (f16[32,3072]{1,0:T(8,128)(2,1)S(1)}, f16[32,3072]{1,0:T(8,128)(2,1)S(1)}, u32[]{:S(2)}, u32[]{:S(2)}) collective-permute-start(f16[32,3072]{1,0:T(8,128)(2,1)S(1)} %get-tuple-element.27), channel_id=1, source_target_pairs={{0,192},{1,49},{16,208},{17,1},{32,224},{33,17},{48,240},{49,33},{... | collective-permute-start | bytes 589832 | tf_op jit(solution)/shard_map/plane_sum/ppermute | solution.py:242
  41.7 6.3 %collective-permute-start.8 = (f16[32,3072]{1,0:T(8,128)(2,1)S(1)}, f16[32,3072]{1,0:T(8,128)(2,1)S(1)}, u32[]{:S(2)}, u32[]{:S(2)}) collective-permute-start(f16[32,3072]{1,0:T(8,128)(2,1)S(1)} %get-tuple-element.26), channel_id=1, source_target_pairs={{0,128},{1,33},{16,144},{17,49},{32,160},{33,1},{48,176},{49,17},{... | collective-permute-start | bytes 589832 | tf_op jit(solution)/shard_map/plane_sum/ppermute | solution.py:242
  48.0 18.2 %copy-start = (f32[16,24576]{1,0:T(8,128)S(1)}, f32[16,24576]{1,0:T(8,128)}, u32[]{:S(2)}) copy-start(f32[16,24576]{1,0:T(8,128)} %refs_0_.1) | copy-start | bytes 4718596
  48.2 6.8 %collective-permute-start.10 = (f32[8,3072]{1,0:T(8,128)S(1)}, f32[8,3072]{1,0:T(8,128)S(1)}, u32[]{:S(2)}, u32[]{:S(2)}) collective-permute-start(f32[8,3072]{1,0:T(8,128)S(1)} %get-tuple-element.30), channel_id=1, source_target_pairs={{0,14},{2,0},{4,2},{6,4},{8,6},{10,8},{12,10},{14,12},{1,15},{3,1}... | collective-permute-start | bytes 294920 | tf_op jit(solution)/shard_map/depth_sum/ppermute | solution.py:234
  53.3 6.1 %collective-permute-start.11 = (f32[8,3072]{1,0:T(8,128)S(1)}, f32[8,3072]{1,0:T(8,128)S(1)}, u32[]{:S(2)}, u32[]{:S(2)}) collective-permute-start(f32[8,3072]{1,0:T(8,128)S(1)} %get-tuple-element.29), channel_id=1, source_target_pairs={{0,4},{2,6},{4,8},{6,10},{8,12},{10,14},{12,0},{14,2},{1,5},{3,7},... | collective-permute-start | bytes 294920 | tf_op jit(solution)/shard_map/depth_sum/ppermute | solution.py:234
  53.3 6.3 %collective-permute-start.9 = (f32[8,3072]{1,0:T(8,128)S(1)}, f32[8,3072]{1,0:T(8,128)S(1)}, u32[]{:S(2)}, u32[]{:S(2)}) collective-permute-start(f32[8,3072]{1,0:T(8,128)S(1)} %get-tuple-element.28), channel_id=1, source_target_pairs={{0,2},{2,4},{4,6},{6,8},{8,10},{10,12},{12,14},{14,0},{1,3},{3,5},... | collective-permute-start | bytes 294920 | tf_op jit(solution)/shard_map/depth_sum/ppermute | solution.py:234
  60.3 7.7 %collective-permute-start.12 = (f32[8,3072]{1,0:T(8,128)}, f32[8,3072]{1,0:T(8,128)}, u32[]{:S(2)}, u32[]{:S(2)}) collective-permute-start(f32[8,3072]{1,0:T(8,128)} %fusion.14), channel_id=1, source_target_pairs={{0,8},{8,0},{1,9},{9,1},{2,10},{10,2},{3,11},{11,3},{4,12},{12,4},... | collective-permute-start | bytes 294920 | tf_op jit(solution)/shard_map/depth_sum/ppermute | solution.py:269
  66.5 14.0 %copy-start.7 = (bf16[32,8]{1,0:T(8,128)(2,1)S(1)}, bf16[32,8]{1,0:T(8,128)(2,1)}, u32[]{:S(2)}) copy-start(bf16[32,8]{1,0:T(8,128)(2,1)} %constant.62) | copy-start | bytes 1540
  66.6 11.7 %copy-start.9 = (bf16[32,4]{1,0:T(8,128)(2,1)S(1)}, bf16[32,4]{1,0:T(8,128)(2,1)}, u32[]{:S(2)}) copy-start(bf16[32,4]{1,0:T(8,128)(2,1)} %constant.59) | copy-start | bytes 772
  66.6 11.9 %copy-start.8 = (bf16[32,4]{1,0:T(8,128)(2,1)S(1)}, bf16[32,4]{1,0:T(8,128)(2,1)}, u32[]{:S(2)}) copy-start(bf16[32,4]{1,0:T(8,128)(2,1)} %constant.60) | copy-start | bytes 772
  69.0 12.7 %copy-start.6 = (bf16[32,8]{1,0:T(8,128)(2,1)S(1)}, bf16[32,8]{1,0:T(8,128)(2,1)}, u32[]{:S(2)}) copy-start(bf16[32,8]{1,0:T(8,128)(2,1)} %constant.63) | copy-start | bytes 1540
  69.0 5.8 %collective-permute-start.13 = (f32[8,3072]{1,0:T(8,128)S(1)}, f32[8,3072]{1,0:T(8,128)S(1)}, u32[]{:S(2)}, u32[]{:S(2)}) collective-permute-start(f32[8,3072]{1,0:T(8,128)S(1)} %add.91), channel_id=1, source_target_pairs={{0,1},{1,0},{2,3},{3,2},{4,5},{5,4},{6,7},{7,6},{8,9},{9,8},{10,11... | collective-permute-start | bytes 294920 | tf_op jit(solution)/shard_map/depth_sum/ppermute | solution.py:270
  74.8 7.0 %copy-start.5 = (bf16[32,8]{1,0:T(8,128)(2,1)S(1)}, bf16[32,8]{1,0:T(8,128)(2,1)}, u32[]{:S(2)}) copy-start(bf16[32,8]{1,0:T(8,128)(2,1)} %constant.61) | copy-start | bytes 1540
  75.3 5.2 %collective-permute-start.15 = (bf16[8,3072]{1,0:T(8,128)(2,1)S(1)}, bf16[8,3072]{1,0:T(8,128)(2,1)S(1)}, u32[]{:S(2)}, u32[]{:S(2)}) collective-permute-start(bf16[8,3072]{1,0:T(8,128)(2,1)S(1)} %pad_maximum_fusion.1), channel_id=1, source_target_pairs={{0,4},{2,6},{4,8},{6,10},{8,12},{10,14},{12,0},{14,2},{1,5},{3,7},... | collective-permute-start | bytes 147464 | tf_op jit(solution)/shard_map/depth_gather/ppermute | solution.py:234
  75.4 6.2 %collective-permute-start.16 = (bf16[8,3072]{1,0:T(8,128)(2,1)S(1)}, bf16[8,3072]{1,0:T(8,128)(2,1)S(1)}, u32[]{:S(2)}, u32[]{:S(2)}) collective-permute-start(bf16[8,3072]{1,0:T(8,128)(2,1)S(1)} %pad_maximum_fusion.1), channel_id=1, source_target_pairs={{0,2},{2,4},{4,6},{6,8},{8,10},{10,12},{12,14},{14,0},{1,3},{3,5},... | collective-permute-start | bytes 147464 | tf_op jit(solution)/shard_map/depth_gather/ppermute | solution.py:234
  76.0 5.8 %collective-permute-start.14 = (bf16[8,3072]{1,0:T(8,128)(2,1)S(1)}, bf16[8,3072]{1,0:T(8,128)(2,1)S(1)}, u32[]{:S(2)}, u32[]{:S(2)}) collective-permute-start(bf16[8,3072]{1,0:T(8,128)(2,1)S(1)} %pad_maximum_fusion.1), channel_id=1, source_target_pairs={{0,14},{2,0},{4,2},{6,4},{8,6},{10,8},{12,10},{14,12},{1,15},{3,1}... | collective-permute-start | bytes 147464 | tf_op jit(solution)/shard_map/depth_gather/ppermute | solution.py:234
  111.7 5.3 %copy-start.2 = (f32[16,24576]{1,0:T(8,128)S(1)}, f32[16,24576]{1,0:T(8,128)}, u32[]{:S(2)}) copy-start(f32[16,24576]{1,0:T(8,128)} %refs_1_.1) | copy-start | bytes 4718596
  111.7 10.4 %collective-permute-start.17 = (bf16[512,3072]{1,0:T(8,128)(2,1)S(1)}, bf16[512,3072]{1,0:T(8,128)(2,1)S(1)}, u32[]{:S(2)}, u32[]{:S(2)}) collective-permute-start(bf16[512,3072]{1,0:T(8,128)(2,1)S(1)} %bitcast.24), channel_id=1, source_target_pairs={{0,1},{1,0},{2,3},{3,2},{4,5},{5,4},{6,7},{7,6},{8,9},{9,8},{10,11... | collective-permute-start | bytes 9437192 | tf_op jit(solution)/shard_map/ppermute | solution.py:301

commit v6 on v5

--- a/solution.py
+++ b/solution.py
@@ -168,7 +168,8 @@
 
 def lay_kernel(place_ref, own_ref, other_ref, out_ref, held_ref, sems):
     slots, tile = sems.shape[0], held_ref.shape[3]
-    parts, half = own_ref.shape[0] // 2, own_ref.shape[1]
+    mine, half = own_ref.shape[1] // 2, own_ref.shape[2]
+    parts = own_ref.shape[0] * mine
     m = lax.broadcasted_iota(jnp.int32, (parts, parts), 0)
     n = lax.broadcasted_iota(jnp.int32, (parts, parts), 1)
     ahead = ((m >> 4) - place_ref[1]) & 3
@@ -188,7 +189,7 @@
                 leaving(j - slots, k).wait()
         side, at = divmod(j * tile, half)
         for ref, core in ((own_ref, place_ref[0]), (other_ref, 1 - place_ref[0])):
-            values = ref[side * parts : (side + 1) * parts, at : at + tile]
+            values = ref[:, side * mine : (side + 1) * mine, at : at + tile].reshape(parts, tile)
             rows = jnp.dot(pick, values, preferred_element_type=jnp.float32).astype(out_ref.dtype)
             for k in range(PROJ):
                 for zl in range(NZL):
@@ -203,7 +204,7 @@
 
 
 def lay(place, own, other, rows, tile=768, slots=4):
-    width = 2 * own.shape[1]
+    width = 2 * own.shape[2]
     return pl.pallas_call(
         lay_kernel,
         in_specs=[pl.BlockSpec(memory_space=pltpu.SMEM)]
@@ -233,6 +234,15 @@
         ring = NZH * NZL
         return lax.ppermute(a, ("zh", "zl"), [(z, (z + by) % ring) for z in range(ring)])
 
+    def opposite(a):
+        ring = NZH * NZL
+        pairs = [
+            (z * NC + c, (z + (2 if c == 0 else ring - 2)) % ring * NC + c)
+            for z in range(ring)
+            for c in range(NC)
+        ]
+        return lax.ppermute(a, ("zh", "zl", "c"), pairs)
+
     def onward(a, by, turned):
         pairs = []
         for n in range(PLANE * NC):
@@ -265,7 +275,7 @@
         part = shared(part[: block // 4], part[block // 4 :], 1)
     with jax.named_scope("depth_sum"):
         part = (part * (4.0 / SEND_SCALE)).reshape(NZL, NC * PROJ, half)
-        part = part[0] + ahead(part[1], 1) + ahead(part[3], 7) + ahead(part[2], 2)
+        part = part[0] + ahead(part[1], 1) + ahead(part[3], 7) + opposite(part[2])
         part = part + lax.ppermute(part, "zh", swap)
         came = lax.ppermute(part, "c", swap)
         gradient = jnp.where(
@@ -286,7 +296,7 @@
             jnp.concatenate([a[:, :half], a[:, half:]], axis=0) for a in (unit, gradient)
         )
     with jax.named_scope("depth_gather"):
-        units = [unit, ahead(unit, 7), ahead(unit, 2), ahead(unit, 1)]
+        units = [unit, ahead(unit, 7), opposite(unit), ahead(unit, 1)]
     with jax.named_scope("plane_gather"):
         order = np.arange(2 * NZL * PROJ).reshape(NZL, 2, PROJ).swapaxes(0, 1).reshape(-1)
         turn = jnp.asarray(np.eye(2 * NZL * PROJ)[order] * UNIT_SCALE, jnp.bfloat16)
@@ -296,8 +306,6 @@
         came = came.reshape(PLANE, 2 * (NZL + 1) * PROJ, half)
         grads = came[:, 2 * NZL * PROJ :].astype(jnp.float32).reshape(2 * PLANE * PROJ, half)
         own = came[:, : 2 * NZL * PROJ].astype(jnp.bfloat16)
-        own = jnp.swapaxes(own.reshape(PLANE, 2, NZL * PROJ, half), 0, 1)
-        own = own.reshape(2 * PLANE * NZL * PROJ, half)
     other = lax.ppermute(own, "c", swap)
     new_master, new_moment, new_second = step(grads, master, moment, second)
     gathered = lay(place, own, other, NZL * NC * master.shape[0])

time: 127 us -> 126 us (level)
    ppermute x6 -> x4, waiting for transfers between devices: 9.01 us -> 3.18 us  [ahead(): lax.ppermute(a, ('zh', 'zl'), [(z, (z + by) % ring) for z in range(ring)])]
    ppermute x0 -> x2, waiting for transfers between devices: none -> 3.08 us  [opposite(): return lax.ppermute(a, ('zh', 'zl', 'c'), pairs)]
    ppermute x1, waiting for transfers between devices: 1.37 us -> 4.14 us  [shards(): part = part + lax.ppermute(part, 'zh', swap)]
    ppermute x1, starting transfers between devices: 4.15 us -> 1.4 us  [shards(): part = part + lax.ppermute(part, 'zh', swap)]
    ppermute x0 -> x2, starting transfers between devices: none -> 1.52 us  [opposite(): return lax.ppermute(a, ('zh', 'zl', 'c'), pairs)]
    ppermute x6 -> x4, starting transfers between devices: 8.14 us -> 8.57 us  [ahead(): lax.ppermute(a, ('zh', 'zl'), [(z, (z + by) % ring) for z in range(ring)])]
where the time goes in v6:
time: 126 us
  waiting for transfers between devices  33.1 us (26%)
  starting transfers between devices  32 us (25%)
  blocking collectives  28.7 us (23%)
  Pallas kernels  18.3 us (15%)
  local copies, waits for them, and re-layouts  6.09 us (5%)
  other arithmetic  5.88 us (5%)
    all_gather x1, blocking collectives, shards(): came = lax.all_gather(payload, ('y', 'x'), axis=0, tiled=True)  28.7 us
    ppermute x6, waiting for transfers between devices, onward(): return lax.ppermute(a, ('y', 'x', 'c'), pairs)  20.5 us
    pallas_call x3, Pallas kernels, terms(): pl.pallas_call(functools.partial(terms_kernel, rows, len(sides), tile), i...  8.91 us
    ppermute x4, starting transfers between devices, ahead(): lax.ppermute(a, ('zh', 'zl'), [(z, (z + by) % ring) for z in range(ring)])  8.57 us
    ppermute x6, starting transfers between devices, onward(): return lax.ppermute(a, ('y', 'x', 'c'), pairs)  6.24 us
    ppermute x1, starting transfers between devices, shards(): came = lax.ppermute(part, 'c', swap)  5.55 us
    ppermute x1, starting transfers between devices, shards(): other = lax.ppermute(own, 'c', swap)  4.89 us
    pallas_call x1, Pallas kernels, lay(): pl.pallas_call(lay_kernel, in_specs=[pl.BlockSpec(memory_space=pltpu.SMEM...  4.32 us
  transfers between devices with their start and end apart: 18, of which 12 were waited for; matrix products, arithmetic and copies ran while one was open for 3% of the time, Pallas kernels for 8%

profile of v6, /device:TPU:1, one launch (start us, length us, event | category | flops | bytes accessed | tf_op | source)
XLA Modules:
  0.0 126.2 jit_solution(18094210158467248536)
XLA Ops:
  0.6 2.9 %constant_dynamic-slice_fusion.3 = (bf16[192,3072]{1,0:T(8,128)(2,1)S(1)}, bf16[192,3072]{1,0:T(8,128)(2,1)}) fusion(bf16[192,6144]{1,0:T(8,128)(2,1)} %param.7, s32[]{:T(128)S(6)} %select_n.27, s32[]{:T(128)S(6)} %select_n.28), kind=kLoop, calls=%fused_computation.36 | loop fusion | bytes 4718600 | tf_op jit(solution)/shard_map/pair/dynamic_slice | solution.py:260
  3.6 3.2 %collective-permute-start.1 = (bf16[192,3072]{1,0:T(8,128)(2,1)}, bf16[192,3072]{1,0:T(8,128)(2,1)S(1)}, u32[]{:S(2)}, u32[]{:S(2)}) collective-permute-start(bf16[192,3072]{1,0:T(8,128)(2,1)} %get-tuple-element.24), channel_id=1, source_target_pairs={{0,1},{1,0},{2,3},{3,2},{4,5},{5,4},{6,7},{7,6},{8,9},{9,8},{10,11... | collective-permute-start | bytes 3538952 | tf_op jit(solution)/shard_map/pair/ppermute | solution.py:265
  6.8 1.2 constant_dynamic-slice_fusion.2
  8.1 0.9 copy-done.3
  9.0 1.2 lefts.1
  10.8 2.2 %terms.4.refs_3_ = f32[384,3072]{1,0:T(8,128)S(1)} custom-call(bf16[512,192]{1,0:T(8,128)(2,1)S(1)} %get-tuple-element.9.refs_0_, bf16[192,3072]{1,0:T(8,128)(2,1)S(1)} %get-tuple-element.23.refs_1_, bf16[192,3072]{1,0:T(8,128)(2,1)S(1)} %get-tuple-element.21.refs_2_), custom_call_target="tpu_custom_call" | custom-call | flops 905969664 | bytes 4718592 | tf_op jit(solution)/shard_map/pair/terms/pallas_call | solution.py:93
  13.1 3.5 %terms.5 = f32[384,3072]{1,0:T(8,128)S(1)} custom-call(bf16[512,192]{1,0:T(8,128)(2,1)S(1)} %collective-permute-done.refs_3_.refs_0_, bf16[192,3072]{1,0:T(8,128)(2,1)S(1)} %collective-permute-done.1.refs_4_.refs_1_, bf16[192,3072]{1,0:T(8,128)(2,1)} %collective-permute-done.2.refs_5_.refs_2_, f32[384,3072]{1,0:T(8,128)S(1)} %terms.4.refs_3_), custom_call_target="tpu_custom_call" | custom-call | flops 905969664 | bytes 4718592 | tf_op jit(solution)/shard_map/pair/terms/pallas_call | solution.py:93
  17.5 2.7 %collective-permute-start.4 = (f16[128,3072]{1,0:T(8,128)(2,1)S(1)}, f16[128,3072]{1,0:T(8,128)(2,1)S(1)}, u32[]{:S(2)}, u32[]{:S(2)}) collective-permute-start(f16[128,3072]{1,0:T(8,128)(2,1)S(1)} %get-tuple-element.20), channel_id=1, source_target_pairs={{0,48},{1,193},{16,0},{17,209},{32,16},{33,225},{48,32},{49,241},{... | collective-permute-start | bytes 2359304 | tf_op jit(solution)/shard_map/plane_sum/ppermute | solution.py:252
  20.2 3.1 %terms.3 = f32[128,3072]{1,0:T(8,128)S(1)} custom-call(bf16[512,192]{1,0:T(8,128)(2,1)S(1)} %get-tuple-element.9.refs_0_, bf16[192,3072]{1,0:T(8,128)(2,1)S(1)} %get-tuple-element.23.refs_1_, bf16[192,3072]{1,0:T(8,128)(2,1)S(1)} %get-tuple-element.21.refs_2_, bf16[512,192]{1,0:T(8,128)(2,1)S(1)} %collective-permute-done.refs_3_.refs_0_, ...), custom_call_target="tpu_custom_call" | custom-call | flops 603979776 | bytes 4718592 | tf_op jit(solution)/shard_map/plane_sum/terms/pallas_call | solution.py:93
  23.4 14.9 %collective-permute-done.3 = f16[128,3072]{1,0:T(8,128)(2,1)S(1)} collective-permute-done((f16[128,3072]{1,0:T(8,128)(2,1)S(1)}, f16[128,3072]{1,0:T(8,128)(2,1)S(1)}, u32[]{:S(2)}, u32[]{:S(2)}) %collective-permute-start.3) | collective-permute-done | bytes 786464 | tf_op jit(solution)/shard_map/plane_sum/ppermute | solution.py:252
  39.5 2.3 %collective-permute-start.7 = (f16[32,3072]{1,0:T(8,128)(2,1)S(1)}, f16[32,3072]{1,0:T(8,128)(2,1)S(1)}, u32[]{:S(2)}, u32[]{:S(2)}) collective-permute-start(f16[32,3072]{1,0:T(8,128)(2,1)S(1)} %get-tuple-element.27), channel_id=1, source_target_pairs={{0,192},{1,49},{16,208},{17,1},{32,224},{33,17},{48,240},{49,33},{... | collective-permute-start | bytes 589832 | tf_op jit(solution)/shard_map/plane_sum/ppermute | solution.py:252
  42.5 2.6 %collective-permute-done.6 = f16[32,3072]{1,0:T(8,128)(2,1)S(1)} collective-permute-done((f16[32,3072]{1,0:T(8,128)(2,1)S(1)}, f16[32,3072]{1,0:T(8,128)(2,1)S(1)}, u32[]{:S(2)}, u32[]{:S(2)}) %collective-permute-start.6) | collective-permute-done | bytes 196640 | tf_op jit(solution)/shard_map/plane_sum/ppermute | solution.py:252
  45.1 1.4 %collective-permute-done.7 = f16[32,3072]{1,0:T(8,128)(2,1)S(1)} collective-permute-done((f16[32,3072]{1,0:T(8,128)(2,1)S(1)}, f16[32,3072]{1,0:T(8,128)(2,1)S(1)}, u32[]{:S(2)}, u32[]{:S(2)}) %collective-permute-start.7) | collective-permute-done | bytes 196640 | tf_op jit(solution)/shard_map/plane_sum/ppermute | solution.py:252
  46.4 1.6 %collective-permute-done.8 = f16[32,3072]{1,0:T(8,128)(2,1)S(1)} collective-permute-done((f16[32,3072]{1,0:T(8,128)(2,1)S(1)}, f16[32,3072]{1,0:T(8,128)(2,1)S(1)}, u32[]{:S(2)}, u32[]{:S(2)}) %collective-permute-start.8) | collective-permute-done | bytes 196640 | tf_op jit(solution)/shard_map/plane_sum/ppermute | solution.py:252
  48.2 5.1 %collective-permute-start.10 = (f32[8,3072]{1,0:T(8,128)S(1)}, f32[8,3072]{1,0:T(8,128)S(1)}, u32[]{:S(2)}, u32[]{:S(2)}) collective-permute-start(f32[8,3072]{1,0:T(8,128)S(1)} %get-tuple-element.30), channel_id=1, source_target_pairs={{0,14},{2,0},{4,2},{6,4},{8,6},{10,8},{12,10},{14,12},{1,15},{3,1}... | collective-permute-start | bytes 294920 | tf_op jit(solution)/shard_map/depth_sum/ppermute | solution.py:235
  53.3 1.2 collective-permute-start.11
  55.3 2.6 %collective-permute-done.11 = f32[8,3072]{1,0:T(8,128)S(1)} collective-permute-done((f32[8,3072]{1,0:T(8,128)S(1)}, f32[8,3072]{1,0:T(8,128)S(1)}, u32[]{:S(2)}, u32[]{:S(2)}) %collective-permute-start.11) | collective-permute-done | bytes 98336 | tf_op jit(solution)/shard_map/depth_sum/ppermute | solution.py:244
  57.8 1.8 %collective-permute-done.9 = f32[8,3072]{1,0:T(8,128)S(1)} collective-permute-done((f32[8,3072]{1,0:T(8,128)S(1)}, f32[8,3072]{1,0:T(8,128)S(1)}, u32[]{:S(2)}, u32[]{:S(2)}) %collective-permute-start.9) | collective-permute-done | bytes 98336 | tf_op jit(solution)/shard_map/depth_sum/ppermute | solution.py:235
  60.3 1.4 %collective-permute-start.12 = (f32[8,3072]{1,0:T(8,128)}, f32[8,3072]{1,0:T(8,128)}, u32[]{:S(2)}, u32[]{:S(2)}) collective-permute-start(f32[8,3072]{1,0:T(8,128)} %fusion.14), channel_id=1, source_target_pairs={{0,8},{8,0},{1,9},{9,1},{2,10},{10,2},{3,11},{11,3},{4,12},{12,4},... | collective-permute-start | bytes 294920 | tf_op jit(solution)/shard_map/depth_sum/ppermute | solution.py:279
  61.7 1.7 %multiply_reduce_fusion.1 = (f32[24576]{0:T(1024)S(1)}, f32[24576]{0:T(1024)S(1)}) fusion(f32[16,24576]{1,0:T(8,128)S(1)} %copy-done.1, s32[]{:T(128)S(6)} %select_n.25, f32[16,24576]{1,0:T(8,128)} %refs_1_.1), kind=kLoop, calls=%fused_computation.27 | loop fusion | flops 49152 | bytes 393220 | tf_op jit(solution)/shard_map/own_row/mul | solution.py:29
  63.9 4.1 %collective-permute-done.12 = f32[8,3072]{1,0:T(8,128)} collective-permute-done((f32[8,3072]{1,0:T(8,128)}, f32[8,3072]{1,0:T(8,128)}, u32[]{:S(2)}, u32[]{:S(2)}) %collective-permute-start.12) | collective-permute-done | bytes 98336 | tf_op jit(solution)/shard_map/depth_sum/ppermute | solution.py:279
  68.0 1.0 add.91
  69.0 5.5 %collective-permute-start.13 = (f32[8,3072]{1,0:T(8,128)S(1)}, f32[8,3072]{1,0:T(8,128)S(1)}, u32[]{:S(2)}, u32[]{:S(2)}) collective-permute-start(f32[8,3072]{1,0:T(8,128)S(1)} %add.91), channel_id=1, source_target_pairs={{0,1},{1,0},{2,3},{3,2},{4,5},{5,4},{6,7},{7,6},{8,9},{9,8},{10,11... | collective-permute-start | bytes 294920 | tf_op jit(solution)/shard_map/depth_sum/ppermute | solution.py:280
  74.5 0.9 collective-permute-done.13
  76.3 2.1 %collective-permute-start.16 = (bf16[8,3072]{1,0:T(8,128)(2,1)S(1)}, bf16[8,3072]{1,0:T(8,128)(2,1)S(1)}, u32[]{:S(2)}, u32[]{:S(2)}) collective-permute-start(bf16[8,3072]{1,0:T(8,128)(2,1)S(1)} %pad_maximum_fusion.1), channel_id=1, source_target_pairs={{0,2},{2,4},{4,6},{6,8},{8,10},{10,12},{12,14},{14,0},{1,3},{3,5},... | collective-permute-start | bytes 147464 | tf_op jit(solution)/shard_map/depth_gather/ppermute | solution.py:235
  80.1 1.2 collective-permute-done.16
  82.0 28.7 %all-gather.1 = f16[640,3072]{1,0:T(8,128)(2,1)S(1)} all-gather(f16[40,3072]{1,0:T(8,128)(2,1)S(1)} %pad_maximum_fusion), channel_id=1, replica_groups=mesh['y'=4,'x'=4,'zh'=2,'zl'=4,'c'=2] {'y','x'}, dimensions={0}, use_global_device_ids=true | all-gather | bytes 4177920 | tf_op jit(solution)/shard_map/plane_gather/all_gather | solution.py:305
  110.7 0.8 slice_convert_fusion.own_ref
  111.5 4.9 %collective-permute-start.17 = (bf16[16,32,3072]{2,1,0:T(8,128)(2,1)S(1)}, bf16[16,32,3072]{2,1,0:T(8,128)(2,1)S(1)}, u32[]{:S(2)}, u32[]{:S(2)}) collective-permute-start(bf16[16,32,3072]{2,1,0:T(8,128)(2,1)S(1)} %slice_convert_fusion.own_ref), channel_id=1, source_target_pairs={{0,1},{1,0},{2,3},{3,2},{4,5},{5,4},{6,7},{7,6},{8,9},{9,8},{10,11... | collective-permute-start | bytes 9437192 | tf_op jit(solution)/shard_map/ppermute | solution.py:309
  116.5 3.9 %step.1 = (f32[16,24576]{1,0:T(8,128)}, f32[16,24576]{1,0:T(8,128)}, f32[16,24576]{1,0:T(8,128)}) custom-call(f32[128,3072]{1,0:T(8,128)S(1)} %fusion.4.g_ref, f32[16,24576]{1,0:T(8,128)S(1)} %copy-done, f32[16,24576]{1,0:T(8,128)S(1)} %copy-done.2, f32[16,24576]{1,0:T(8,128)S(1)} %copy-done.1), custom_call_target="tpu_custom_call" | custom-call | flops 7864320 | bytes 9437184 | tf_op jit(solution)/shard_map/step/pallas_call | solution.py:151
  120.4 1.2 collective-permute-done.17.other_ref
  121.7 4.3 %lay.1 = bf16[128,24576]{1,0:T(8,128)(2,1)} custom-call(s32[4]{0:T(128)S(1)} %pad_add_fusion.place_ref, bf16[16,32,3072]{2,1,0:T(8,128)(2,1)S(1)} %slice_convert_fusion.own_ref, bf16[16,32,3072]{2,1,0:T(8,128)(2,1)S(1)} %collective-permute-done.17.other_ref), custom_call_target="tpu_custom_call" | custom-call | flops 805306368 | bytes 6291456 | tf_op jit(solution)/shard_map/lay/pallas_call | solution.py:208
  (63 shorter events, 8.7 us)
Async XLA Ops:
  0.6 6.2 %copy-start.4 = (bf16[192,6144]{1,0:T(8,128)(2,1)S(1)}, bf16[192,6144]{1,0:T(8,128)(2,1)}, u32[]{:S(2)}) copy-start(bf16[192,6144]{1,0:T(8,128)(2,1)} %param.8) | copy-start | bytes 7077892
  3.6 9.4 %collective-permute-start.1 = (bf16[192,3072]{1,0:T(8,128)(2,1)}, bf16[192,3072]{1,0:T(8,128)(2,1)S(1)}, u32[]{:S(2)}, u32[]{:S(2)}) collective-permute-start(bf16[192,3072]{1,0:T(8,128)(2,1)} %get-tuple-element.24), channel_id=1, source_target_pairs={{0,1},{1,0},{2,3},{3,2},{4,5},{5,4},{6,7},{7,6},{8,9},{9,8},{10,11... | collective-permute-start | bytes 3538952 | tf_op jit(solution)/shard_map/pair/ppermute | solution.py:265
  8.0 5.1 %collective-permute-start.2 = (bf16[192,3072]{1,0:T(8,128)(2,1)}, bf16[192,3072]{1,0:T(8,128)(2,1)}, u32[]{:S(2)}, u32[]{:S(2)}) collective-permute-start(bf16[192,3072]{1,0:T(8,128)(2,1)} %get-tuple-element.22), channel_id=1, source_target_pairs={{0,1},{1,0},{2,3},{3,2},{4,5},{5,4},{6,7},{7,6},{8,9},{9,8},{10,11... | collective-permute-start | bytes 3538952 | tf_op jit(solution)/shard_map/pair/ppermute | solution.py:266
  8.1 0.9 copy-start.3
  10.2 2.8 %collective-permute-start = (bf16[512,192]{1,0:T(8,128)(2,1)S(1)}, bf16[512,192]{1,0:T(8,128)(2,1)S(1)}, u32[]{:S(2)}, u32[]{:S(2)}) collective-permute-start(bf16[512,192]{1,0:T(8,128)(2,1)S(1)} %get-tuple-element.10), channel_id=1, source_target_pairs={{0,1},{1,0},{2,3},{3,2},{4,5},{5,4},{6,7},{7,6},{8,9},{9,8},{10,11... | collective-permute-start | bytes 589832 | tf_op jit(solution)/shard_map/pair/ppermute | solution.py:264
  17.4 20.8 %collective-permute-start.3 = (f16[128,3072]{1,0:T(8,128)(2,1)S(1)}, f16[128,3072]{1,0:T(8,128)(2,1)S(1)}, u32[]{:S(2)}, u32[]{:S(2)}) collective-permute-start(f16[128,3072]{1,0:T(8,128)(2,1)S(1)} %get-tuple-element.18), channel_id=1, source_target_pairs={{0,16},{1,65},{16,32},{17,81},{32,48},{33,97},{48,0},{49,113},{64,... | collective-permute-start | bytes 2359304 | tf_op jit(solution)/shard_map/plane_sum/ppermute | solution.py:252
  17.5 20.8 %collective-permute-start.4 = (f16[128,3072]{1,0:T(8,128)(2,1)S(1)}, f16[128,3072]{1,0:T(8,128)(2,1)S(1)}, u32[]{:S(2)}, u32[]{:S(2)}) collective-permute-start(f16[128,3072]{1,0:T(8,128)(2,1)S(1)} %get-tuple-element.20), channel_id=1, source_target_pairs={{0,48},{1,193},{16,0},{17,209},{32,16},{33,225},{48,32},{49,241},{... | collective-permute-start | bytes 2359304 | tf_op jit(solution)/shard_map/plane_sum/ppermute | solution.py:252
  20.2 18.1 %collective-permute-start.5 = (f16[128,3072]{1,0:T(8,128)(2,1)S(1)}, f16[128,3072]{1,0:T(8,128)(2,1)S(1)}, u32[]{:S(2)}, u32[]{:S(2)}) collective-permute-start(f16[128,3072]{1,0:T(8,128)(2,1)S(1)} %get-tuple-element.19), channel_id=1, source_target_pairs={{0,32},{1,129},{16,48},{17,145},{32,0},{33,161},{48,16},{49,177},{... | collective-permute-start | bytes 2359304 | tf_op jit(solution)/shard_map/plane_sum/ppermute | solution.py:252
  38.8 22.8 %copy-start.1 = (f32[16,24576]{1,0:T(8,128)S(1)}, f32[16,24576]{1,0:T(8,128)}, u32[]{:S(2)}) copy-start(f32[16,24576]{1,0:T(8,128)} %refs_2_.1) | copy-start | bytes 4718596
  39.0 6.1 %collective-permute-start.6 = (f16[32,3072]{1,0:T(8,128)(2,1)S(1)}, f16[32,3072]{1,0:T(8,128)(2,1)S(1)}, u32[]{:S(2)}, u32[]{:S(2)}) collective-permute-start(f16[32,3072]{1,0:T(8,128)(2,1)S(1)} %get-tuple-element.25), channel_id=1, source_target_pairs={{0,64},{1,17},{16,80},{17,33},{32,96},{33,49},{48,112},{49,1},{64,... | collective-permute-start | bytes 589832 | tf_op jit(solution)/shard_map/plane_sum/ppermute | solution.py:252
  39.5 7.0 %collective-permute-start.7 = (f16[32,3072]{1,0:T(8,128)(2,1)S(1)}, f16[32,3072]{1,0:T(8,128)(2,1)S(1)}, u32[]{:S(2)}, u32[]{:S(2)}) collective-permute-start(f16[32,3072]{1,0:T(8,128)(2,1)S(1)} %get-tuple-element.27), channel_id=1, source_target_pairs={{0,192},{1,49},{16,208},{17,1},{32,224},{33,17},{48,240},{49,33},{... | collective-permute-start | bytes 589832 | tf_op jit(solution)/shard_map/plane_sum/ppermute | solution.py:252
  41.7 6.3 %collective-permute-start.8 = (f16[32,3072]{1,0:T(8,128)(2,1)S(1)}, f16[32,3072]{1,0:T(8,128)(2,1)S(1)}, u32[]{:S(2)}, u32[]{:S(2)}) collective-permute-start(f16[32,3072]{1,0:T(8,128)(2,1)S(1)} %get-tuple-element.26), channel_id=1, source_target_pairs={{0,128},{1,33},{16,144},{17,49},{32,160},{33,1},{48,176},{49,17},{... | collective-permute-start | bytes 589832 | tf_op jit(solution)/shard_map/plane_sum/ppermute | solution.py:252
  48.0 15.4 %copy-start = (f32[16,24576]{1,0:T(8,128)S(1)}, f32[16,24576]{1,0:T(8,128)}, u32[]{:S(2)}) copy-start(f32[16,24576]{1,0:T(8,128)} %refs_0_.1) | copy-start | bytes 4718596
  48.2 7.1 %collective-permute-start.10 = (f32[8,3072]{1,0:T(8,128)S(1)}, f32[8,3072]{1,0:T(8,128)S(1)}, u32[]{:S(2)}, u32[]{:S(2)}) collective-permute-start(f32[8,3072]{1,0:T(8,128)S(1)} %get-tuple-element.30), channel_id=1, source_target_pairs={{0,14},{2,0},{4,2},{6,4},{8,6},{10,8},{12,10},{14,12},{1,15},{3,1}... | collective-permute-start | bytes 294920 | tf_op jit(solution)/shard_map/depth_sum/ppermute | solution.py:235
  53.3 4.5 %collective-permute-start.11 = (f32[8,3072]{1,0:T(8,128)S(1)}, f32[8,3072]{1,0:T(8,128)S(1)}, u32[]{:S(2)}, u32[]{:S(2)}) collective-permute-start(f32[8,3072]{1,0:T(8,128)S(1)} %get-tuple-element.29), channel_id=1, source_target_pairs={{0,4},{1,13},{2,6},{3,15},{4,8},{5,1},{6,10},{7,3},{8,12},{9,5},{1... | collective-permute-start | bytes 294920 | tf_op jit(solution)/shard_map/depth_sum/ppermute | solution.py:244
  54.5 5.1 %collective-permute-start.9 = (f32[8,3072]{1,0:T(8,128)S(1)}, f32[8,3072]{1,0:T(8,128)S(1)}, u32[]{:S(2)}, u32[]{:S(2)}) collective-permute-start(f32[8,3072]{1,0:T(8,128)S(1)} %get-tuple-element.28), channel_id=1, source_target_pairs={{0,2},{2,4},{4,6},{6,8},{8,10},{10,12},{12,14},{14,0},{1,3},{3,5},... | collective-permute-start | bytes 294920 | tf_op jit(solution)/shard_map/depth_sum/ppermute | solution.py:235
  60.3 7.7 %collective-permute-start.12 = (f32[8,3072]{1,0:T(8,128)}, f32[8,3072]{1,0:T(8,128)}, u32[]{:S(2)}, u32[]{:S(2)}) collective-permute-start(f32[8,3072]{1,0:T(8,128)} %fusion.14), channel_id=1, source_target_pairs={{0,8},{8,0},{1,9},{9,1},{2,10},{10,2},{3,11},{11,3},{4,12},{12,4},... | collective-permute-start | bytes 294920 | tf_op jit(solution)/shard_map/depth_sum/ppermute | solution.py:279
  63.8 16.2 %copy-start.7 = (bf16[32,8]{1,0:T(8,128)(2,1)S(1)}, bf16[32,8]{1,0:T(8,128)(2,1)}, u32[]{:S(2)}) copy-start(bf16[32,8]{1,0:T(8,128)(2,1)} %constant.62) | copy-start | bytes 1540
  63.8 15.2 %copy-start.9 = (bf16[32,4]{1,0:T(8,128)(2,1)S(1)}, bf16[32,4]{1,0:T(8,128)(2,1)}, u32[]{:S(2)}) copy-start(bf16[32,4]{1,0:T(8,128)(2,1)} %constant.59) | copy-start | bytes 772
  63.8 15.4 %copy-start.8 = (bf16[32,4]{1,0:T(8,128)(2,1)S(1)}, bf16[32,4]{1,0:T(8,128)(2,1)}, u32[]{:S(2)}) copy-start(bf16[32,4]{1,0:T(8,128)(2,1)} %constant.60) | copy-start | bytes 772
  68.9 12.3 %copy-start.6 = (bf16[32,8]{1,0:T(8,128)(2,1)S(1)}, bf16[32,8]{1,0:T(8,128)(2,1)}, u32[]{:S(2)}) copy-start(bf16[32,8]{1,0:T(8,128)(2,1)} %constant.63) | copy-start | bytes 1540
  69.0 6.5 %collective-permute-start.13 = (f32[8,3072]{1,0:T(8,128)S(1)}, f32[8,3072]{1,0:T(8,128)S(1)}, u32[]{:S(2)}, u32[]{:S(2)}) collective-permute-start(f32[8,3072]{1,0:T(8,128)S(1)} %add.91), channel_id=1, source_target_pairs={{0,1},{1,0},{2,3},{3,2},{4,5},{5,4},{6,7},{7,6},{8,9},{9,8},{10,11... | collective-permute-start | bytes 294920 | tf_op jit(solution)/shard_map/depth_sum/ppermute | solution.py:280
  75.5 6.2 %copy-start.5 = (bf16[32,8]{1,0:T(8,128)(2,1)S(1)}, bf16[32,8]{1,0:T(8,128)(2,1)}, u32[]{:S(2)}) copy-start(bf16[32,8]{1,0:T(8,128)(2,1)} %constant.61) | copy-start | bytes 1540
  76.0 4.0 %collective-permute-start.15 = (bf16[8,3072]{1,0:T(8,128)(2,1)S(1)}, bf16[8,3072]{1,0:T(8,128)(2,1)S(1)}, u32[]{:S(2)}, u32[]{:S(2)}) collective-permute-start(bf16[8,3072]{1,0:T(8,128)(2,1)S(1)} %pad_maximum_fusion.1), channel_id=1, source_target_pairs={{0,4},{1,13},{2,6},{3,15},{4,8},{5,1},{6,10},{7,3},{8,12},{9,5},{1... | collective-permute-start | bytes 147464 | tf_op jit(solution)/shard_map/depth_gather/ppermute | solution.py:244
  76.3 5.0 %collective-permute-start.16 = (bf16[8,3072]{1,0:T(8,128)(2,1)S(1)}, bf16[8,3072]{1,0:T(8,128)(2,1)S(1)}, u32[]{:S(2)}, u32[]{:S(2)}) collective-permute-start(bf16[8,3072]{1,0:T(8,128)(2,1)S(1)} %pad_maximum_fusion.1), channel_id=1, source_target_pairs={{0,2},{2,4},{4,6},{6,8},{8,10},{10,12},{12,14},{14,0},{1,3},{3,5},... | collective-permute-start | bytes 147464 | tf_op jit(solution)/shard_map/depth_gather/ppermute | solution.py:235
  78.4 3.2 %collective-permute-start.14 = (bf16[8,3072]{1,0:T(8,128)(2,1)S(1)}, bf16[8,3072]{1,0:T(8,128)(2,1)S(1)}, u32[]{:S(2)}, u32[]{:S(2)}) collective-permute-start(bf16[8,3072]{1,0:T(8,128)(2,1)S(1)} %pad_maximum_fusion.1), channel_id=1, source_target_pairs={{0,14},{2,0},{4,2},{6,4},{8,6},{10,8},{12,10},{14,12},{1,15},{3,1}... | collective-permute-start | bytes 147464 | tf_op jit(solution)/shard_map/depth_gather/ppermute | solution.py:235
  111.5 5.0 %copy-start.2 = (f32[16,24576]{1,0:T(8,128)S(1)}, f32[16,24576]{1,0:T(8,128)}, u32[]{:S(2)}) copy-start(f32[16,24576]{1,0:T(8,128)} %refs_1_.1) | copy-start | bytes 4718596
  111.5 10.2 %collective-permute-start.17 = (bf16[16,32,3072]{2,1,0:T(8,128)(2,1)S(1)}, bf16[16,32,3072]{2,1,0:T(8,128)(2,1)S(1)}, u32[]{:S(2)}, u32[]{:S(2)}) collective-permute-start(bf16[16,32,3072]{2,1,0:T(8,128)(2,1)S(1)} %slice_convert_fusion.own_ref), channel_id=1, source_target_pairs={{0,1},{1,0},{2,3},{3,2},{4,5},{5,4},{6,7},{7,6},{8,9},{9,8},{10,11... | collective-permute-start | bytes 9437192 | tf_op jit(solution)/shard_map/ppermute | solution.py:309

commit v7 on v6

--- a/solution.py
+++ b/solution.py
@@ -203,7 +203,7 @@
             leaving(j, k).wait()
 
 
-def lay(place, own, other, rows, tile=768, slots=4):
+def lay(place, own, other, rows, tile=1536, slots=4):
     width = 2 * own.shape[2]
     return pl.pallas_call(
         lay_kernel,

time: 126 us -> 126 us (level)
  no operation moved by 1% of the time
where the time goes in v7:
time: 126 us
  waiting for transfers between devices  33.1 us (26%)
  starting transfers between devices  32 us (25%)
  blocking collectives  28.7 us (23%)
  Pallas kernels  17.9 us (14%)
  local copies, waits for them, and re-layouts  6.09 us (5%)
  other arithmetic  5.88 us (5%)
    all_gather x1, blocking collectives, shards(): came = lax.all_gather(payload, ('y', 'x'), axis=0, tiled=True)  28.7 us
    ppermute x6, waiting for transfers between devices, onward(): return lax.ppermute(a, ('y', 'x', 'c'), pairs)  20.5 us
    pallas_call x3, Pallas kernels, terms(): pl.pallas_call(functools.partial(terms_kernel, rows, len(sides), tile), i...  8.91 us
    ppermute x4, starting transfers between devices, ahead(): lax.ppermute(a, ('zh', 'zl'), [(z, (z + by) % ring) for z in range(ring)])  8.57 us
    ppermute x6, starting transfers between devices, onward(): return lax.ppermute(a, ('y', 'x', 'c'), pairs)  6.24 us
    ppermute x1, starting transfers between devices, shards(): came = lax.ppermute(part, 'c', swap)  5.55 us
    ppermute x1, starting transfers between devices, shards(): other = lax.ppermute(own, 'c', swap)  4.89 us
    ppermute x1, waiting for transfers between devices, shards(): part = part + lax.ppermute(part, 'zh', swap)  4.14 us
  transfers between devices with their start and end apart: 18, of which 12 were waited for; matrix products, arithmetic and copies ran while one was open for 3% of the time, Pallas kernels for 8%

profile of v7, /device:TPU:1, one launch (start us, length us, event | category | flops | bytes accessed | tf_op | source)
XLA Modules:
  0.0 125.7 jit_solution(9804082433851706700)
XLA Ops:
  0.6 2.9 %constant_dynamic-slice_fusion.3 = (bf16[192,3072]{1,0:T(8,128)(2,1)S(1)}, bf16[192,3072]{1,0:T(8,128)(2,1)}) fusion(bf16[192,6144]{1,0:T(8,128)(2,1)} %param.7, s32[]{:T(128)S(6)} %select_n.27, s32[]{:T(128)S(6)} %select_n.28), kind=kLoop, calls=%fused_computation.36 | loop fusion | bytes 4718600 | tf_op jit(solution)/shard_map/pair/dynamic_slice | solution.py:260
  3.6 3.2 %collective-permute-start.1 = (bf16[192,3072]{1,0:T(8,128)(2,1)}, bf16[192,3072]{1,0:T(8,128)(2,1)S(1)}, u32[]{:S(2)}, u32[]{:S(2)}) collective-permute-start(bf16[192,3072]{1,0:T(8,128)(2,1)} %get-tuple-element.24), channel_id=1, source_target_pairs={{0,1},{1,0},{2,3},{3,2},{4,5},{5,4},{6,7},{7,6},{8,9},{9,8},{10,11... | collective-permute-start | bytes 3538952 | tf_op jit(solution)/shard_map/pair/ppermute | solution.py:265
  6.8 1.2 constant_dynamic-slice_fusion.2
  8.1 0.9 copy-done.3
  9.0 1.2 lefts.1
  10.8 2.2 %terms.4.refs_3_ = f32[384,3072]{1,0:T(8,128)S(1)} custom-call(bf16[512,192]{1,0:T(8,128)(2,1)S(1)} %get-tuple-element.9.refs_0_, bf16[192,3072]{1,0:T(8,128)(2,1)S(1)} %get-tuple-element.23.refs_1_, bf16[192,3072]{1,0:T(8,128)(2,1)S(1)} %get-tuple-element.21.refs_2_), custom_call_target="tpu_custom_call" | custom-call | flops 905969664 | bytes 4718592 | tf_op jit(solution)/shard_map/pair/terms/pallas_call | solution.py:93
  13.1 3.5 %terms.5 = f32[384,3072]{1,0:T(8,128)S(1)} custom-call(bf16[512,192]{1,0:T(8,128)(2,1)S(1)} %collective-permute-done.refs_3_.refs_0_, bf16[192,3072]{1,0:T(8,128)(2,1)S(1)} %collective-permute-done.1.refs_4_.refs_1_, bf16[192,3072]{1,0:T(8,128)(2,1)} %collective-permute-done.2.refs_5_.refs_2_, f32[384,3072]{1,0:T(8,128)S(1)} %terms.4.refs_3_), custom_call_target="tpu_custom_call" | custom-call | flops 905969664 | bytes 4718592 | tf_op jit(solution)/shard_map/pair/terms/pallas_call | solution.py:93
  17.5 2.7 %collective-permute-start.4 = (f16[128,3072]{1,0:T(8,128)(2,1)S(1)}, f16[128,3072]{1,0:T(8,128)(2,1)S(1)}, u32[]{:S(2)}, u32[]{:S(2)}) collective-permute-start(f16[128,3072]{1,0:T(8,128)(2,1)S(1)} %get-tuple-element.20), channel_id=1, source_target_pairs={{0,48},{1,193},{16,0},{17,209},{32,16},{33,225},{48,32},{49,241},{... | collective-permute-start | bytes 2359304 | tf_op jit(solution)/shard_map/plane_sum/ppermute | solution.py:252
  20.2 3.1 %terms.3 = f32[128,3072]{1,0:T(8,128)S(1)} custom-call(bf16[512,192]{1,0:T(8,128)(2,1)S(1)} %get-tuple-element.9.refs_0_, bf16[192,3072]{1,0:T(8,128)(2,1)S(1)} %get-tuple-element.23.refs_1_, bf16[192,3072]{1,0:T(8,128)(2,1)S(1)} %get-tuple-element.21.refs_2_, bf16[512,192]{1,0:T(8,128)(2,1)S(1)} %collective-permute-done.refs_3_.refs_0_, ...), custom_call_target="tpu_custom_call" | custom-call | flops 603979776 | bytes 4718592 | tf_op jit(solution)/shard_map/plane_sum/terms/pallas_call | solution.py:93
  23.4 14.9 %collective-permute-done.3 = f16[128,3072]{1,0:T(8,128)(2,1)S(1)} collective-permute-done((f16[128,3072]{1,0:T(8,128)(2,1)S(1)}, f16[128,3072]{1,0:T(8,128)(2,1)S(1)}, u32[]{:S(2)}, u32[]{:S(2)}) %collective-permute-start.3) | collective-permute-done | bytes 786464 | tf_op jit(solution)/shard_map/plane_sum/ppermute | solution.py:252
  39.5 2.3 %collective-permute-start.7 = (f16[32,3072]{1,0:T(8,128)(2,1)S(1)}, f16[32,3072]{1,0:T(8,128)(2,1)S(1)}, u32[]{:S(2)}, u32[]{:S(2)}) collective-permute-start(f16[32,3072]{1,0:T(8,128)(2,1)S(1)} %get-tuple-element.27), channel_id=1, source_target_pairs={{0,192},{1,49},{16,208},{17,1},{32,224},{33,17},{48,240},{49,33},{... | collective-permute-start | bytes 589832 | tf_op jit(solution)/shard_map/plane_sum/ppermute | solution.py:252
  42.5 2.6 %collective-permute-done.6 = f16[32,3072]{1,0:T(8,128)(2,1)S(1)} collective-permute-done((f16[32,3072]{1,0:T(8,128)(2,1)S(1)}, f16[32,3072]{1,0:T(8,128)(2,1)S(1)}, u32[]{:S(2)}, u32[]{:S(2)}) %collective-permute-start.6) | collective-permute-done | bytes 196640 | tf_op jit(solution)/shard_map/plane_sum/ppermute | solution.py:252
  45.1 1.4 %collective-permute-done.7 = f16[32,3072]{1,0:T(8,128)(2,1)S(1)} collective-permute-done((f16[32,3072]{1,0:T(8,128)(2,1)S(1)}, f16[32,3072]{1,0:T(8,128)(2,1)S(1)}, u32[]{:S(2)}, u32[]{:S(2)}) %collective-permute-start.7) | collective-permute-done | bytes 196640 | tf_op jit(solution)/shard_map/plane_sum/ppermute | solution.py:252
  46.4 1.6 %collective-permute-done.8 = f16[32,3072]{1,0:T(8,128)(2,1)S(1)} collective-permute-done((f16[32,3072]{1,0:T(8,128)(2,1)S(1)}, f16[32,3072]{1,0:T(8,128)(2,1)S(1)}, u32[]{:S(2)}, u32[]{:S(2)}) %collective-permute-start.8) | collective-permute-done | bytes 196640 | tf_op jit(solution)/shard_map/plane_sum/ppermute | solution.py:252
  48.2 5.1 %collective-permute-start.10 = (f32[8,3072]{1,0:T(8,128)S(1)}, f32[8,3072]{1,0:T(8,128)S(1)}, u32[]{:S(2)}, u32[]{:S(2)}) collective-permute-start(f32[8,3072]{1,0:T(8,128)S(1)} %get-tuple-element.30), channel_id=1, source_target_pairs={{0,14},{2,0},{4,2},{6,4},{8,6},{10,8},{12,10},{14,12},{1,15},{3,1}... | collective-permute-start | bytes 294920 | tf_op jit(solution)/shard_map/depth_sum/ppermute | solution.py:235
  53.3 1.2 collective-permute-start.11
  55.3 2.6 %collective-permute-done.11 = f32[8,3072]{1,0:T(8,128)S(1)} collective-permute-done((f32[8,3072]{1,0:T(8,128)S(1)}, f32[8,3072]{1,0:T(8,128)S(1)}, u32[]{:S(2)}, u32[]{:S(2)}) %collective-permute-start.11) | collective-permute-done | bytes 98336 | tf_op jit(solution)/shard_map/depth_sum/ppermute | solution.py:244
  57.8 1.8 %collective-permute-done.9 = f32[8,3072]{1,0:T(8,128)S(1)} collective-permute-done((f32[8,3072]{1,0:T(8,128)S(1)}, f32[8,3072]{1,0:T(8,128)S(1)}, u32[]{:S(2)}, u32[]{:S(2)}) %collective-permute-start.9) | collective-permute-done | bytes 98336 | tf_op jit(solution)/shard_map/depth_sum/ppermute | solution.py:235
  60.3 1.4 %collective-permute-start.12 = (f32[8,3072]{1,0:T(8,128)}, f32[8,3072]{1,0:T(8,128)}, u32[]{:S(2)}, u32[]{:S(2)}) collective-permute-start(f32[8,3072]{1,0:T(8,128)} %fusion.14), channel_id=1, source_target_pairs={{0,8},{8,0},{1,9},{9,1},{2,10},{10,2},{3,11},{11,3},{4,12},{12,4},... | collective-permute-start | bytes 294920 | tf_op jit(solution)/shard_map/depth_sum/ppermute | solution.py:279
  61.7 1.7 %multiply_reduce_fusion.1 = (f32[24576]{0:T(1024)S(1)}, f32[24576]{0:T(1024)S(1)}) fusion(f32[16,24576]{1,0:T(8,128)S(1)} %copy-done.1, s32[]{:T(128)S(6)} %select_n.25, f32[16,24576]{1,0:T(8,128)} %refs_1_.1), kind=kLoop, calls=%fused_computation.27 | loop fusion | flops 49152 | bytes 393220 | tf_op jit(solution)/shard_map/own_row/mul | solution.py:29
  63.9 4.1 %collective-permute-done.12 = f32[8,3072]{1,0:T(8,128)} collective-permute-done((f32[8,3072]{1,0:T(8,128)}, f32[8,3072]{1,0:T(8,128)}, u32[]{:S(2)}, u32[]{:S(2)}) %collective-permute-start.12) | collective-permute-done | bytes 98336 | tf_op jit(solution)/shard_map/depth_sum/ppermute | solution.py:279
  68.0 1.0 add.91
  69.0 5.5 %collective-permute-start.13 = (f32[8,3072]{1,0:T(8,128)S(1)}, f32[8,3072]{1,0:T(8,128)S(1)}, u32[]{:S(2)}, u32[]{:S(2)}) collective-permute-start(f32[8,3072]{1,0:T(8,128)S(1)} %add.91), channel_id=1, source_target_pairs={{0,1},{1,0},{2,3},{3,2},{4,5},{5,4},{6,7},{7,6},{8,9},{9,8},{10,11... | collective-permute-start | bytes 294920 | tf_op jit(solution)/shard_map/depth_sum/ppermute | solution.py:280
  74.5 0.9 collective-permute-done.13
  76.3 2.1 %collective-permute-start.16 = (bf16[8,3072]{1,0:T(8,128)(2,1)S(1)}, bf16[8,3072]{1,0:T(8,128)(2,1)S(1)}, u32[]{:S(2)}, u32[]{:S(2)}) collective-permute-start(bf16[8,3072]{1,0:T(8,128)(2,1)S(1)} %pad_maximum_fusion.1), channel_id=1, source_target_pairs={{0,2},{2,4},{4,6},{6,8},{8,10},{10,12},{12,14},{14,0},{1,3},{3,5},... | collective-permute-start | bytes 147464 | tf_op jit(solution)/shard_map/depth_gather/ppermute | solution.py:235
  80.1 1.2 collective-permute-done.16
  82.0 28.7 %all-gather.1 = f16[640,3072]{1,0:T(8,128)(2,1)S(1)} all-gather(f16[40,3072]{1,0:T(8,128)(2,1)S(1)} %pad_maximum_fusion), channel_id=1, replica_groups=mesh['y'=4,'x'=4,'zh'=2,'zl'=4,'c'=2] {'y','x'}, dimensions={0}, use_global_device_ids=true | all-gather | bytes 4177920 | tf_op jit(solution)/shard_map/plane_gather/all_gather | solution.py:305
  110.7 0.8 slice_convert_fusion.own_ref
  111.5 4.9 %collective-permute-start.17 = (bf16[16,32,3072]{2,1,0:T(8,128)(2,1)S(1)}, bf16[16,32,3072]{2,1,0:T(8,128)(2,1)S(1)}, u32[]{:S(2)}, u32[]{:S(2)}) collective-permute-start(bf16[16,32,3072]{2,1,0:T(8,128)(2,1)S(1)} %slice_convert_fusion.own_ref), channel_id=1, source_target_pairs={{0,1},{1,0},{2,3},{3,2},{4,5},{5,4},{6,7},{7,6},{8,9},{9,8},{10,11... | collective-permute-start | bytes 9437192 | tf_op jit(solution)/shard_map/ppermute | solution.py:309
  116.5 3.9 %step.1 = (f32[16,24576]{1,0:T(8,128)}, f32[16,24576]{1,0:T(8,128)}, f32[16,24576]{1,0:T(8,128)}) custom-call(f32[128,3072]{1,0:T(8,128)S(1)} %fusion.4.g_ref, f32[16,24576]{1,0:T(8,128)S(1)} %copy-done, f32[16,24576]{1,0:T(8,128)S(1)} %copy-done.2, f32[16,24576]{1,0:T(8,128)S(1)} %copy-done.1), custom_call_target="tpu_custom_call" | custom-call | flops 7864320 | bytes 9437184 | tf_op jit(solution)/shard_map/step/pallas_call | solution.py:151
  120.4 1.2 collective-permute-done.17.other_ref
  121.7 3.9 %lay.1 = bf16[128,24576]{1,0:T(8,128)(2,1)} custom-call(s32[4]{0:T(128)S(1)} %pad_add_fusion.place_ref, bf16[16,32,3072]{2,1,0:T(8,128)(2,1)S(1)} %slice_convert_fusion.own_ref, bf16[16,32,3072]{2,1,0:T(8,128)(2,1)S(1)} %collective-permute-done.17.other_ref), custom_call_target="tpu_custom_call" | custom-call | flops 805306368 | bytes 6291456 | tf_op jit(solution)/shard_map/lay/pallas_call | solution.py:208
  (63 shorter events, 8.7 us)
Async XLA Ops:
  0.6 6.2 %copy-start.4 = (bf16[192,6144]{1,0:T(8,128)(2,1)S(1)}, bf16[192,6144]{1,0:T(8,128)(2,1)}, u32[]{:S(2)}) copy-start(bf16[192,6144]{1,0:T(8,128)(2,1)} %param.8) | copy-start | bytes 7077892
  3.6 9.4 %collective-permute-start.1 = (bf16[192,3072]{1,0:T(8,128)(2,1)}, bf16[192,3072]{1,0:T(8,128)(2,1)S(1)}, u32[]{:S(2)}, u32[]{:S(2)}) collective-permute-start(bf16[192,3072]{1,0:T(8,128)(2,1)} %get-tuple-element.24), channel_id=1, source_target_pairs={{0,1},{1,0},{2,3},{3,2},{4,5},{5,4},{6,7},{7,6},{8,9},{9,8},{10,11... | collective-permute-start | bytes 3538952 | tf_op jit(solution)/shard_map/pair/ppermute | solution.py:265
  8.0 5.1 %collective-permute-start.2 = (bf16[192,3072]{1,0:T(8,128)(2,1)}, bf16[192,3072]{1,0:T(8,128)(2,1)}, u32[]{:S(2)}, u32[]{:S(2)}) collective-permute-start(bf16[192,3072]{1,0:T(8,128)(2,1)} %get-tuple-element.22), channel_id=1, source_target_pairs={{0,1},{1,0},{2,3},{3,2},{4,5},{5,4},{6,7},{7,6},{8,9},{9,8},{10,11... | collective-permute-start | bytes 3538952 | tf_op jit(solution)/shard_map/pair/ppermute | solution.py:266
  8.1 0.9 copy-start.3
  10.2 2.8 %collective-permute-start = (bf16[512,192]{1,0:T(8,128)(2,1)S(1)}, bf16[512,192]{1,0:T(8,128)(2,1)S(1)}, u32[]{:S(2)}, u32[]{:S(2)}) collective-permute-start(bf16[512,192]{1,0:T(8,128)(2,1)S(1)} %get-tuple-element.10), channel_id=1, source_target_pairs={{0,1},{1,0},{2,3},{3,2},{4,5},{5,4},{6,7},{7,6},{8,9},{9,8},{10,11... | collective-permute-start | bytes 589832 | tf_op jit(solution)/shard_map/pair/ppermute | solution.py:264
  17.4 20.8 %collective-permute-start.3 = (f16[128,3072]{1,0:T(8,128)(2,1)S(1)}, f16[128,3072]{1,0:T(8,128)(2,1)S(1)}, u32[]{:S(2)}, u32[]{:S(2)}) collective-permute-start(f16[128,3072]{1,0:T(8,128)(2,1)S(1)} %get-tuple-element.18), channel_id=1, source_target_pairs={{0,16},{1,65},{16,32},{17,81},{32,48},{33,97},{48,0},{49,113},{64,... | collective-permute-start | bytes 2359304 | tf_op jit(solution)/shard_map/plane_sum/ppermute | solution.py:252
  17.5 20.8 %collective-permute-start.4 = (f16[128,3072]{1,0:T(8,128)(2,1)S(1)}, f16[128,3072]{1,0:T(8,128)(2,1)S(1)}, u32[]{:S(2)}, u32[]{:S(2)}) collective-permute-start(f16[128,3072]{1,0:T(8,128)(2,1)S(1)} %get-tuple-element.20), channel_id=1, source_target_pairs={{0,48},{1,193},{16,0},{17,209},{32,16},{33,225},{48,32},{49,241},{... | collective-permute-start | bytes 2359304 | tf_op jit(solution)/shard_map/plane_sum/ppermute | solution.py:252
  20.2 18.1 %collective-permute-start.5 = (f16[128,3072]{1,0:T(8,128)(2,1)S(1)}, f16[128,3072]{1,0:T(8,128)(2,1)S(1)}, u32[]{:S(2)}, u32[]{:S(2)}) collective-permute-start(f16[128,3072]{1,0:T(8,128)(2,1)S(1)} %get-tuple-element.19), channel_id=1, source_target_pairs={{0,32},{1,129},{16,48},{17,145},{32,0},{33,161},{48,16},{49,177},{... | collective-permute-start | bytes 2359304 | tf_op jit(solution)/shard_map/plane_sum/ppermute | solution.py:252
  38.8 22.8 %copy-start.1 = (f32[16,24576]{1,0:T(8,128)S(1)}, f32[16,24576]{1,0:T(8,128)}, u32[]{:S(2)}) copy-start(f32[16,24576]{1,0:T(8,128)} %refs_2_.1) | copy-start | bytes 4718596
  39.0 6.1 %collective-permute-start.6 = (f16[32,3072]{1,0:T(8,128)(2,1)S(1)}, f16[32,3072]{1,0:T(8,128)(2,1)S(1)}, u32[]{:S(2)}, u32[]{:S(2)}) collective-permute-start(f16[32,3072]{1,0:T(8,128)(2,1)S(1)} %get-tuple-element.25), channel_id=1, source_target_pairs={{0,64},{1,17},{16,80},{17,33},{32,96},{33,49},{48,112},{49,1},{64,... | collective-permute-start | bytes 589832 | tf_op jit(solution)/shard_map/plane_sum/ppermute | solution.py:252
  39.5 7.0 %collective-permute-start.7 = (f16[32,3072]{1,0:T(8,128)(2,1)S(1)}, f16[32,3072]{1,0:T(8,128)(2,1)S(1)}, u32[]{:S(2)}, u32[]{:S(2)}) collective-permute-start(f16[32,3072]{1,0:T(8,128)(2,1)S(1)} %get-tuple-element.27), channel_id=1, source_target_pairs={{0,192},{1,49},{16,208},{17,1},{32,224},{33,17},{48,240},{49,33},{... | collective-permute-start | bytes 589832 | tf_op jit(solution)/shard_map/plane_sum/ppermute | solution.py:252
  41.7 6.3 %collective-permute-start.8 = (f16[32,3072]{1,0:T(8,128)(2,1)S(1)}, f16[32,3072]{1,0:T(8,128)(2,1)S(1)}, u32[]{:S(2)}, u32[]{:S(2)}) collective-permute-start(f16[32,3072]{1,0:T(8,128)(2,1)S(1)} %get-tuple-element.26), channel_id=1, source_target_pairs={{0,128},{1,33},{16,144},{17,49},{32,160},{33,1},{48,176},{49,17},{... | collective-permute-start | bytes 589832 | tf_op jit(solution)/shard_map/plane_sum/ppermute | solution.py:252
  48.0 15.4 %copy-start = (f32[16,24576]{1,0:T(8,128)S(1)}, f32[16,24576]{1,0:T(8,128)}, u32[]{:S(2)}) copy-start(f32[16,24576]{1,0:T(8,128)} %refs_0_.1) | copy-start | bytes 4718596
  48.2 7.1 %collective-permute-start.10 = (f32[8,3072]{1,0:T(8,128)S(1)}, f32[8,3072]{1,0:T(8,128)S(1)}, u32[]{:S(2)}, u32[]{:S(2)}) collective-permute-start(f32[8,3072]{1,0:T(8,128)S(1)} %get-tuple-element.30), channel_id=1, source_target_pairs={{0,14},{2,0},{4,2},{6,4},{8,6},{10,8},{12,10},{14,12},{1,15},{3,1}... | collective-permute-start | bytes 294920 | tf_op jit(solution)/shard_map/depth_sum/ppermute | solution.py:235
  53.3 4.5 %collective-permute-start.11 = (f32[8,3072]{1,0:T(8,128)S(1)}, f32[8,3072]{1,0:T(8,128)S(1)}, u32[]{:S(2)}, u32[]{:S(2)}) collective-permute-start(f32[8,3072]{1,0:T(8,128)S(1)} %get-tuple-element.29), channel_id=1, source_target_pairs={{0,4},{1,13},{2,6},{3,15},{4,8},{5,1},{6,10},{7,3},{8,12},{9,5},{1... | collective-permute-start | bytes 294920 | tf_op jit(solution)/shard_map/depth_sum/ppermute | solution.py:244
  54.5 5.1 %collective-permute-start.9 = (f32[8,3072]{1,0:T(8,128)S(1)}, f32[8,3072]{1,0:T(8,128)S(1)}, u32[]{:S(2)}, u32[]{:S(2)}) collective-permute-start(f32[8,3072]{1,0:T(8,128)S(1)} %get-tuple-element.28), channel_id=1, source_target_pairs={{0,2},{2,4},{4,6},{6,8},{8,10},{10,12},{12,14},{14,0},{1,3},{3,5},... | collective-permute-start | bytes 294920 | tf_op jit(solution)/shard_map/depth_sum/ppermute | solution.py:235
  60.3 7.7 %collective-permute-start.12 = (f32[8,3072]{1,0:T(8,128)}, f32[8,3072]{1,0:T(8,128)}, u32[]{:S(2)}, u32[]{:S(2)}) collective-permute-start(f32[8,3072]{1,0:T(8,128)} %fusion.14), channel_id=1, source_target_pairs={{0,8},{8,0},{1,9},{9,1},{2,10},{10,2},{3,11},{11,3},{4,12},{12,4},... | collective-permute-start | bytes 294920 | tf_op jit(solution)/shard_map/depth_sum/ppermute | solution.py:279
  63.8 16.2 %copy-start.7 = (bf16[32,8]{1,0:T(8,128)(2,1)S(1)}, bf16[32,8]{1,0:T(8,128)(2,1)}, u32[]{:S(2)}) copy-start(bf16[32,8]{1,0:T(8,128)(2,1)} %constant.62) | copy-start | bytes 1540
  63.8 15.2 %copy-start.9 = (bf16[32,4]{1,0:T(8,128)(2,1)S(1)}, bf16[32,4]{1,0:T(8,128)(2,1)}, u32[]{:S(2)}) copy-start(bf16[32,4]{1,0:T(8,128)(2,1)} %constant.59) | copy-start | bytes 772
  63.8 15.4 %copy-start.8 = (bf16[32,4]{1,0:T(8,128)(2,1)S(1)}, bf16[32,4]{1,0:T(8,128)(2,1)}, u32[]{:S(2)}) copy-start(bf16[32,4]{1,0:T(8,128)(2,1)} %constant.60) | copy-start | bytes 772
  68.9 12.3 %copy-start.6 = (bf16[32,8]{1,0:T(8,128)(2,1)S(1)}, bf16[32,8]{1,0:T(8,128)(2,1)}, u32[]{:S(2)}) copy-start(bf16[32,8]{1,0:T(8,128)(2,1)} %constant.63) | copy-start | bytes 1540
  69.0 6.5 %collective-permute-start.13 = (f32[8,3072]{1,0:T(8,128)S(1)}, f32[8,3072]{1,0:T(8,128)S(1)}, u32[]{:S(2)}, u32[]{:S(2)}) collective-permute-start(f32[8,3072]{1,0:T(8,128)S(1)} %add.91), channel_id=1, source_target_pairs={{0,1},{1,0},{2,3},{3,2},{4,5},{5,4},{6,7},{7,6},{8,9},{9,8},{10,11... | collective-permute-start | bytes 294920 | tf_op jit(solution)/shard_map/depth_sum/ppermute | solution.py:280
  75.5 6.2 %copy-start.5 = (bf16[32,8]{1,0:T(8,128)(2,1)S(1)}, bf16[32,8]{1,0:T(8,128)(2,1)}, u32[]{:S(2)}) copy-start(bf16[32,8]{1,0:T(8,128)(2,1)} %constant.61) | copy-start | bytes 1540
  76.0 4.0 %collective-permute-start.15 = (bf16[8,3072]{1,0:T(8,128)(2,1)S(1)}, bf16[8,3072]{1,0:T(8,128)(2,1)S(1)}, u32[]{:S(2)}, u32[]{:S(2)}) collective-permute-start(bf16[8,3072]{1,0:T(8,128)(2,1)S(1)} %pad_maximum_fusion.1), channel_id=1, source_target_pairs={{0,4},{1,13},{2,6},{3,15},{4,8},{5,1},{6,10},{7,3},{8,12},{9,5},{1... | collective-permute-start | bytes 147464 | tf_op jit(solution)/shard_map/depth_gather/ppermute | solution.py:244
  76.3 5.0 %collective-permute-start.16 = (bf16[8,3072]{1,0:T(8,128)(2,1)S(1)}, bf16[8,3072]{1,0:T(8,128)(2,1)S(1)}, u32[]{:S(2)}, u32[]{:S(2)}) collective-permute-start(bf16[8,3072]{1,0:T(8,128)(2,1)S(1)} %pad_maximum_fusion.1), channel_id=1, source_target_pairs={{0,2},{2,4},{4,6},{6,8},{8,10},{10,12},{12,14},{14,0},{1,3},{3,5},... | collective-permute-start | bytes 147464 | tf_op jit(solution)/shard_map/depth_gather/ppermute | solution.py:235
  78.4 3.2 %collective-permute-start.14 = (bf16[8,3072]{1,0:T(8,128)(2,1)S(1)}, bf16[8,3072]{1,0:T(8,128)(2,1)S(1)}, u32[]{:S(2)}, u32[]{:S(2)}) collective-permute-start(bf16[8,3072]{1,0:T(8,128)(2,1)S(1)} %pad_maximum_fusion.1), channel_id=1, source_target_pairs={{0,14},{2,0},{4,2},{6,4},{8,6},{10,8},{12,10},{14,12},{1,15},{3,1}... | collective-permute-start | bytes 147464 | tf_op jit(solution)/shard_map/depth_gather/ppermute | solution.py:235
  111.5 5.0 %copy-start.2 = (f32[16,24576]{1,0:T(8,128)S(1)}, f32[16,24576]{1,0:T(8,128)}, u32[]{:S(2)}) copy-start(f32[16,24576]{1,0:T(8,128)} %refs_1_.1) | copy-start | bytes 4718596
  111.5 10.2 %collective-permute-start.17 = (bf16[16,32,3072]{2,1,0:T(8,128)(2,1)S(1)}, bf16[16,32,3072]{2,1,0:T(8,128)(2,1)S(1)}, u32[]{:S(2)}, u32[]{:S(2)}) collective-permute-start(bf16[16,32,3072]{2,1,0:T(8,128)(2,1)S(1)} %slice_convert_fusion.own_ref), channel_id=1, source_target_pairs={{0,1},{1,0},{2,3},{3,2},{4,5},{5,4},{6,7},{7,6},{8,9},{9,8},{10,11... | collective-permute-start | bytes 9437192 | tf_op jit(solution)/shard_map/ppermute | solution.py:309
